TPU v7x, 128 devices: a whole 4x4x4 slice. The times are simulated.
128 devices in a mesh: fsdp: 32 (over z, x_hi, y), tp: 4 (over x_lo, core).
Axes of the slice: x: 4 (x_hi: 2, x_lo: 2; x = x_hi * 2 + x_lo), y: 4, z: 4, core: 2. Of those that a mesh axis runs over, the one named last changes fastest.
Arguments:
- tokens: bfloat16 [16384, 2048], P(('fsdp', 'tp')), may hold values from -6 to 6
- g_attn: bfloat16 [2048], P('fsdp'), may hold values from 0.5 to 1.5
- query_matrix: bfloat16 [2048, 2048], P('fsdp', 'tp'), may hold values from -0.125 to 0.125
- key_matrix: bfloat16 [2048, 512], P('fsdp', 'tp'), may hold values from -0.125 to 0.125
- value_matrix: bfloat16 [2048, 512], P('fsdp', 'tp'), may hold values from -0.125 to 0.125
- w_out: bfloat16 [2048, 2048], P('fsdp', 'tp'), may hold values from -1 to 1
- g_ffn: bfloat16 [2048], P('fsdp'), may hold values from 0.5 to 1.5
- w_router: bfloat16 [2048, 64], P('fsdp'), may hold values from -0.09375 to 0.09375
- shared_gate: bfloat16 [2048, 2816], P('fsdp', 'tp'), may hold values from -0.125 to 0.125
- shared_up: bfloat16 [2048, 2816], P('fsdp', 'tp'), may hold values from -0.125 to 0.125
- shared_down: bfloat16 [2048, 2816], P('fsdp', 'tp'), may hold values from -0.109375 to 0.109375
- expert_gate: bfloat16 [64, 2048, 1408], P('fsdp', None, 'tp'), may hold values from -0.125 to 0.125
- expert_up: bfloat16 [64, 2048, 1408], P('fsdp', None, 'tp'), may hold values from -0.125 to 0.125
- expert_down: bfloat16 [64, 2048, 1408], P('fsdp', None, 'tp'), may hold values from -0.15625 to 0.15625
- lengths: int32 [32, 3], P('fsdp'), may hold values from 1 to 510, as said below
- routes: int32 [16384, 2], P('fsdp'), may hold values from 0 to 63, all different within a row; in each aligned block of 512 rows (0 to 511, 512 to 1023, ...) at most 20 rows name the same one
- cotangent: bfloat16 [16384, 2048], P(('fsdp', 'tp')), may hold values from -6 to 6
Outputs:
- output: bfloat16 [16384, 2048], P(('fsdp', 'tp'))
- grad_tokens: bfloat16 [16384, 2048], P(('fsdp', 'tp'))
- grad_g_attn: float32 [2048], P('fsdp')
- grad_w_query: float32 [2048, 2048], P('fsdp', 'tp')
- grad_w_key: float32 [2048, 512], P('fsdp', 'tp')
- grad_w_value: float32 [2048, 512], P('fsdp', 'tp')
- grad_w_out: float32 [2048, 2048], P('fsdp', 'tp')
- grad_g_ffn: float32 [2048], P('fsdp')
- grad_w_router: float32 [2048, 64], P('fsdp')
- grad_shared_gate: float32 [2048, 2816], P('fsdp', 'tp')
- grad_shared_up: float32 [2048, 2816], P('fsdp', 'tp')
- grad_shared_down: float32 [2048, 2816], P('fsdp', 'tp')
- grad_expert_gate: float32 [64, 2048, 1408], P('fsdp', None, 'tp')
- grad_expert_up: float32 [64, 2048, 1408], P('fsdp', None, 'tp')
- grad_expert_down: float32 [64, 2048, 1408], P('fsdp', None, 'tp')
Inputs may be any that keep to these rules, and one draw needn't show every extreme that they name: In each group of 512 tokens the 3 lengths sum to 512; one of them, in a place drawn from the seed, is longer than 384; in one group, drawn from the seed, the two others are 1 token each. `routes`: each token names 2 different experts; among the rows of one device (one group) no expert is named more than 20 times, a bound that some block reaches.
All inputs are finite; a program needn't handle non-finite values.
Results may differ from a plain program's by a relative error of at most 0.03.
Values may be sent and summed in bfloat16 or wider, within the bound.
No kernel may reach another device: no remote copies, remote signals or barrier semaphores. Data moves between devices by JAX's collectives and lax.ppermute only.
A program may use at most 256 MiB of HBM per device.

v0:
```python
import jax
import jax.numpy as jnp
from jax import lax
from jax.sharding import PartitionSpec as P

HEAD_SIZE = 128


epsilon = 1e-06


def contract_first(left_op, right_op):
    return lax.dot_general(
        left_op, right_op, (((0,), (0,)), ((), ())), preferred_element_type=jnp.float32
    )


def contract_last(left_op, right_op):
    return lax.dot_general(
        left_op, right_op, (((1,), (1,)), ((), ())), preferred_element_type=jnp.float32
    )


def silu_slope(values):
    sigmoid_v = jax.nn.sigmoid(values)
    return sigmoid_v * (1.0 + values * (1.0 - sigmoid_v))


def sequence_ids(seq_lens, row_count):
    seq_ends = jnp.cumsum(seq_lens)
    places = jnp.arange(row_count, dtype=jnp.int32)
    return jnp.sum((places[:, None] >= seq_ends[None, :]).astype(jnp.int32), axis=1)


def norm_rows(values, gain_vec):
    factor = lax.rsqrt(jnp.mean(values * values, axis=-1, keepdims=True) + epsilon)
    return (values * factor * gain_vec, factor)


def norm_back(values, factor, gain_vec, upstream):
    scaled_up = upstream * gain_vec
    grad_gain = jnp.sum(upstream * values * factor, axis=0)
    grad_values = factor * scaled_up - values * factor * factor * factor * jnp.mean(
        scaled_up * values, axis=-1, keepdims=True
    )
    return (grad_values, grad_gain)


def per_device(
    tokens,
    g_attn,
    query_matrix,
    key_matrix,
    value_matrix,
    w_out,
    g_ffn,
    w_router,
    shared_gate,
    shared_up,
    shared_down,
    expert_gate,
    expert_up,
    expert_down,
    lengths,
    routes,
    cotangent,
):
    tok_dev = tokens.shape[0]
    tp_count = lax.axis_size("tp")
    fsdp_count = lax.axis_size("fsdp")
    group_rows = tok_dev * tp_count
    own_start = lax.axis_index("tp") * tok_dev
    gathered = (
        lax.all_gather(g_attn, "fsdp", axis=0, tiled=True),
        lax.all_gather(query_matrix, "fsdp", axis=0, tiled=True),
        lax.all_gather(key_matrix, "fsdp", axis=0, tiled=True),
        lax.all_gather(value_matrix, "fsdp", axis=0, tiled=True),
        lax.all_gather(w_out, "fsdp", axis=0, tiled=True),
        lax.all_gather(g_ffn, "fsdp", axis=0, tiled=True),
        lax.all_gather(w_router, "fsdp", axis=0, tiled=True),
        lax.all_gather(shared_gate, "fsdp", axis=0, tiled=True),
        lax.all_gather(shared_up, "fsdp", axis=0, tiled=True),
        lax.all_gather(shared_down, "fsdp", axis=0, tiled=True),
    )
    (
        gain_one,
        full_query,
        full_key,
        full_value,
        full_out,
        gain_two,
        full_router,
        full_sgate,
        full_sup,
        full_sdown,
    ) = gathered
    gain_one = gain_one.astype(jnp.float32)
    gain_two = gain_two.astype(jnp.float32)
    token_rows, grad_rows = (
        lax.all_gather(tokens, "tp", axis=0, tiled=True),
        lax.all_gather(cotangent, "tp", axis=0, tiled=True),
    )
    residual = token_rows.astype(jnp.float32)
    grad_full = grad_rows.astype(jnp.float32)
    normed_one, factor_one = norm_rows(residual, gain_one)
    h_attn = normed_one.astype(jnp.bfloat16)
    kv_local = full_key.shape[1] // HEAD_SIZE
    heads_local = full_query.shape[1] // HEAD_SIZE
    repeat_factor = heads_local // kv_local
    query_rows = jnp.dot(h_attn, full_query, preferred_element_type=jnp.float32).astype(
        jnp.bfloat16
    )
    key_vectors = (
        jnp.dot(h_attn, full_key, preferred_element_type=jnp.float32)
        .astype(jnp.bfloat16)
        .reshape(group_rows, kv_local, HEAD_SIZE)
    )
    value_vectors = (
        jnp.dot(h_attn, full_value, preferred_element_type=jnp.float32)
        .astype(jnp.bfloat16)
        .reshape(group_rows, kv_local, HEAD_SIZE)
    )
    seq_of = sequence_ids(lengths[0], group_rows)
    places = jnp.arange(group_rows, dtype=jnp.int32)
    block_count = group_rows // group_rows
    score_scale = HEAD_SIZE ** (-0.5)
    query_blocks = query_rows.reshape(block_count, group_rows, kv_local, repeat_factor, HEAD_SIZE)
    starts = jnp.arange(block_count, dtype=jnp.int32) * group_rows

    def masked_scores(query_block, start_at):
        raw_scores = (
            jnp.einsum(
                "qgrd,kgd->grqk", query_block, key_vectors, preferred_element_type=jnp.float32
            )
            * score_scale
        )
        block_pos = start_at + jnp.arange(group_rows, dtype=jnp.int32)
        visible = (seq_of[:, None] == seq_of[None, :]) & (places[None, :] <= block_pos[:, None])
        return jnp.where(visible[None, None], raw_scores, -1e30)

    def forward_block(inputs):
        query_block, start_at = inputs
        scores = masked_scores(query_block, start_at)
        top_score = jnp.max(scores, axis=-1, keepdims=True)
        exponent = jnp.exp(scores - top_score)
        row_total = jnp.sum(exponent, axis=-1, keepdims=True)
        probability = (exponent / row_total).astype(jnp.bfloat16)
        block_out = jnp.einsum(
            "grqk,kgd->qgrd", probability, value_vectors, preferred_element_type=jnp.float32
        )
        return (block_out.astype(jnp.bfloat16), top_score[..., 0] + jnp.log(row_total[..., 0]))

    attended, log_totals = lax.map(forward_block, (query_blocks, starts))
    attended = attended.reshape(group_rows, heads_local * HEAD_SIZE)
    attn_part = contract_last(attended, full_out)
    attn_sum = lax.psum(attn_part, "tp")
    middle = residual + attn_sum
    normed_two, factor_two = norm_rows(middle, gain_two)
    h_ffn = normed_two.astype(jnp.bfloat16)
    logits = jnp.dot(h_ffn, full_router, preferred_element_type=jnp.float32)
    experts = full_router.shape[1]
    top_count = routes.shape[1]
    expert_ids = jnp.arange(experts, dtype=jnp.int32)
    route_hot = routes[:, :, None] == expert_ids[None, None, :]
    chosen = jnp.sum(jnp.where(route_hot, logits[:, None, :], 0.0), axis=-1)
    gate_vals = jax.nn.softmax(chosen, axis=-1)
    capacity = max(2, 5 * top_count * group_rows // (4 * experts))
    pair_hot = route_hot.reshape(group_rows * top_count, experts).astype(jnp.int32)
    earlier = jnp.cumsum(pair_hot, axis=0) - pair_hot
    slot_of = jnp.sum(earlier * pair_hot, axis=1).reshape(group_rows, top_count)
    position = routes * capacity + slot_of
    slot_count = experts * capacity
    slot_hot = position[:, :, None] == jnp.arange(slot_count, dtype=jnp.int32)[None, None, :]
    dispatch = jnp.any(slot_hot, axis=1).astype(jnp.bfloat16)
    slot_gate = jnp.sum(jnp.where(slot_hot, gate_vals[:, :, None], 0.0), axis=(0, 1))
    slot_source = jnp.sum(jnp.where(slot_hot, places[:, None, None], 0), axis=(0, 1))
    local_experts = expert_gate.shape[0]
    send_width = h_ffn.shape[1]
    outgoing = (
        contract_first(dispatch, h_ffn)
        .astype(jnp.bfloat16)
        .reshape(fsdp_count, local_experts, capacity, send_width)
    )
    slot_grad = (
        (slot_gate[:, None] * grad_full[slot_source])
        .astype(jnp.bfloat16)
        .reshape(fsdp_count, local_experts, capacity, send_width)
    )
    rows_in = lax.all_to_all(outgoing, "fsdp", split_axis=0, concat_axis=0, tiled=True)
    grad_in = lax.all_to_all(slot_grad, "fsdp", split_axis=0, concat_axis=0, tiled=True)
    gate_pre = jnp.einsum(
        "secd,edf->secf", rows_in, expert_gate, preferred_element_type=jnp.float32
    )
    up_pre = jnp.einsum("secd,edf->secf", rows_in, expert_up, preferred_element_type=jnp.float32)
    hidden = (jax.nn.silu(gate_pre) * up_pre).astype(jnp.bfloat16)
    partial_out = jnp.einsum(
        "secf,edf->secd", hidden, expert_down, preferred_element_type=jnp.float32
    )
    returned = lax.all_to_all(
        partial_out.astype(jnp.bfloat16), "fsdp", split_axis=0, concat_axis=0, tiled=True
    ).astype(partial_out.dtype)
    returned, kept_gate, kept_up, kept_rows, at_experts = (
        returned,
        gate_pre,
        up_pre,
        rows_in,
        grad_in,
    )
    flat_back = returned.reshape(slot_count, send_width)
    picked = flat_back[position]
    routed = jnp.sum(gate_vals[:, :, None] * picked, axis=1)
    s_gate_pre = jnp.dot(h_ffn, full_sgate, preferred_element_type=jnp.float32)
    s_up_pre = jnp.dot(h_ffn, full_sup, preferred_element_type=jnp.float32)
    s_hidden = (jax.nn.silu(s_gate_pre) * s_up_pre).astype(jnp.bfloat16)
    shared_out = contract_last(s_hidden, full_sdown)
    expert_own = lax.psum_scatter(
        (routed + shared_out).astype(jnp.bfloat16), "tp", scatter_dimension=0, tiled=True
    ).astype(jnp.float32)
    middle_own = lax.dynamic_slice_in_dim(middle, own_start, tok_dev, 0)
    output = (middle_own + expert_own).astype(jnp.bfloat16)
    grad_sdown = contract_first(grad_rows, s_hidden)
    grad_shidden = jnp.dot(grad_rows, full_sdown, preferred_element_type=jnp.float32)
    grad_sgate_pre = (grad_shidden * s_up_pre * silu_slope(s_gate_pre)).astype(jnp.bfloat16)
    grad_sup_pre = (grad_shidden * jax.nn.silu(s_gate_pre)).astype(jnp.bfloat16)
    grad_sgate = contract_first(h_ffn, grad_sgate_pre)
    grad_sup = contract_first(h_ffn, grad_sup_pre)
    grad_h_ffn = contract_last(grad_sgate_pre, full_sgate) + contract_last(grad_sup_pre, full_sup)
    grad_gates = jnp.sum(grad_full[:, None, :] * picked, axis=-1)
    hidden_again = (jax.nn.silu(kept_gate) * kept_up).astype(jnp.bfloat16)
    grad_edown = jnp.einsum(
        "secd,secf->edf", at_experts, hidden_again, preferred_element_type=jnp.float32
    )
    grad_hidden = jnp.einsum(
        "secd,edf->secf", at_experts, expert_down, preferred_element_type=jnp.float32
    )
    grad_gate_pre = (grad_hidden * kept_up * silu_slope(kept_gate)).astype(jnp.bfloat16)
    grad_up_pre = (grad_hidden * jax.nn.silu(kept_gate)).astype(jnp.bfloat16)
    grad_egate = jnp.einsum(
        "secd,secf->edf", kept_rows, grad_gate_pre, preferred_element_type=jnp.float32
    )
    grad_expert_up_weight = jnp.einsum(
        "secd,secf->edf", kept_rows, grad_up_pre, preferred_element_type=jnp.float32
    )
    grad_sent = jnp.einsum(
        "secf,edf->secd", grad_gate_pre, expert_gate, preferred_element_type=jnp.float32
    ) + jnp.einsum("secf,edf->secd", grad_up_pre, expert_up, preferred_element_type=jnp.float32)
    grad_returned = (
        lax.all_to_all(
            grad_sent.astype(jnp.bfloat16), "fsdp", split_axis=0, concat_axis=0, tiled=True
        )
        .astype(grad_sent.dtype)
        .reshape(slot_count, send_width)
    )
    grad_routed = jnp.sum(grad_returned[position], axis=1)
    grad_h_ffn = grad_h_ffn + grad_routed
    grad_h_ffn, grad_gates = (
        lax.psum(grad_h_ffn.astype(jnp.bfloat16), "tp").astype(jnp.float32),
        lax.psum(grad_gates.astype(jnp.bfloat16), "tp").astype(jnp.float32),
    )
    grad_chosen = gate_vals * (grad_gates - jnp.sum(gate_vals * grad_gates, axis=-1, keepdims=True))
    grad_logits = jnp.sum(jnp.where(route_hot, grad_chosen[:, :, None], 0.0), axis=1).astype(
        jnp.bfloat16
    )
    grad_router = contract_first(h_ffn, grad_logits)
    grad_h_ffn = grad_h_ffn + contract_last(grad_logits, full_router)
    grad_middle, grad_gain_two = norm_back(middle, factor_two, gain_two, grad_h_ffn)
    grad_middle = grad_middle + grad_full
    grad_att = grad_middle.astype(jnp.bfloat16)
    grad_wout = contract_first(grad_att, attended)
    grad_attended = (
        jnp.dot(grad_att, full_out, preferred_element_type=jnp.float32)
        .astype(jnp.bfloat16)
        .reshape(block_count, group_rows, kv_local, repeat_factor, HEAD_SIZE)
    )

    def backward_block(accum_pair, inputs):
        key_acc, value_acc = accum_pair
        query_block, grad_block, log_block, start_at = inputs
        scores = masked_scores(query_block, start_at)
        probability = jnp.exp(scores - log_block[..., None])
        grad_prob = jnp.einsum(
            "qgrd,kgd->grqk", grad_block, value_vectors, preferred_element_type=jnp.float32
        )
        grad_scores = (
            probability * (grad_prob - jnp.sum(probability * grad_prob, axis=-1, keepdims=True))
        ).astype(jnp.bfloat16)
        grad_query = (
            jnp.einsum(
                "grqk,kgd->qgrd", grad_scores, key_vectors, preferred_element_type=jnp.float32
            )
            * score_scale
        ).astype(jnp.bfloat16)
        key_acc = (
            key_acc
            + jnp.einsum(
                "grqk,qgrd->kgd", grad_scores, query_block, preferred_element_type=jnp.float32
            )
            * score_scale
        )
        value_acc = value_acc + jnp.einsum(
            "grqk,qgrd->kgd",
            probability.astype(jnp.bfloat16),
            grad_block,
            preferred_element_type=jnp.float32,
        )
        return ((key_acc, value_acc), grad_query)

    zeros_kv = jnp.zeros((group_rows, kv_local, HEAD_SIZE), jnp.float32)
    (key_acc, value_acc), grad_queries = lax.scan(
        backward_block, (zeros_kv, zeros_kv), (query_blocks, grad_attended, log_totals, starts)
    )
    grad_queries = grad_queries.reshape(group_rows, heads_local * HEAD_SIZE)
    grad_keys = key_acc.astype(jnp.bfloat16).reshape(group_rows, kv_local * HEAD_SIZE)
    grad_values = value_acc.astype(jnp.bfloat16).reshape(group_rows, kv_local * HEAD_SIZE)
    grad_wquery = contract_first(h_attn, grad_queries)
    grad_wkey = contract_first(h_attn, grad_keys)
    grad_wvalue = contract_first(h_attn, grad_values)
    grad_h_attn = (
        contract_last(grad_queries, full_query)
        + contract_last(grad_keys, full_key)
        + contract_last(grad_values, full_value)
    )
    grad_h_attn = lax.psum(grad_h_attn.astype(jnp.bfloat16), "tp").astype(jnp.float32)
    grad_resid, grad_gain_one = norm_back(residual, factor_one, gain_one, grad_h_attn)
    grad_resid = grad_resid + grad_middle
    grad_tokens = lax.dynamic_slice_in_dim(grad_resid, own_start, tok_dev, 0).astype(jnp.bfloat16)
    grad_sums = (
        lax.psum_scatter(
            grad_gain_one.astype(jnp.bfloat16), "fsdp", scatter_dimension=0, tiled=True
        ).astype(jnp.float32),
        lax.psum_scatter(
            grad_wquery.astype(jnp.bfloat16), "fsdp", scatter_dimension=0, tiled=True
        ).astype(jnp.float32),
        lax.psum_scatter(
            grad_wkey.astype(jnp.bfloat16), "fsdp", scatter_dimension=0, tiled=True
        ).astype(jnp.float32),
        lax.psum_scatter(
            grad_wvalue.astype(jnp.bfloat16), "fsdp", scatter_dimension=0, tiled=True
        ).astype(jnp.float32),
        lax.psum_scatter(
            grad_wout.astype(jnp.bfloat16), "fsdp", scatter_dimension=0, tiled=True
        ).astype(jnp.float32),
        lax.psum_scatter(
            grad_gain_two.astype(jnp.bfloat16), "fsdp", scatter_dimension=0, tiled=True
        ).astype(jnp.float32),
        lax.psum_scatter(
            grad_router.astype(jnp.bfloat16), "fsdp", scatter_dimension=0, tiled=True
        ).astype(jnp.float32),
        lax.psum_scatter(
            grad_sgate.astype(jnp.bfloat16), "fsdp", scatter_dimension=0, tiled=True
        ).astype(jnp.float32),
        lax.psum_scatter(
            grad_sup.astype(jnp.bfloat16), "fsdp", scatter_dimension=0, tiled=True
        ).astype(jnp.float32),
        lax.psum_scatter(
            grad_sdown.astype(jnp.bfloat16), "fsdp", scatter_dimension=0, tiled=True
        ).astype(jnp.float32),
    )
    return (
        output,
        grad_tokens,
        grad_sums[0],
        grad_sums[1],
        grad_sums[2],
        grad_sums[3],
        grad_sums[4],
        grad_sums[5],
        grad_sums[6],
        grad_sums[7],
        grad_sums[8],
        grad_sums[9],
        grad_egate,
        grad_expert_up_weight,
        grad_edown,
    )


def solution(mesh):
    in_specs = (
        P(("fsdp", "tp"), None),
        P("fsdp"),
        P("fsdp", "tp"),
        P("fsdp", "tp"),
        P("fsdp", "tp"),
        P("fsdp", "tp"),
        P("fsdp"),
        P("fsdp", None),
        P("fsdp", "tp"),
        P("fsdp", "tp"),
        P("fsdp", "tp"),
        P("fsdp", None, "tp"),
        P("fsdp", None, "tp"),
        P("fsdp", None, "tp"),
        P("fsdp", None),
        P("fsdp", None),
        P(("fsdp", "tp"), None),
    )
    out_specs = (
        P(("fsdp", "tp"), None),
        P(("fsdp", "tp"), None),
        P("fsdp"),
        P("fsdp", "tp"),
        P("fsdp", "tp"),
        P("fsdp", "tp"),
        P("fsdp", "tp"),
        P("fsdp"),
        P("fsdp", None),
        P("fsdp", "tp"),
        P("fsdp", "tp"),
        P("fsdp", "tp"),
        P("fsdp", None, "tp"),
        P("fsdp", None, "tp"),
        P("fsdp", None, "tp"),
    )
    return jax.shard_map(
        per_device, mesh=mesh, in_specs=in_specs, out_specs=out_specs, check_vma=False
    )
```

profile of v0, /device:TPU:1, one launch (start us, length us, event | category | flops | bytes accessed | tf_op | source)
XLA Modules:
  0.0 2689.4 jit_solution(7213015488341789346)
XLA Ops:
  13.2 86.0 %all-reduce.5 = (bf16[2048]{0:T(1024)(128)(2,1)S(1)}, bf16[2048]{0:T(1024)(128)(2,1)S(1)}) all-reduce(bf16[2048]{0:T(1024)(128)(2,1)S(1)} %dynamic-update-slice, bf16[2048]{0:T(1024)(128)(2,1)S(1)} %dynamic-update-slice.1), channel_id=1, replica_groups=mesh['fsdp'=32,'tp'=4] {'fsdp'}, use_global_device_ids=true, to_apply=%add | all-reduce | flops 4096 | bytes 16384
  101.0 77.8 %all_gather.38 = bf16[2048,128]{1,0:T(8,128)(2,1)S(1)} all-gather(bf16[64,128]{1,0:T(8,128)(2,1)} %param.21), channel_id=1, replica_groups=mesh['fsdp'=32,'tp'=4] {'fsdp'}, dimensions={0}, use_global_device_ids=true | all-gather | bytes 540672 | tf_op jit(solution)/shard_map/all_gather | solution.py:77
  178.8 82.8 %all_gather.39 = bf16[2048,128]{1,0:T(8,128)(2,1)} all-gather(bf16[64,128]{1,0:T(8,128)(2,1)} %param.20), channel_id=1, replica_groups=mesh['fsdp'=32,'tp'=4] {'fsdp'}, dimensions={0}, use_global_device_ids=true | all-gather | bytes 540672 | tf_op jit(solution)/shard_map/all_gather | solution.py:76
  282.6 18.0 reduce-window.19
  302.8 105.9 %all-reduce.10.cloned.1.call-done = f32[512,2048]{1,0:T(8,128)} async-done(((f32[512,2048]{1,0:T(8,128)}), f32[512,2048]{1,0:T(8,128)}) %all-reduce.10.cloned.1.call-update) | async-done | bytes 4194320 | tf_op jit(solution)/shard_map/psum | solution.py:156
  451.6 146.1 %all_gather.43 = bf16[2048,64]{1,0:T(8,128)(2,1)S(1)} all-gather(bf16[64,64]{1,0:T(8,128)(2,1)S(1)} %copy-done.54), channel_id=1, replica_groups=mesh['fsdp'=32,'tp'=4] {'fsdp'}, dimensions={0}, use_global_device_ids=true | all-gather | bytes 270336 | tf_op jit(solution)/shard_map/all_gather | solution.py:80
  602.0 13.0 gather_fusion.1
  615.0 12.5 gather.13
  639.3 11.1 copy.209
  673.4 38.9 %all-to-all-done.2 = bf16[32,2,20,2048]{3,1,2,0:T(2,128)(2,1)} async-done(((bf16[32,2,20,2048]{3,1,2,0:T(2,128)(2,1)}), bf16[32,2,20,2048]{3,1,2,0:T(2,128)(2,1)}, u32[]{:S(2)}, u32[]{:S(2)}) %all-to-all-start.2) | async-done | bytes 5242912 | tf_op jit(solution)/shard_map/all_to_all | solution.py:190
  740.5 17.3 all-to-all-start.3
  769.3 52.7 %all-gather.18.cloned.1.call-done = bf16[2048,704]{1,0:T(8,128)(2,1)} async-done(((bf16[64,704]{1,0:T(8,128)(2,1)}), bf16[2048,704]{1,0:T(8,128)(2,1)}) %all-gather.18.cloned.1.call-update) | async-done | bytes 2883600 | tf_op jit(solution)/shard_map/all_gather | solution.py:83
  843.0 14.9 copy.215
  857.8 12.7 reshape.339
  870.6 13.0 gather_fusion.2
  894.1 13.3 reduce_sum.186
  946.6 11.6 all-to-all-start.1
  964.4 75.9 %all-to-all-done.1 = bf16[32,2,20,2048]{3,1,2,0:T(2,128)(2,1)} async-done(((bf16[32,2,20,2048]{3,1,2,0:T(2,128)(2,1)}), bf16[32,2,20,2048]{3,1,2,0:T(2,128)(2,1)}, u32[]{:S(2)}, u32[]{:S(2)}) %all-to-all-start.1) | async-done | bytes 5242912 | tf_op jit(solution)/shard_map/all_to_all | solution.py:199
  1049.7 14.7 copy.207
  1064.4 12.9 reshape.337
  1077.4 13.0 gather_fusion
  1101.0 19.7 multiply_reduce_fusion
  1212.5 29.8 %reduce-scatter.28.cloned.1.call-done = bf16[64,704]{1,0:T(8,128)(2,1)} async-done(((bf16[2048,704]{1,0:T(8,128)(2,1)}), bf16[64,704]{1,0:T(8,128)(2,1)}) %reduce-scatter.28.cloned.1.call-update) | async-done | bytes 90128
  1244.1 225.0 %reduce-scatter.24.cloned.1.call-done = bf16[64,704]{1,0:T(8,128)(2,1)} async-done(((bf16[2048,704]{1,0:T(8,128)(2,1)}), bf16[64,704]{1,0:T(8,128)(2,1)}) %reduce-scatter.24.cloned.1.call-update) | async-done | bytes 90128 | tf_op jit(solution)/shard_map/reduce_scatter | solution.py:349
  1470.6 225.2 %reduce-scatter.26.cloned.1.call-done = bf16[64,704]{1,0:T(8,128)(2,1)} async-done(((bf16[2048,704]{1,0:T(8,128)(2,1)}), bf16[64,704]{1,0:T(8,128)(2,1)}) %reduce-scatter.26.cloned.1.call-update) | async-done | bytes 90128 | tf_op jit(solution)/shard_map/reduce_scatter | solution.py:352
  1697.5 158.3 %reduce-scatter.22.cloned.1.call-done = bf16[64,64]{1,0:T(8,128)(2,1)} async-done(((bf16[2048,64]{1,0:T(8,128)(2,1)}), bf16[64,64]{1,0:T(8,128)(2,1)}) %reduce-scatter.22.cloned.1.call-update) | async-done | bytes 8208 | tf_op jit(solution)/shard_map/reduce_scatter | solution.py:346
  1857.1 180.3 %reduce-scatter.16.cloned.1.call-done = bf16[64,128]{1,0:T(8,128)(2,1)} async-done(((bf16[2048,128]{1,0:T(8,128)(2,1)}), bf16[64,128]{1,0:T(8,128)(2,1)}) %reduce-scatter.16.cloned.1.call-update) | async-done | bytes 16400 | tf_op jit(solution)/shard_map/reduce_scatter | solution.py:334
  2038.8 179.9 %reduce-scatter.18.cloned.1.call-done = bf16[64,128]{1,0:T(8,128)(2,1)} async-done(((bf16[2048,128]{1,0:T(8,128)(2,1)}), bf16[64,128]{1,0:T(8,128)(2,1)}) %reduce-scatter.18.cloned.1.call-update) | async-done | bytes 16400 | tf_op jit(solution)/shard_map/reduce_scatter | solution.py:337
  2220.1 79.7 %all-reduce.14.cloned.1.call-done = bf16[512,2048]{1,0:T(8,128)(2,1)} async-done(((bf16[512,2048]{1,0:T(8,128)(2,1)}), bf16[512,2048]{1,0:T(8,128)(2,1)}) %all-reduce.14.cloned.1.call-update) | async-done | bytes 2097168 | tf_op jit(solution)/shard_map/psum | solution.py:323
  2306.9 85.2 %all-reduce.4 = (bf16[2048]{0:T(1024)(128)(2,1)S(1)}, bf16[2048]{0:T(1024)(128)(2,1)S(1)}) all-reduce(bf16[2048]{0:T(1024)(128)(2,1)S(1)} %get-tuple-element.181, bf16[2048]{0:T(1024)(128)(2,1)S(1)} %get-tuple-element.177), channel_id=3, replica_groups=mesh['fsdp'=32,'tp'=4] {'fsdp'}, use_global_device_ids=true, to_apply=%region_29.30.clone | all-reduce | flops 4096 | bytes 16384
  2397.9 100.9 %reduce-scatter.14.cloned.1.call-done = bf16[64,512]{1,0:T(8,128)(2,1)} async-done(((bf16[2048,512]{1,0:T(8,128)(2,1)}), bf16[64,512]{1,0:T(8,128)(2,1)}) %reduce-scatter.14.cloned.1.call-update) | async-done | bytes 65552 | tf_op jit(solution)/shard_map/reduce_scatter | solution.py:331
  2500.3 180.9 %reduce-scatter.20.cloned.1.call-done = bf16[64,512]{1,0:T(8,128)(2,1)} async-done(((bf16[2048,512]{1,0:T(8,128)(2,1)}), bf16[64,512]{1,0:T(8,128)(2,1)}) %reduce-scatter.20.cloned.1.call-update) | async-done | bytes 65552 | tf_op jit(solution)/shard_map/reduce_scatter | solution.py:340
  (290 shorter events, 363.8 us)
Async XLA Ops:
  7.2 705.2 %copy-start = (bf16[2,2048,352]{1,2,0:T(8,128)(2,1)S(1)}, bf16[2,2048,352]{1,2,0:T(8,128)(2,1)}, u32[]{:S(2)}) copy-start(bf16[2,2048,352]{1,2,0:T(8,128)(2,1)} %param.30) | copy-start | bytes 8650756
  7.2 254.4 %all-gather.8.cloned.1.call-start = ((), (), s32[]{:S(2)}) async-start(), calls=%async_computation.13 | async-start | bytes 2621440 | tf_op jit(solution)/shard_map/all_gather | solution.py:100
  7.9 259.7 %all-gather.10.cloned.1.call-start = ((), (), s32[]{:S(2)}) async-start(), calls=%async_computation.14 | async-start | bytes 2162688 | tf_op jit(solution)/shard_map/all_gather | solution.py:75
  8.7 267.1 %all-gather.12.cloned.1.call-start = ((), (), s32[]{:S(2)}) async-start(), calls=%async_computation.15 | async-start | bytes 2162688 | tf_op jit(solution)/shard_map/all_gather | solution.py:78
  9.4 399.3 %all-reduce.10.cloned.1.call-start = ((), (), s32[]{:S(2)}) async-start(), calls=%async_computation.16 | async-start | bytes 8388608 | tf_op jit(solution)/shard_map/psum | solution.py:156
  99.1 168.5 %copy-start.47 = (f32[2048]{0:T(1024)}, f32[2048]{0:T(1024)S(1)}, u32[]{:S(2)}) copy-start(f32[2048]{0:T(1024)S(1)} %convert_element_type.231) | copy-start | bytes 24580
  178.8 88.9 %copy-start.22 = (bf16[2048,128]{1,0:T(8,128)(2,1)}, bf16[2048,128]{1,0:T(8,128)(2,1)S(1)}, u32[]{:S(2)}) copy-start(bf16[2048,128]{1,0:T(8,128)(2,1)S(1)} %all_gather.38) | copy-start | bytes 1572868
  280.9 316.8 %all-gather.20.cloned.1.call-start = ((), (), s32[]{:S(2)}) async-start(), calls=%async_computation.21 | async-start | bytes 2621440 | tf_op jit(solution)/shard_map/all_gather | solution.py:101
  281.5 477.1 %all-gather.14.cloned.1.call-start = ((), (), s32[]{:S(2)}) async-start(), calls=%async_computation.17 | async-start | bytes 3244032 | tf_op jit(solution)/shard_map/all_gather | solution.py:81
  301.6 110.7 %copy-start.38 = (f32[2048]{0:T(1024)}, f32[2048]{0:T(1024)S(1)}, u32[]{:S(2)}) copy-start(f32[2048]{0:T(1024)S(1)} %convert_element_type.241) | copy-start | bytes 24580
  440.8 209.6 %all-to-all-start = ((bf16[32,2,20,2048]{3,1,2,0:T(2,128)(2,1)}), bf16[32,2,20,2048]{3,1,2,0:T(2,128)(2,1)}, u32[]{:S(2)}, u32[]{:S(2)}) async-start(bf16[32,2,20,2048]{3,1,2,0:T(2,128)(2,1)} %copy.201), calls=%async_computation | async-start | bytes 10485760 | tf_op jit(solution)/shard_map/all_to_all | solution.py:189
  450.2 313.8 %all-gather.16.cloned.1.call-start = ((), (), s32[]{:S(2)}) async-start(), calls=%async_computation.18 | async-start | bytes 3244032 | tf_op jit(solution)/shard_map/all_gather | solution.py:82
  597.7 29.7 %copy-start.13 = (bf16[2048,64]{1,0:T(8,128)(2,1)}, bf16[2048,64]{1,0:T(8,128)(2,1)S(1)}, u32[]{:S(2)}) copy-start(bf16[2048,64]{1,0:T(8,128)(2,1)S(1)} %all_gather.43) | copy-start | bytes 786436
  650.4 62.0 %all-to-all-start.2 = ((bf16[32,2,20,2048]{3,1,2,0:T(2,128)(2,1)}), bf16[32,2,20,2048]{3,1,2,0:T(2,128)(2,1)}, u32[]{:S(2)}, u32[]{:S(2)}) async-start(bf16[32,2,20,2048]{3,1,2,0:T(2,128)(2,1)} %copy.209), calls=%async_computation.3 | async-start | bytes 10485760 | tf_op jit(solution)/shard_map/all_to_all | solution.py:190
  655.3 166.8 %all-gather.18.cloned.1.call-start = ((), (), s32[]{:S(2)}) async-start(), calls=%async_computation.19 | async-start | bytes 3244032 | tf_op jit(solution)/shard_map/all_gather | solution.py:83
  740.5 17.8 copy-start.53
  740.5 93.0 %all-to-all-start.3 = ((bf16[32,2,20,2048]{3,1,2,0:T(2,128)(2,1)}), bf16[32,2,20,2048]{3,1,2,0:T(2,128)(2,1)}, u32[]{:S(2)}, u32[]{:S(2)}) async-start(bf16[32,2,20,2048]{3,1,2,0:T(2,128)(2,1)} %copy.213), calls=%async_computation.4 | async-start | bytes 10485760 | tf_op jit(solution)/shard_map/all_to_all | solution.py:248
  757.8 374.8 %all-reduce.12.cloned.1.call-start = ((), (), s32[]{:S(2)}) async-start(), calls=%async_computation.22 | async-start | bytes 4194304 | tf_op jit(solution)/shard_map/psum | solution.py:257
  915.1 327.1 %reduce-scatter.28.cloned.1.call-start = ((), (), s32[]{:S(2)}) async-start(), calls=%async_computation.31 | async-start | bytes 3244032
  925.1 544.0 %reduce-scatter.24.cloned.1.call-start = ((), (), s32[]{:S(2)}) async-start(), calls=%async_computation.29 | async-start | bytes 3244032 | tf_op jit(solution)/shard_map/reduce_scatter | solution.py:349
  946.6 93.7 %all-to-all-start.1 = ((bf16[32,2,20,2048]{3,1,2,0:T(2,128)(2,1)}), bf16[32,2,20,2048]{3,1,2,0:T(2,128)(2,1)}, u32[]{:S(2)}, u32[]{:S(2)}) async-start(bf16[32,2,20,2048]{3,1,2,0:T(2,128)(2,1)} %copy.205), calls=%async_computation.1 | async-start | bytes 10485760 | tf_op jit(solution)/shard_map/all_to_all | solution.py:199
  958.2 737.7 %reduce-scatter.26.cloned.1.call-start = ((), (), s32[]{:S(2)}) async-start(), calls=%async_computation.30 | async-start | bytes 3244032 | tf_op jit(solution)/shard_map/reduce_scatter | solution.py:352
  964.1 891.7 %reduce-scatter.22.cloned.1.call-start = ((), (), s32[]{:S(2)}) async-start(), calls=%async_computation.28 | async-start | bytes 540672 | tf_op jit(solution)/shard_map/reduce_scatter | solution.py:346
  1101.0 26.9 copy-start.35
  1101.0 28.3 %copy-start.43 = (s32[512,2]{0,1:T(2,128)S(1)}, s32[512,2]{0,1:T(2,128)}, u32[]{:S(2)}) copy-start(s32[512,2]{0,1:T(2,128)} %param.32) | copy-start | bytes 12292
  1120.8 11.8 copy-start.14
  1132.5 905.0 %reduce-scatter.16.cloned.1.call-start = ((), (), s32[]{:S(2)}) async-start(), calls=%async_computation.25 | async-start | bytes 540672 | tf_op jit(solution)/shard_map/reduce_scatter | solution.py:334
  1149.6 1069.1 %reduce-scatter.18.cloned.1.call-start = ((), (), s32[]{:S(2)}) async-start(), calls=%async_computation.26 | async-start | bytes 540672 | tf_op jit(solution)/shard_map/reduce_scatter | solution.py:337
  1159.2 1140.6 %all-reduce.14.cloned.1.call-start = ((), (), s32[]{:S(2)}) async-start(), calls=%async_computation.23 | async-start | bytes 4194304 | tf_op jit(solution)/shard_map/psum | solution.py:323
  1167.8 1227.8 %reduce-scatter.12.cloned.1.call-start = ((), (), s32[]{:S(2)}) async-start(), calls=%async_computation.20 | async-start | bytes 2621440 | tf_op jit(solution)/shard_map/reduce_scatter | solution.py:216
  1174.5 1324.3 %reduce-scatter.14.cloned.1.call-start = ((), (), s32[]{:S(2)}) async-start(), calls=%async_computation.24 | async-start | bytes 2162688 | tf_op jit(solution)/shard_map/reduce_scatter | solution.py:331
  1179.2 1502.1 %reduce-scatter.20.cloned.1.call-start = ((), (), s32[]{:S(2)}) async-start(), calls=%async_computation.27 | async-start | bytes 2162688 | tf_op jit(solution)/shard_map/reduce_scatter | solution.py:340
  (51 other events, 218.5 us)
Sparse Core Ops, SparseCore 0:
  9.7 33.3 all-gather.7
  46.3 69.9 all-gather.9
  119.5 69.9 all-gather.11
  281.1 127.6 all-reduce.9
  410.4 30.0 all-gather.19
  443.7 123.8 all-gather.13
  571.0 74.3 all-gather.15
  659.6 162.4 all-gather.17
  915.3 77.9 all-reduce.11
  998.0 244.1 reduce-scatter.27
  1247.1 221.8 reduce-scatter.23
  1473.9 221.9 reduce-scatter.25
  1698.2 157.5 reduce-scatter.21
  1858.7 178.7 reduce-scatter.15
  2039.7 179.0 reduce-scatter.17
  2221.3 78.4 all-reduce.13
  2302.1 29.7 reduce-scatter.11
  2334.1 164.5 reduce-scatter.13
  2501.2 180.0 reduce-scatter.19
where the time goes:
time: 2720 us; the launch traced here: 2690 us
  waiting for transfers between devices  1640 us (60%)
  blocking collectives  484 us (18%)
  local copies, waits for them, and re-layouts  204 us (8%)
  matrix products  180 us (7%)
  other arithmetic  121 us (4%)
  starting transfers between devices  46.1 us (2%)
    reduce_scatter x1, waiting for transfers between devices, per_device(): lax.psum_scatter(grad_sup.astype(jnp.bfloat16), 'fsdp', scatter_dimension...  225 us
    reduce_scatter x1, waiting for transfers between devices, per_device(): lax.psum_scatter(grad_sgate.astype(jnp.bfloat16), 'fsdp', scatter_dimensi...  225 us
    reduce_scatter x1, waiting for transfers between devices, per_device(): lax.psum_scatter(grad_wout.astype(jnp.bfloat16), 'fsdp', scatter_dimensio...  181 us
    reduce_scatter x1, waiting for transfers between devices, per_device(): lax.psum_scatter(grad_wkey.astype(jnp.bfloat16), 'fsdp', scatter_dimensio...  180 us
    reduce_scatter x1, waiting for transfers between devices, per_device(): lax.psum_scatter(grad_wvalue.astype(jnp.bfloat16), 'fsdp', scatter_dimens...  180 us
    unnamed x2, blocking collectives  171 us
    reduce_scatter x1, waiting for transfers between devices, per_device(): lax.psum_scatter(grad_router.astype(jnp.bfloat16), 'fsdp', scatter_dimens...  158 us
    all_gather x1, blocking collectives, per_device(): lax.all_gather(w_router, 'fsdp', axis=0, tiled=True)  146 us
  transfers between devices with their start and end apart: 23, of which 13 were waited for; matrix products, arithmetic and copies ran while one was open for 15% of the time, Pallas kernels for 0%

commit v1 on v0

v1 whole, which is shorter than its diff:
```python
import functools

import jax
import jax.numpy as jnp
from jax import lax
from jax.experimental import pallas as pl
from jax.experimental.pallas import tpu as pltpu
from jax.sharding import PartitionSpec as P

HEAD_SIZE = 128
NZ, NX, NY = 4, 2, 4
FSDP = NZ * NX * NY
TP = 4
CAP = 20
LANES = 128
BLOCK_ORDER = (0, 2, 1, 3)
bf16 = jnp.bfloat16
f32 = jnp.float32

epsilon = 1e-06


def contract_first(left_op, right_op):
    return lax.dot_general(
        left_op, right_op, (((0,), (0,)), ((), ())), preferred_element_type=f32
    )


def contract_last(left_op, right_op):
    return lax.dot_general(
        left_op, right_op, (((1,), (1,)), ((), ())), preferred_element_type=f32
    )


def matmul(left_op, right_op):
    return jnp.dot(left_op, right_op, preferred_element_type=f32)


def silu_slope(values):
    sigmoid_v = jax.nn.sigmoid(values)
    return sigmoid_v * (1.0 + values * (1.0 - sigmoid_v))


def norm_rows(values, gain_vec):
    factor = lax.rsqrt(jnp.mean(values * values, axis=-1, keepdims=True) + epsilon)
    return (values * factor * gain_vec, factor)


def norm_back(values, factor, gain_vec, upstream):
    scaled_up = upstream * gain_vec
    return factor * scaled_up - values * factor * factor * factor * jnp.mean(
        scaled_up * values, axis=-1, keepdims=True
    )


def move_fsdp(values, dz, dx, dy):
    pairs = []
    for z in range(NZ):
        for x in range(NX):
            for y in range(NY):
                target = (((z + dz) % NZ) * NX + (x + dx) % NX) * NY + (y + dy) % NY
                pairs.append(((z * NX + x) * NY + y, target))
    return lax.ppermute(values, "fsdp", pairs)


def move_tp(values, flip):
    return lax.ppermute(values, "tp", [(i, i ^ flip) for i in range(TP)])


def gather_tp(own):
    pair = jnp.concatenate([own, move_tp(own, 2)], axis=0)
    return jnp.concatenate([pair, move_tp(pair, 1)], axis=0)


def scatter_tp(near_part, far_part):
    summed = near_part + move_tp(far_part.astype(bf16), 1).astype(f32)
    rows = summed.shape[0] // 2
    return summed[:rows] + move_tp(summed[rows:].astype(bf16), 2).astype(f32)


def small_sum_tp(values):
    return values + move_tp(values, 1) + move_tp(values, 2) + move_tp(values, 3)


def swap_fsdp(values):
    shape = values.shape
    blocks = values.reshape(FSDP, shape[0] // FSDP, shape[1])
    return lax.all_to_all(blocks, "fsdp", split_axis=0, concat_axis=0, tiled=True).reshape(shape)


def place_kernel(cuts, spot, *refs):
    first, second = refs[:NZ], refs[NZ : NZ + NY]
    outs = refs[NZ + NY :]
    z, x, y = spot[0], spot[1], spot[2]
    half = first[0].shape[3]
    for zr in range(NZ):
        for xr in range(NX):
            for yr in range(NY):
                at = (lax.rem(z + zr, NZ), lax.rem(x + xr, NX), lax.rem(y + yr, NY))
                for number, (item, start, width) in enumerate(cuts):
                    columns = slice(start, start + width)
                    outs[number][at[0], at[1], at[2], :half] = first[zr][yr, xr, item, :, columns]
                    outs[number][at[0], at[1], at[2], half:] = second[yr][zr, xr, item, :, columns]


def gather_fsdp(stacked, spot, cuts):
    items, rows, columns = stacked.shape
    half = rows // 2
    pair = jnp.stack([stacked, move_fsdp(stacked, 0, 1, 0)])
    near_y, near_z = pair[:, :, :half], pair[:, :, half:]
    by_y = jnp.stack([near_y] + [move_fsdp(near_y, 0, 0, -r) for r in range(1, NY)])
    by_z = jnp.stack([near_z] + [move_fsdp(near_z, -r, 0, 0) for r in range(1, NZ)])
    first = [by_y] + [move_fsdp(by_y, -r, 0, 0) for r in range(1, NZ)]
    second = [by_z] + [move_fsdp(by_z, 0, 0, -r) for r in range(1, NY)]
    total = FSDP * rows
    wholes = pl.pallas_call(
        functools.partial(place_kernel, cuts),
        out_shape=[jax.ShapeDtypeStruct((NZ, NX, NY, rows, width), bf16) for _, _, width in cuts],
        in_specs=[pl.BlockSpec(memory_space=pltpu.SMEM)]
        + [pl.BlockSpec(memory_space=pltpu.VMEM)] * (NZ + NY),
        out_specs=[pl.BlockSpec(memory_space=pltpu.VMEM)] * len(cuts),
        compiler_params=pltpu.CompilerParams(vmem_limit_bytes=32 * 1024 * 1024),
        cost_estimate=pl.CostEstimate(
            flops=0, bytes_accessed=4 * total * sum(w for _, _, w in cuts), transcendentals=0
        ),
        name="place",
    )(spot, *first, *second)
    return [whole.reshape(total, width) for whole, (_, _, width) in zip(wholes, cuts)]


def pick(values, index, axis):
    return lax.dynamic_index_in_dim(values, index, axis, keepdims=False)


def scatter_fsdp(join, grads, spot):
    z, x, y = spot[0], spot[1], spot[2]
    rows = grads[0].shape[0] // FSDP
    views = [g.reshape(NZ, NX, NY, 2, rows // 2, g.shape[1]) for g in grads]
    joined = lambda parts: join([p[None] for p in parts])

    def first_sum(cut, count, send):
        total = cut(0).astype(f32)
        for r in range(1, count):
            total = total + send(cut(r), r).astype(f32)
        return total.astype(bf16)

    def last_sum(kept):
        mine, theirs = pick(kept, x, 1), pick(kept, 1 - x, 1)
        return mine.astype(f32) + move_fsdp(theirs, 0, 1, 0).astype(f32)

    def send_z(part, r):
        return move_fsdp(part, r, 0, 0)

    def send_y(part, r):
        return move_fsdp(part, 0, 0, r)

    def z_index(r):
        return lax.rem(z + r, NZ)

    def y_index(r):
        return lax.rem(y + r, NY)

    one = first_sum(lambda r: joined([pick(v, z_index(r), 0)[:, :, 0] for v in views]), NZ, send_z)
    two = first_sum(
        lambda r: joined([pick(v, y_index(r), 2)[:, :, 1] for v in views]), NY, send_y
    )
    one = first_sum(lambda r: pick(one, y_index(r), 2), NY, send_y)
    two = first_sum(lambda r: pick(two, z_index(r), 1), NZ, send_z)
    return jnp.concatenate([last_sum(one), last_sum(two)], axis=1)


def fill_bias(where, bias):
    size = bias.shape[0]
    rank, end_one, end_two = where[0], where[1], where[2]

    def place_of(index):
        block = lax.div(index, LANES)
        block = 2 * lax.rem(block, 2) + lax.div(block, 2)
        return jnp.bitwise_xor(block, rank) * LANES + lax.rem(index, LANES)

    queries = place_of(lax.broadcasted_iota(jnp.int32, (size, 1), 0))
    keys = place_of(lax.broadcasted_iota(jnp.int32, (1, size), 1))
    start = jnp.where(queries >= end_two, end_two, jnp.where(queries >= end_one, end_one, 0))
    visible = (keys <= queries) & (keys >= start)
    bias[...] = jnp.where(visible, 0.0, -1e30).astype(f32)


def exponents(q_ref, k_ref, bias):
    scores = contract_last(q_ref[...], k_ref[...]) * (HEAD_SIZE**-0.5) + bias[...]
    exponent = jnp.exp(scores - jnp.max(scores, axis=-1, keepdims=True))
    return exponent / jnp.sum(exponent, axis=-1, keepdims=True)


def attend_kernel(where, q_ref, k_ref, v_ref, out_ref, bias):
    @pl.when(pl.program_id(0) == 0)
    def _():
        fill_bias(where, bias)

    probability = exponents(q_ref, k_ref, bias).astype(bf16)
    out_ref[...] = matmul(probability, v_ref[...]).astype(bf16)


def attend(where, qkv, heads):
    rows = qkv.shape[0]
    block = (rows, HEAD_SIZE)
    return pl.pallas_call(
        attend_kernel,
        out_shape=jax.ShapeDtypeStruct((rows, heads * HEAD_SIZE), bf16),
        grid_spec=pltpu.PrefetchScalarGridSpec(
            num_scalar_prefetch=1,
            grid=(heads,),
            in_specs=[
                pl.BlockSpec(block, lambda h, w: (0, h)),
                pl.BlockSpec(block, lambda h, w: (0, heads)),
                pl.BlockSpec(block, lambda h, w: (0, heads + 1)),
            ],
            out_specs=pl.BlockSpec(block, lambda h, w: (0, h)),
            scratch_shapes=[pltpu.VMEM((rows, rows), f32)],
        ),
        compiler_params=pltpu.CompilerParams(vmem_limit_bytes=40 * 1024 * 1024),
        cost_estimate=pl.CostEstimate(
            flops=4 * heads * rows * rows * HEAD_SIZE,
            bytes_accessed=4 * rows * heads * HEAD_SIZE,
            transcendentals=heads * rows * rows,
        ),
        name="attend",
    )(where, qkv, qkv, qkv)


def attend_back_kernel(heads, where, q_ref, k_ref, v_ref, g_ref, out_ref, bias, key_sum, value_sum):
    head = pl.program_id(0)

    @pl.when(head == 0)
    def _():
        fill_bias(where, bias)
        key_sum[...] = jnp.zeros_like(key_sum)
        value_sum[...] = jnp.zeros_like(value_sum)

    scale = HEAD_SIZE**-0.5
    probability = exponents(q_ref, k_ref, bias)
    grad_prob = contract_last(g_ref[...], v_ref[...])
    inner = jnp.sum(probability * grad_prob, axis=-1, keepdims=True)
    grad_scores = (probability * (grad_prob - inner)).astype(bf16)
    columns = pl.ds(pl.multiple_of(head * HEAD_SIZE, HEAD_SIZE), HEAD_SIZE)
    out_ref[:, columns] = (matmul(grad_scores, k_ref[...]) * scale).astype(bf16)
    key_sum[...] += contract_first(grad_scores, q_ref[...])
    value_sum[...] += contract_first(probability.astype(bf16), g_ref[...])

    @pl.when(head == heads - 1)
    def _():
        wide = heads * HEAD_SIZE
        out_ref[:, wide : wide + HEAD_SIZE] = (key_sum[...] * scale).astype(bf16)
        out_ref[:, wide + HEAD_SIZE :] = value_sum[...].astype(bf16)


def attend_back(where, qkv, grads, heads):
    rows = qkv.shape[0]
    block = (rows, HEAD_SIZE)
    return pl.pallas_call(
        functools.partial(attend_back_kernel, heads),
        out_shape=jax.ShapeDtypeStruct(qkv.shape, bf16),
        grid_spec=pltpu.PrefetchScalarGridSpec(
            num_scalar_prefetch=1,
            grid=(heads,),
            in_specs=[
                pl.BlockSpec(block, lambda h, w: (0, h)),
                pl.BlockSpec(block, lambda h, w: (0, heads)),
                pl.BlockSpec(block, lambda h, w: (0, heads + 1)),
                pl.BlockSpec(block, lambda h, w: (0, h)),
            ],
            out_specs=pl.BlockSpec(qkv.shape, lambda h, w: (0, 0)),
            scratch_shapes=[
                pltpu.VMEM((rows, rows), f32),
                pltpu.VMEM(block, f32),
                pltpu.VMEM(block, f32),
            ],
        ),
        compiler_params=pltpu.CompilerParams(vmem_limit_bytes=40 * 1024 * 1024),
        cost_estimate=pl.CostEstimate(
            flops=10 * heads * rows * rows * HEAD_SIZE,
            bytes_accessed=6 * rows * heads * HEAD_SIZE,
            transcendentals=heads * rows * rows,
        ),
        name="attend_back",
    )(where, qkv, qkv, qkv, grads)


def expert_grads_kernel(core, rows_own, rows_far, grads_own, grads_far, d_gate, d_up, scaled, *outs):
    half = pl.program_id(0)

    def write(rows, grads):
        outs[0][...] = contract_first(d_gate[...], rows[...])
        outs[1][...] = contract_first(d_up[...], rows[...])
        outs[2][...] = contract_first(scaled[...], grads[...])

    pl.when(half == 0)(lambda: write(rows_own, grads_own))
    pl.when(half == 1)(lambda: write(rows_far, grads_far))


def expert_grads(core, rows_own, rows_far, grads_own, grads_far, d_gate, d_up, scaled):
    rows, wide = rows_own.shape
    hidden = d_gate.shape[1]
    full = pl.BlockSpec((rows, wide), lambda h, c: (0, 0))
    part = pl.BlockSpec((rows, hidden), lambda h, c: (0, 0))
    result = pl.BlockSpec((hidden, wide), lambda h, c: (0, jnp.bitwise_xor(h, c[0])))
    return pl.pallas_call(
        expert_grads_kernel,
        out_shape=[jax.ShapeDtypeStruct((hidden, 2 * wide), f32)] * 3,
        grid_spec=pltpu.PrefetchScalarGridSpec(
            num_scalar_prefetch=1,
            grid=(2,),
            in_specs=[full] * 4 + [part] * 3,
            out_specs=[result] * 3,
        ),
        compiler_params=pltpu.CompilerParams(vmem_limit_bytes=56 * 1024 * 1024),
        cost_estimate=pl.CostEstimate(
            flops=12 * rows * wide * hidden,
            bytes_accessed=24 * hidden * wide + 12 * rows * wide,
            transcendentals=0,
        ),
        name="expert_grads",
    )(core, rows_own, rows_far, grads_own, grads_far, d_gate, d_up, scaled)


def per_device(
    tokens,
    g_attn,
    query_matrix,
    key_matrix,
    value_matrix,
    w_out,
    g_ffn,
    w_router,
    shared_gate,
    shared_up,
    shared_down,
    expert_gate,
    expert_up,
    expert_down,
    lengths,
    routes,
    cotangent,
):
    tok_dev, dim = tokens.shape
    group_rows = tok_dev * TP
    near = group_rows // 2
    experts = w_router.shape[1]
    own_rows = w_router.shape[0]
    q_width, kv_width = query_matrix.shape[1], key_matrix.shape[1]
    qkv_width = q_width + 2 * kv_width
    heads = q_width // HEAD_SIZE
    local_experts, _, hidden_own = expert_gate.shape
    half_dim = dim // 2
    fsdp_at = lax.axis_index("fsdp")
    rank = lax.axis_index("tp")
    core = lax.rem(rank, 2)
    core_vec = core.astype(jnp.int32).reshape(1)
    spot = jnp.stack(
        [fsdp_at // (NX * NY), lax.rem(fsdp_at // NY, NX), lax.rem(fsdp_at, NY)]
    ).astype(jnp.int32)

    small_tile = jnp.concatenate(
        [
            w_router,
            g_attn[:, None],
            g_ffn[:, None],
            jnp.zeros((own_rows, LANES - experts - 2), bf16),
        ],
        axis=1,
    )
    qkv_own = jnp.concatenate([query_matrix, key_matrix, value_matrix], axis=1)
    w_qkv, w_tile = gather_fsdp(
        jnp.concatenate([qkv_own, small_tile], axis=1)[None],
        spot,
        ((0, 0, qkv_width), (0, qkv_width, LANES)),
    )
    token_rows = gather_tp(tokens)
    grad_rows = gather_tp(cotangent)
    (w_out_all,) = gather_fsdp(w_out[None], spot, ((0, 0, q_width),))
    wide = shared_gate.shape[1]
    w_sgate, w_sup, w_sdown = gather_fsdp(
        jnp.stack([shared_gate, shared_up, shared_down]),
        spot,
        ((0, 0, wide), (1, 0, wide), (2, 0, wide)),
    )
    lane = lax.broadcasted_iota(jnp.int32, (8, LANES), 1)
    gain_pick = (lane == experts + lax.broadcasted_iota(jnp.int32, (8, LANES), 0)).astype(bf16)
    gains = contract_last(gain_pick, w_tile)
    gain_one, gain_two = gains[0:1], gains[1:2]

    route_blocks = routes.reshape(TP, tok_dev, routes.shape[1])
    own_routes = jnp.concatenate(
        [pick(route_blocks, jnp.bitwise_xor(b, rank), 0) for b in BLOCK_ORDER], axis=0
    )
    places = jnp.concatenate(
        [jnp.bitwise_xor(b, rank) * tok_dev + jnp.arange(tok_dev) for b in BLOCK_ORDER]
    ).astype(jnp.int32)
    expert_lane = jnp.arange(LANES, dtype=jnp.int32)[None, :]
    hot = (own_routes[:, 0:1] == expert_lane) | (own_routes[:, 1:2] == expert_lane)
    before = (places[None, :] < places[:, None]).astype(bf16)
    earlier = matmul(before, hot.astype(bf16))
    slots = experts * CAP
    slot_ids = jnp.arange(slots, dtype=jnp.int32)
    spread = (slot_ids[None, :] // CAP == jnp.arange(LANES, dtype=jnp.int32)[:, None]).astype(bf16)
    slot_wanted = matmul(jnp.where(hot, earlier, -1.0).astype(bf16), spread)
    dispatch = (slot_wanted == (slot_ids % CAP).astype(f32)[None, :]).astype(bf16)

    def core_half(values):
        return lax.dynamic_slice_in_dim(values, core * half_dim, half_dim, 1)

    slot_grads = contract_first(dispatch, core_half(grad_rows)).astype(bf16)
    grads_own = swap_fsdp(slot_grads)
    grads_far = move_tp(grads_own, 1)

    hidden_all = local_experts * hidden_own

    def expert_halves(weights):
        both = jnp.swapaxes(weights, 1, 2).reshape(hidden_all, dim)
        return core_half(both), lax.dynamic_slice_in_dim(both, (1 - core) * half_dim, half_dim, 1)

    eg_own, eg_far = expert_halves(expert_gate)
    eu_own, eu_far = expert_halves(expert_up)
    ed_own, ed_far = expert_halves(expert_down)

    ends = jnp.cumsum(lengths[0])
    where = jnp.stack([rank.astype(jnp.int32), ends[0], ends[1]]).astype(jnp.int32)
    normed_one, _ = norm_rows(token_rows.astype(f32), gain_one)
    h_attn = normed_one.astype(bf16)
    qkv = matmul(h_attn, w_qkv).astype(bf16)
    attended = attend(where, qkv, heads)
    attn_own = scatter_tp(
        contract_last(attended[:near], w_out_all), contract_last(attended[near:], w_out_all)
    )
    own_tokens = tokens.astype(f32)
    middle = own_tokens + attn_own
    normed_two, factor_two = norm_rows(middle, gain_two)
    h_ffn = gather_tp(normed_two.astype(bf16))

    slot_rows = contract_first(dispatch, core_half(h_ffn)).astype(bf16)
    rows_own = swap_fsdp(slot_rows)
    rows_far = move_tp(rows_own, 1)

    logits = matmul(h_ffn, w_tile)
    top = jnp.max(jnp.where(hot, logits, -1e30), axis=-1, keepdims=True)
    gate_exp = jnp.where(hot, jnp.exp(jnp.minimum(logits - top, 0.0)), 0.0)
    gates = gate_exp / jnp.sum(gate_exp, axis=-1, keepdims=True)
    gate_high = gates.astype(bf16)
    gate_low = (gates - gate_high.astype(f32)).astype(bf16)
    gate_lanes = jnp.concatenate([gate_high[:, :experts], gate_low[:, :experts]], axis=1)
    gated = (matmul(gate_high, spread) * dispatch.astype(f32)).astype(bf16)
    slot_gates = swap_fsdp(contract_first(dispatch, gate_lanes).astype(bf16))

    s_gate_pre = matmul(h_ffn, w_sgate)
    s_up_pre = matmul(h_ffn, w_sup)
    s_hidden = (jax.nn.silu(s_gate_pre) * s_up_pre).astype(bf16)
    grad_shidden = matmul(grad_rows, w_sdown)
    grad_sgate_pre = (grad_shidden * s_up_pre * silu_slope(s_gate_pre)).astype(bf16)
    grad_sup_pre = (grad_shidden * jax.nn.silu(s_gate_pre)).astype(bf16)
    grad_sdown = contract_first(grad_rows, s_hidden).astype(bf16)
    grad_sgate = contract_first(h_ffn, grad_sgate_pre).astype(bf16)
    grad_sup = contract_first(h_ffn, grad_sup_pre).astype(bf16)
    shared_sums = scatter_fsdp(
        lambda parts: jnp.concatenate(parts, axis=0), [grad_sgate, grad_sup, grad_sdown], spot
    )
    shared_out = contract_last(s_hidden, w_sdown)
    shared_back = contract_last(grad_sgate_pre, w_sgate) + contract_last(grad_sup_pre, w_sup)

    row_ids = lax.broadcasted_iota(jnp.int32, (slots, 1), 0)
    second = (row_ids % (local_experts * CAP)) // CAP
    mine = second == (lax.broadcasted_iota(jnp.int32, (1, hidden_all), 1) // hidden_own)

    gate_pre = contract_last(rows_own, eg_own) + contract_last(rows_far, eg_far)
    up_pre = contract_last(rows_own, eu_own) + contract_last(rows_far, eu_far)
    down_back = contract_last(grads_own, ed_own) + contract_last(grads_far, ed_far)
    silu_gate = jax.nn.silu(gate_pre)
    hidden_wide = jnp.where(mine, silu_gate * up_pre, 0.0)
    hidden = hidden_wide.astype(bf16)
    d_gate = jnp.where(mine, down_back * up_pre * silu_slope(gate_pre), 0.0).astype(bf16)
    d_up = jnp.where(mine, down_back * silu_gate, 0.0).astype(bf16)
    slot_dot = jnp.sum(hidden_wide * down_back, axis=1, keepdims=True)
    lane_ids = lax.broadcasted_iota(jnp.int32, (1, LANES), 1)
    expert_of = local_experts * fsdp_at.astype(jnp.int32) + second
    dot_high = slot_dot.astype(bf16)
    dot_low = (slot_dot - dot_high.astype(f32)).astype(bf16)
    zero = jnp.zeros((), bf16)
    dot_lanes = jnp.where(lane_ids == expert_of, dot_high, zero) + jnp.where(
        lane_ids == experts + expert_of, dot_low, zero
    )

    def back_product(gate_w, up_w):
        return matmul(d_gate, gate_w) + matmul(d_up, up_w)

    sent_far = move_tp(back_product(eg_far, eu_far).astype(bf16), 1)
    sent_own = (back_product(eg_own, eu_own) + sent_far.astype(f32)).astype(bf16)
    returned = swap_fsdp(jnp.concatenate([sent_own, dot_lanes], axis=1))

    out_far = move_tp(matmul(hidden, ed_far).astype(bf16), 1)
    out_own = (matmul(hidden, ed_own) + out_far.astype(f32)).astype(bf16)
    out_back = swap_fsdp(out_own)

    is_gate = (lane_ids == expert_of) | (lane_ids == experts + expert_of)
    gate_of = jnp.sum(jnp.where(is_gate, slot_gates.astype(f32), 0.0), axis=1, keepdims=True)
    grad_egate, grad_eup, grad_edown = expert_grads(
        core_vec,
        rows_own,
        rows_far,
        grads_own,
        grads_far,
        (gate_of * d_gate.astype(f32)).astype(bf16),
        (gate_of * d_up.astype(f32)).astype(bf16),
        (gate_of * hidden.astype(f32)).astype(bf16),
    )

    def expert_layout(grads):
        return jnp.swapaxes(grads.reshape(local_experts, hidden_own, dim), 1, 2)

    def whole_width(values):
        return jnp.concatenate(
            [jnp.where(core == 0, values, 0.0), jnp.where(core == 1, values, 0.0)], axis=1
        )

    routed = matmul(gated, out_back)
    out_part = shared_out + whole_width(routed)
    output = (middle + scatter_tp(out_part[:near], out_part[near:])).astype(bf16)

    combined = matmul(gated, returned)
    dots = combined[:, half_dim : half_dim + experts] + combined[:, half_dim + experts :]
    d_logits = dots - gates[:, :experts] * jnp.sum(dots, axis=-1, keepdims=True)
    d_logits = jnp.pad(d_logits.astype(bf16), ((0, 0), (0, LANES - experts)))
    ffn_part = (
        shared_back + whole_width(combined[:, :half_dim]) + contract_last(d_logits, w_tile)
    )
    d_h_ffn = scatter_tp(ffn_part[:near], ffn_part[near:])
    d_middle = cotangent.astype(f32) + norm_back(middle, factor_two, gain_two, d_h_ffn)
    gain_terms = (d_h_ffn * middle * factor_two).astype(bf16)
    gain_lane = jnp.broadcast_to(lane_ids == experts, (tok_dev, LANES)).astype(bf16)
    grad_tile = (contract_first(h_ffn, d_logits) + contract_first(gain_terms, gain_lane)).astype(
        bf16
    )
    d_att = gather_tp(d_middle.astype(bf16))
    grad_wout = contract_first(d_att, attended).astype(bf16)
    out_sums = scatter_fsdp(
        lambda parts: jnp.concatenate(parts, axis=-1), [grad_wout, grad_tile], spot
    )[0]
    tile_sums = small_sum_tp(out_sums[:, q_width:])

    d_attended = matmul(d_att, w_out_all).astype(bf16)
    d_qkv = attend_back(where, qkv, d_attended, heads)
    grad_wqkv = contract_first(h_attn, d_qkv).astype(bf16)
    qkv_sums = scatter_fsdp(lambda parts: parts[0], [grad_wqkv], spot)[0]
    d_h_attn = scatter_tp(
        contract_last(d_qkv[:near], w_qkv), contract_last(d_qkv[near:], w_qkv)
    )
    _, factor_one = norm_rows(own_tokens, gain_one)
    grad_tokens = (d_middle + norm_back(own_tokens, factor_one, gain_one, d_h_attn)).astype(bf16)
    gain_sum = jnp.sum(qkv_sums * qkv_own.astype(f32), axis=1)
    grad_g_attn = small_sum_tp(gain_sum) / g_attn.astype(f32)
    return (
        output,
        grad_tokens,
        grad_g_attn,
        qkv_sums[:, :q_width],
        qkv_sums[:, q_width : q_width + kv_width],
        qkv_sums[:, q_width + kv_width :],
        out_sums[:, :q_width],
        tile_sums[:, experts],
        tile_sums[:, :experts],
        shared_sums[0],
        shared_sums[1],
        shared_sums[2],
        expert_layout(grad_egate),
        expert_layout(grad_eup),
        expert_layout(grad_edown),
    )


def solution(mesh):
    in_specs = (
        P(("fsdp", "tp"), None),
        P("fsdp"),
        P("fsdp", "tp"),
        P("fsdp", "tp"),
        P("fsdp", "tp"),
        P("fsdp", "tp"),
        P("fsdp"),
        P("fsdp", None),
        P("fsdp", "tp"),
        P("fsdp", "tp"),
        P("fsdp", "tp"),
        P("fsdp", None, "tp"),
        P("fsdp", None, "tp"),
        P("fsdp", None, "tp"),
        P("fsdp", None),
        P("fsdp", None),
        P(("fsdp", "tp"), None),
    )
    out_specs = (
        P(("fsdp", "tp"), None),
        P(("fsdp", "tp"), None),
        P("fsdp"),
        P("fsdp", "tp"),
        P("fsdp", "tp"),
        P("fsdp", "tp"),
        P("fsdp", "tp"),
        P("fsdp"),
        P("fsdp", None),
        P("fsdp", "tp"),
        P("fsdp", "tp"),
        P("fsdp", "tp"),
        P("fsdp", None, "tp"),
        P("fsdp", None, "tp"),
        P("fsdp", None, "tp"),
    )
    return jax.shard_map(
        per_device, mesh=mesh, in_specs=in_specs, out_specs=out_specs, check_vma=False
    )
```

time: 2720 us -> 836 us (0.31)
  waiting for transfers between devices: 1640 us -> 288 us
  blocking collectives: 484 us -> 0 us
  starting transfers between devices: 46.1 us -> 209 us
  local copies, waits for them, and re-layouts: 204 us -> 88.7 us
  other arithmetic: 121 us -> 65.5 us
  matrix products: 180 us -> 132 us
  Pallas kernels: 0 us -> 39.5 us
    reduce_scatter x8 -> x0, waiting for transfers between devices: 1250 us -> none  [the longest x1 225 us: per_device(): lax.psum_scatter(grad_sup.astype(jnp.bfloat16), 'fsdp', scatter_dimension...]
    all_gather x3 -> x0, blocking collectives: 307 us -> none  [the longest x1 146 us: per_device(): lax.all_gather(w_router, 'fsdp', axis=0, tiled=True)]
    ppermute x0 -> x107, waiting for transfers between devices: none -> 239 us  [the longest x81 213 us: move_fsdp(): return lax.ppermute(values, 'fsdp', pairs)]
    psum x3 -> x0, waiting for transfers between devices: 186 us -> none  [the longest x1 106 us: per_device(): attn_sum = lax.psum(attn_part, 'tp')]
    unnamed x2 -> x0, blocking collectives: 171 us -> none
    ppermute x0 -> x107, starting transfers between devices: none -> 171 us  [the longest x81 121 us: move_fsdp(): return lax.ppermute(values, 'fsdp', pairs)]
    reshape x8 -> x1, local copies, waits for them, and re-layouts: 75.6 us -> 0.7 us  [per_device(): route_blocks = routes.reshape(TP, tok_dev, routes.shape[1])]
    gather x6 -> x0, local copies, waits for them, and re-layouts: 72.6 us -> none  [the longest x2 25.4 us: per_device(): grad_full[slot_source]]
  transfers between devices with their start and end apart: 23 -> 112, of which waited for: 13 -> 42; matrix products, arithmetic and copies ran while one was open for 15% -> 30% of each run, Pallas kernels for 0% -> 4%
where the time goes in v1:
time: 836 us; the launch traced here: 826 us
  waiting for transfers between devices  288 us (34%)
  starting transfers between devices  209 us (25%)
  matrix products  132 us (16%)
  local copies, waits for them, and re-layouts  88.7 us (11%)
  other arithmetic  65.5 us (8%)
  Pallas kernels  39.5 us (5%)
    ppermute x81, waiting for transfers between devices, move_fsdp(): return lax.ppermute(values, 'fsdp', pairs)  213 us
    ppermute x81, starting transfers between devices, move_fsdp(): return lax.ppermute(values, 'fsdp', pairs)  121 us
    dot_general x15, matrix products, contract_last(): lax.dot_general(left_op, right_op, (((1,), (1,)), ((), ())), preferred_el...  58.7 us
    ppermute x26, starting transfers between devices, move_tp(): return lax.ppermute(values, 'tp', [(i, i ^ flip) for i in range(TP)])  50.1 us
    all_to_all x5, waiting for transfers between devices, swap_fsdp(): lax.all_to_all(blocks, 'fsdp', split_axis=0, concat_axis=0, tiled=True)  49.1 us
    dot_general x16, matrix products, matmul(): return jnp.dot(left_op, right_op, preferred_element_type=f32)  48 us
    all_to_all x5, starting transfers between devices, swap_fsdp(): lax.all_to_all(blocks, 'fsdp', split_axis=0, concat_axis=0, tiled=True)  38.1 us
    unnamed x242, local copies, waits for them, and re-layouts  29.6 us
  transfers between devices with their start and end apart: 112, of which 42 were waited for; matrix products, arithmetic and copies ran while one was open for 30% of the time, Pallas kernels for 4%

profile of v1, /device:TPU:1, one launch (start us, length us, event | category | flops | bytes accessed | tf_op | source)
XLA Modules:
  0.0 825.7 jit_solution(2764258073551763815)
XLA Ops:
  57.9 16.9 %collective-permute-start.1 = (bf16[256,2048]{1,0:T(8,128)(2,1)}, bf16[256,2048]{1,0:T(8,128)(2,1)}, u32[]{:S(2)}, u32[]{:S(2)}) collective-permute-start(bf16[256,2048]{1,0:T(8,128)(2,1)} %pad_maximum_fusion.12), channel_id=1, source_target_pairs={{0,1},{1,0},{2,3},{3,2},{4,5},{5,4},{6,7},{7,6},{8,9},{9,8},{10,11... | collective-permute-start | bytes 3145736 | tf_op jit(solution)/shard_map/ppermute | solution.py:67
  120.7 6.4 collective-permute-done.34
  135.2 8.1 all-to-all-start.2
  151.8 43.2 %collective-permute-done.40 = bf16[2,3,32,704]{3,2,1,0:T(8,128)(2,1)S(1)} collective-permute-done((bf16[2,3,32,704]{3,2,1,0:T(8,128)(2,1)}, bf16[2,3,32,704]{3,2,1,0:T(8,128)(2,1)S(1)}, u32[]{:S(2)}, u32[]{:S(2)}) %collective-permute-start.40) | collective-permute-done | bytes 270368 | tf_op jit(solution)/shard_map/ppermute | solution.py:63
  195.0 22.2 %collective-permute-start.38 = (bf16[4,2,3,32,704]{4,3,2,1,0:T(8,128)(2,1)}, bf16[4,2,3,32,704]{4,3,2,1,0:T(8,128)(2,1)}, u32[]{:S(2)}, u32[]{:S(2)}) collective-permute-start(bf16[4,2,3,32,704]{4,3,2,1,0:T(8,128)(2,1)} %pad_maximum_fusion.4.refs_0_), channel_id=1, source_target_pairs={{0,32},{4,36},{8,40},{12,44},{16,48},{20,52},{24,56},{28,60},{32,6... | collective-permute-start | bytes 3244040 | tf_op jit(solution)/shard_map/ppermute | solution.py:63
  238.9 14.7 %collective-permute-done.42.refs_5_ = bf16[4,2,3,32,704]{4,3,2,1,0:T(8,128)(2,1)} collective-permute-done((bf16[4,2,3,32,704]{4,3,2,1,0:T(8,128)(2,1)}, bf16[4,2,3,32,704]{4,3,2,1,0:T(8,128)(2,1)}, u32[]{:S(2)}, u32[]{:S(2)}) %collective-permute-start.42) | collective-permute-done | bytes 1081376 | tf_op jit(solution)/shard_map/ppermute | solution.py:63
  256.5 27.3 %collective-permute-done.44.refs_7_ = bf16[4,2,3,32,704]{4,3,2,1,0:T(8,128)(2,1)} collective-permute-done((bf16[4,2,3,32,704]{4,3,2,1,0:T(8,128)(2,1)}, bf16[4,2,3,32,704]{4,3,2,1,0:T(8,128)(2,1)}, u32[]{:S(2)}, u32[]{:S(2)}) %collective-permute-start.44) | collective-permute-done | bytes 1081376 | tf_op jit(solution)/shard_map/ppermute | solution.py:63
  293.8 6.4 fusion.13
  308.5 5.9 all-to-all-start
  381.5 8.9 %all-to-all-start.4 = ((bf16[32,40,128]{2,1,0:T(8,128)(2,1)}), bf16[32,40,128]{2,1,0:T(8,128)(2,1)}, u32[]{:S(2)}, u32[]{:S(2)}) async-start(bf16[32,40,128]{2,1,0:T(8,128)(2,1)} %bitcast.592), calls=%async_computation.4 | async-start | bytes 655360 | tf_op jit(solution)/shard_map/all_to_all | solution.py:88
  399.5 25.7 %all-to-all-done.4 = bf16[32,40,128]{2,1,0:T(8,128)(2,1)} async-done(((bf16[32,40,128]{2,1,0:T(8,128)(2,1)}), bf16[32,40,128]{2,1,0:T(8,128)(2,1)}, u32[]{:S(2)}, u32[]{:S(2)}) %all-to-all-start.4) | async-done | bytes 327712 | tf_op jit(solution)/shard_map/all_to_all | solution.py:88
  427.4 5.8 convolution_add_fusion
  437.3 5.9 fusion.29
  443.2 6.0 convolution_add_fusion.1
  449.2 10.0 %multiply_convert_fusion.1 = (bf16[1280,704]{1,0:T(8,128)(2,1)}, bf16[1280,704]{1,0:T(8,128)(2,1)}, bf16[1280,704]{1,0:T(8,128)(2,1)}, bf16[1280,704]{1,0:T(8,12...) fusion(f32[1280]{0:T(1024)S(1)} %mul.307, f32[1280,704]{1,0:T(8,128)S(1)} %convolution_add_fusion, ...), kind=kOutput, calls=%fused_computation.17 | convolution fusion | flops 1871626240 | bytes 27840516 | tf_op jit(solution)/shard_map/dot_general | solution.py:30
  471.4 5.6 add_convert_fusion.1
  486.1 6.4 all-to-all-start.1
  506.4 5.4 copy.188
  511.8 23.4 %all-to-all-done.1 = bf16[32,40,1024]{2,1,0:T(8,128)(2,1)} async-done(((bf16[32,40,1024]{2,1,0:T(8,128)(2,1)}), bf16[32,40,1024]{2,1,0:T(8,128)(2,1)}, u32[]{:S(2)}, u32[]{:S(2)}) %all-to-all-start.1) | async-done | bytes 2621472 | tf_op jit(solution)/shard_map/all_to_all | solution.py:88
  535.2 8.9 %all-to-all-start.3 = ((bf16[32,40,1152]{2,1,0:T(8,128)(2,1)}), bf16[32,40,1152]{2,1,0:T(8,128)(2,1)}, u32[]{:S(2)}, u32[]{:S(2)}) async-start(bf16[32,40,1152]{2,1,0:T(8,128)(2,1)} %bitcast.563), calls=%async_computation.3 | async-start | bytes 5898240 | tf_op jit(solution)/shard_map/all_to_all | solution.py:88
  550.7 9.2 %collective-permute-done.94 = bf16[3,2,4,32,704]{4,3,2,1,0:T(8,128)(2,1)} collective-permute-done((bf16[3,2,4,32,704]{4,3,2,1,0:T(8,128)(2,1)}, bf16[3,2,4,32,704]{4,3,2,1,0:T(8,128)(2,1)}, u32[]{:S(2)}, u32[]{:S(2)}) %collective-permute-start.94) | collective-permute-done | bytes 1081376 | tf_op jit(solution)/shard_map/ppermute | solution.py:63
  559.9 42.5 %collective-permute-done.93 = bf16[3,2,4,32,704]{4,3,2,1,0:T(8,128)(2,1)} collective-permute-done((bf16[3,2,4,32,704]{4,3,2,1,0:T(8,128)(2,1)}, bf16[3,2,4,32,704]{4,3,2,1,0:T(8,128)(2,1)}, u32[]{:S(2)}, u32[]{:S(2)}) %collective-permute-start.93) | collective-permute-done | bytes 1081376 | tf_op jit(solution)/shard_map/ppermute | solution.py:63
  612.8 6.1 collective-permute-done.103
  659.5 20.9 %expert_grads.1 = (f32[704,2048]{1,0:T(8,128)}, f32[704,2048]{1,0:T(8,128)}, f32[704,2048]{1,0:T(8,128)}) custom-call(s32[1]{0:T(128)} %bitcast.233.core, bf16[1280,1024]{1,0:T(8,128)(2,1)} %bitcast.74.rows_own, bf16[1280,1024]{1,0:T(8,128)(2,1)} %collective-permute-done.45.rows_far, bf16[1280,1024]{1,0:T(8,128)(2,1)} %bitcast.87.grads_own, ...), custom_call_target="tpu_custom_call" | custom-call | flops 11072962560 | bytes 33030144 | tf_op jit(solution)/shard_map/expert_grads/pallas_call | solution.py:306
  687.7 10.1 %collective-permute-done.55 = bf16[128,2048]{1,0:T(8,128)(2,1)S(1)} collective-permute-done((bf16[128,2048]{1,0:T(8,128)(2,1)S(1)}, bf16[128,2048]{1,0:T(8,128)(2,1)S(1)}, u32[]{:S(2)}, u32[]{:S(2)}) %collective-permute-start.55) | collective-permute-done | bytes 524320 | tf_op jit(solution)/shard_map/ppermute | solution.py:67
  703.3 6.0 attend_back.1
  720.8 6.0 collective-permute-done.85
  728.5 7.7 collective-permute-start.68
  738.7 13.0 %collective-permute-done.68 = bf16[1,4,2,32,768]{4,3,2,1,0:T(8,128)(2,1)S(1)} collective-permute-done((bf16[1,4,2,32,768]{4,3,2,1,0:T(8,128)(2,1)S(1)}, bf16[1,4,2,32,768]{4,3,2,1,0:T(8,128)(2,1)S(1)}, u32[]{:S(2)}, u32[]{:S(2)}) %collective-permute-start.68) | collective-permute-done | bytes 393248 | tf_op jit(solution)/shard_map/ppermute | solution.py:63
  775.3 8.8 %collective-permute-start.92 = (f32[64,128]{1,0:T(8,128)S(1)}, f32[64,128]{1,0:T(8,128)S(1)}, u32[]{:S(2)}, u32[]{:S(2)}) collective-permute-start(f32[64,128]{1,0:T(8,128)S(1)} %slice.440), channel_id=1, source_target_pairs={{0,3},{1,2},{2,1},{3,0},{4,7},{5,6},{6,5},{7,4},{8,11},{9,10},{10,... | collective-permute-start | bytes 98312 | tf_op jit(solution)/shard_map/ppermute | solution.py:67
  800.7 5.7 collective-permute-start.75
  811.0 10.4 %collective-permute-done.58 = bf16[128,2048]{1,0:T(8,128)(2,1)S(1)} collective-permute-done((bf16[128,2048]{1,0:T(8,128)(2,1)S(1)}, bf16[128,2048]{1,0:T(8,128)(2,1)S(1)}, u32[]{:S(2)}, u32[]{:S(2)}) %collective-permute-start.58) | collective-permute-done | bytes 524320 | tf_op jit(solution)/shard_map/ppermute | solution.py:67
  (691 shorter events, 412.8 us)
Async XLA Ops:
  49.5 34.7 %collective-permute-start.8 = (bf16[4,2,1,32,896]{4,3,1,2,0:T(8,128)(2,1)}, bf16[4,2,1,32,896]{4,3,1,2,0:T(8,128)(2,1)}, u32[]{:S(2)}, u32[]{:S(2)}) collective-permute-start(bf16[4,2,1,32,896]{4,3,1,2,0:T(8,128)(2,1)} %get-tuple-element.122), channel_id=1, source_target_pairs={{0,32},{4,36},{8,40},{12,44},{16,48},{20,52},{24,56},{28,60},{32,6... | collective-permute-start | bytes 1376264 | tf_op jit(solution)/shard_map/ppermute | solution.py:63
  53.1 32.1 %collective-permute-start.12 = (bf16[4,2,1,32,896]{4,3,2,1,0:T(8,128)(2,1)S(1)}, bf16[4,2,1,32,896]{4,3,2,1,0:T(8,128)(2,1)}, u32[]{:S(2)}, u32[]{:S(2)}) collective-permute-start(bf16[4,2,1,32,896]{4,3,2,1,0:T(8,128)(2,1)S(1)} %pad_maximum_fusion.19.refs_4_), channel_id=1, source_target_pairs={{0,12},{4,0},{8,4},{12,8},{16,28},{20,16},{24,20},{28,24},{32,44},... | collective-permute-start | bytes 1376264 | tf_op jit(solution)/shard_map/ppermute | solution.py:63
  53.1 34.8 %collective-permute-start.13 = (bf16[4,2,1,32,896]{4,3,2,1,0:T(8,128)(2,1)S(1)}, bf16[4,2,1,32,896]{4,3,2,1,0:T(8,128)(2,1)}, u32[]{:S(2)}, u32[]{:S(2)}) collective-permute-start(bf16[4,2,1,32,896]{4,3,2,1,0:T(8,128)(2,1)S(1)} %pad_maximum_fusion.19.refs_4_), channel_id=1, source_target_pairs={{0,8},{4,12},{8,0},{12,4},{16,24},{20,28},{24,16},{28,20},{32,40},... | collective-permute-start | bytes 1376264 | tf_op jit(solution)/shard_map/ppermute | solution.py:63
  54.1 33.8 %collective-permute-start.14 = (bf16[4,2,1,32,896]{4,3,2,1,0:T(8,128)(2,1)S(1)}, bf16[4,2,1,32,896]{4,3,2,1,0:T(8,128)(2,1)}, u32[]{:S(2)}, u32[]{:S(2)}) collective-permute-start(bf16[4,2,1,32,896]{4,3,2,1,0:T(8,128)(2,1)S(1)} %pad_maximum_fusion.19.refs_4_), channel_id=1, source_target_pairs={{0,4},{4,8},{8,12},{12,0},{16,20},{20,24},{24,28},{28,16},{32,36},... | collective-permute-start | bytes 1376264 | tf_op jit(solution)/shard_map/ppermute | solution.py:63
  57.9 33.3 %collective-permute-start.1 = (bf16[256,2048]{1,0:T(8,128)(2,1)}, bf16[256,2048]{1,0:T(8,128)(2,1)}, u32[]{:S(2)}, u32[]{:S(2)}) collective-permute-start(bf16[256,2048]{1,0:T(8,128)(2,1)} %pad_maximum_fusion.12), channel_id=1, source_target_pairs={{0,1},{1,0},{2,3},{3,2},{4,5},{5,4},{6,7},{7,6},{8,9},{9,8},{10,11... | collective-permute-start | bytes 3145736 | tf_op jit(solution)/shard_map/ppermute | solution.py:67
  116.0 34.4 %collective-permute-start.41 = (bf16[2,3,32,704]{3,2,1,0:T(8,128)(2,1)}, bf16[2,3,32,704]{3,2,1,0:T(8,128)(2,1)}, u32[]{:S(2)}, u32[]{:S(2)}) collective-permute-start(bf16[2,3,32,704]{3,2,1,0:T(8,128)(2,1)} %get-tuple-element.112), channel_id=1, source_target_pairs={{0,32},{4,36},{8,40},{12,44},{16,48},{20,52},{24,56},{28,60},{32,6... | collective-permute-start | bytes 811016 | tf_op jit(solution)/shard_map/ppermute | solution.py:63
  128.7 100.1 %collective-permute-start.36 = (bf16[4,2,3,32,704]{4,3,2,1,0:T(8,128)(2,1)}, bf16[4,2,3,32,704]{4,3,2,1,0:T(8,128)(2,1)}, u32[]{:S(2)}, u32[]{:S(2)}) collective-permute-start(bf16[4,2,3,32,704]{4,3,2,1,0:T(8,128)(2,1)} %pad_maximum_fusion.4.refs_0_), channel_id=1, source_target_pairs={{0,96},{4,100},{8,104},{12,108},{16,112},{20,116},{24,120},{28,124... | collective-permute-start | bytes 3244040 | tf_op jit(solution)/shard_map/ppermute | solution.py:63
  131.9 100.6 %collective-permute-start.37 = (bf16[4,2,3,32,704]{4,3,2,1,0:T(8,128)(2,1)}, bf16[4,2,3,32,704]{4,3,2,1,0:T(8,128)(2,1)}, u32[]{:S(2)}, u32[]{:S(2)}) collective-permute-start(bf16[4,2,3,32,704]{4,3,2,1,0:T(8,128)(2,1)} %pad_maximum_fusion.4.refs_0_), channel_id=1, source_target_pairs={{0,64},{4,68},{8,72},{12,76},{16,80},{20,84},{24,88},{28,92},{32,9... | collective-permute-start | bytes 3244040 | tf_op jit(solution)/shard_map/ppermute | solution.py:63
  135.2 158.1 %all-to-all-start.2 = ((bf16[32,40,1024]{2,1,0:T(8,128)(2,1)}), bf16[32,40,1024]{2,1,0:T(8,128)(2,1)}, u32[]{:S(2)}, u32[]{:S(2)}) async-start(bf16[32,40,1024]{2,1,0:T(8,128)(2,1)} %bitcast.568), calls=%async_computation.2 | async-start | bytes 5242880 | tf_op jit(solution)/shard_map/all_to_all | solution.py:88
  147.2 82.2 %collective-permute-start.30 = (bf16[128,2048]{1,0:T(8,128)(2,1)S(1)}, bf16[128,2048]{1,0:T(8,128)(2,1)S(1)}, u32[]{:S(2)}, u32[]{:S(2)}) collective-permute-start(bf16[128,2048]{1,0:T(8,128)(2,1)S(1)} %multiply_convert_fusion.7), channel_id=1, source_target_pairs={{0,2},{1,3},{2,0},{3,1},{4,6},{5,7},{6,4},{7,5},{8,10},{9,11},{10,... | collective-permute-start | bytes 1572872 | tf_op jit(solution)/shard_map/ppermute | solution.py:67
  147.7 47.2 %collective-permute-start.40 = (bf16[2,3,32,704]{3,2,1,0:T(8,128)(2,1)}, bf16[2,3,32,704]{3,2,1,0:T(8,128)(2,1)S(1)}, u32[]{:S(2)}, u32[]{:S(2)}) collective-permute-start(bf16[2,3,32,704]{3,2,1,0:T(8,128)(2,1)} %get-tuple-element.112), channel_id=1, source_target_pairs={{0,64},{4,68},{8,72},{12,76},{16,80},{20,84},{24,88},{28,92},{32,9... | collective-permute-start | bytes 811016 | tf_op jit(solution)/shard_map/ppermute | solution.py:63
  150.4 71.6 %collective-permute-start.39 = (bf16[2,3,32,704]{3,2,1,0:T(8,128)(2,1)}, bf16[2,3,32,704]{3,2,1,0:T(8,128)(2,1)S(1)}, u32[]{:S(2)}, u32[]{:S(2)}) collective-permute-start(bf16[2,3,32,704]{3,2,1,0:T(8,128)(2,1)} %get-tuple-element.112), channel_id=1, source_target_pairs={{0,96},{4,100},{8,104},{12,108},{16,112},{20,116},{24,120},{28,124... | collective-permute-start | bytes 811016 | tf_op jit(solution)/shard_map/ppermute | solution.py:63
  195.0 44.0 %collective-permute-start.38 = (bf16[4,2,3,32,704]{4,3,2,1,0:T(8,128)(2,1)}, bf16[4,2,3,32,704]{4,3,2,1,0:T(8,128)(2,1)}, u32[]{:S(2)}, u32[]{:S(2)}) collective-permute-start(bf16[4,2,3,32,704]{4,3,2,1,0:T(8,128)(2,1)} %pad_maximum_fusion.4.refs_0_), channel_id=1, source_target_pairs={{0,32},{4,36},{8,40},{12,44},{16,48},{20,52},{24,56},{28,60},{32,6... | collective-permute-start | bytes 3244040 | tf_op jit(solution)/shard_map/ppermute | solution.py:63
  230.2 53.5 %collective-permute-start.44 = (bf16[4,2,3,32,704]{4,3,2,1,0:T(8,128)(2,1)}, bf16[4,2,3,32,704]{4,3,2,1,0:T(8,128)(2,1)}, u32[]{:S(2)}, u32[]{:S(2)}) collective-permute-start(bf16[4,2,3,32,704]{4,3,2,1,0:T(8,128)(2,1)} %pad_maximum_fusion.5.refs_4_), channel_id=1, source_target_pairs={{0,4},{4,8},{8,12},{12,0},{16,20},{20,24},{24,28},{28,16},{32,36},... | collective-permute-start | bytes 3244040 | tf_op jit(solution)/shard_map/ppermute | solution.py:63
  232.5 67.6 %collective-permute-start.31 = (bf16[256,2048]{1,0:T(8,128)(2,1)}, bf16[256,2048]{1,0:T(8,128)(2,1)}, u32[]{:S(2)}, u32[]{:S(2)}) collective-permute-start(bf16[256,2048]{1,0:T(8,128)(2,1)} %pad_maximum_fusion.13), channel_id=1, source_target_pairs={{0,1},{1,0},{2,3},{3,2},{4,5},{5,4},{6,7},{7,6},{8,9},{9,8},{10,11... | collective-permute-start | bytes 3145736 | tf_op jit(solution)/shard_map/ppermute | solution.py:67
  293.3 134.1 %collective-permute-start.51 = (bf16[1280,1024]{1,0:T(8,128)(2,1)}, bf16[1280,1024]{1,0:T(8,128)(2,1)}, u32[]{:S(2)}, u32[]{:S(2)}) collective-permute-start(bf16[1280,1024]{1,0:T(8,128)(2,1)} %bitcast.87.grads_own), channel_id=1, source_target_pairs={{0,1},{1,0},{2,3},{3,2},{4,5},{5,4},{6,7},{7,6},{8,9},{9,8},{10,11... | collective-permute-start | bytes 7864328 | tf_op jit(solution)/shard_map/ppermute | solution.py:67
  308.5 73.0 %all-to-all-start = ((bf16[32,40,1024]{2,1,0:T(8,128)(2,1)}), bf16[32,40,1024]{2,1,0:T(8,128)(2,1)}, u32[]{:S(2)}, u32[]{:S(2)}) async-start(bf16[32,40,1024]{2,1,0:T(8,128)(2,1)} %bitcast.569), calls=%async_computation | async-start | bytes 5242880 | tf_op jit(solution)/shard_map/all_to_all | solution.py:88
  361.1 143.1 %collective-permute-start.102 = (bf16[3,4,2,32,704]{4,3,0,2,1:T(8,128)(2,1)}, bf16[3,4,2,32,704]{4,3,0,2,1:T(8,128)(2,1)}, u32[]{:S(2)}, u32[]{:S(2)}) collective-permute-start(bf16[3,4,2,32,704]{4,3,0,2,1:T(8,128)(2,1)} %pad_maximum_fusion.11), channel_id=1, source_target_pairs={{0,12},{4,0},{8,4},{12,8},{16,28},{20,16},{24,20},{28,24},{32,44},... | collective-permute-start | bytes 3244040 | tf_op jit(solution)/shard_map/ppermute | solution.py:63
  365.0 179.2 %collective-permute-start.101 = (bf16[3,4,2,32,704]{4,3,0,2,1:T(8,128)(2,1)}, bf16[3,4,2,32,704]{4,3,0,2,1:T(8,128)(2,1)}, u32[]{:S(2)}, u32[]{:S(2)}) collective-permute-start(bf16[3,4,2,32,704]{4,3,0,2,1:T(8,128)(2,1)} %pad_maximum_fusion.10), channel_id=1, source_target_pairs={{0,8},{4,12},{8,0},{12,4},{16,24},{20,28},{24,16},{28,20},{32,40},... | collective-permute-start | bytes 3244040 | tf_op jit(solution)/shard_map/ppermute | solution.py:63
  367.1 177.1 %collective-permute-start.100 = (bf16[3,4,2,32,704]{4,3,0,2,1:T(8,128)(2,1)}, bf16[3,4,2,32,704]{4,3,0,2,1:T(8,128)(2,1)}, u32[]{:S(2)}, u32[]{:S(2)}) collective-permute-start(bf16[3,4,2,32,704]{4,3,0,2,1:T(8,128)(2,1)} %pad_maximum_fusion.9), channel_id=1, source_target_pairs={{0,4},{4,8},{8,12},{12,0},{16,20},{20,24},{24,28},{28,16},{32,36},... | collective-permute-start | bytes 3244040 | tf_op jit(solution)/shard_map/ppermute | solution.py:63
  381.5 43.8 %all-to-all-start.4 = ((bf16[32,40,128]{2,1,0:T(8,128)(2,1)}), bf16[32,40,128]{2,1,0:T(8,128)(2,1)}, u32[]{:S(2)}, u32[]{:S(2)}) async-start(bf16[32,40,128]{2,1,0:T(8,128)(2,1)} %bitcast.592), calls=%async_computation.4 | async-start | bytes 655360 | tf_op jit(solution)/shard_map/all_to_all | solution.py:88
  390.4 52.7 %collective-permute-start.45 = (bf16[1280,1024]{1,0:T(8,128)(2,1)}, bf16[1280,1024]{1,0:T(8,128)(2,1)}, u32[]{:S(2)}, u32[]{:S(2)}) collective-permute-start(bf16[1280,1024]{1,0:T(8,128)(2,1)} %bitcast.74.rows_own), channel_id=1, source_target_pairs={{0,1},{1,0},{2,3},{3,2},{4,5},{5,4},{6,7},{7,6},{8,9},{9,8},{10,11... | collective-permute-start | bytes 7864328 | tf_op jit(solution)/shard_map/ppermute | solution.py:67
  481.4 68.7 %collective-permute-start.95 = (bf16[3,2,4,32,704]{4,3,2,1,0:T(8,128)(2,1)}, bf16[3,2,4,32,704]{4,3,2,1,0:T(8,128)(2,1)}, u32[]{:S(2)}, u32[]{:S(2)}) collective-permute-start(bf16[3,2,4,32,704]{4,3,2,1,0:T(8,128)(2,1)} %pad_maximum_fusion.8), channel_id=1, source_target_pairs={{0,96},{4,100},{8,104},{12,108},{16,112},{20,116},{24,120},{28,124... | collective-permute-start | bytes 3244040 | tf_op jit(solution)/shard_map/ppermute | solution.py:63
  486.1 49.0 %all-to-all-start.1 = ((bf16[32,40,1024]{2,1,0:T(8,128)(2,1)}), bf16[32,40,1024]{2,1,0:T(8,128)(2,1)}, u32[]{:S(2)}, u32[]{:S(2)}) async-start(bf16[32,40,1024]{2,1,0:T(8,128)(2,1)} %bitcast.570), calls=%async_computation.1 | async-start | bytes 5242880 | tf_op jit(solution)/shard_map/all_to_all | solution.py:88
  496.8 63.1 %collective-permute-start.94 = (bf16[3,2,4,32,704]{4,3,2,1,0:T(8,128)(2,1)}, bf16[3,2,4,32,704]{4,3,2,1,0:T(8,128)(2,1)}, u32[]{:S(2)}, u32[]{:S(2)}) collective-permute-start(bf16[3,2,4,32,704]{4,3,2,1,0:T(8,128)(2,1)} %pad_maximum_fusion.7), channel_id=1, source_target_pairs={{0,64},{4,68},{8,72},{12,76},{16,80},{20,84},{24,88},{28,92},{32,9... | collective-permute-start | bytes 3244040 | tf_op jit(solution)/shard_map/ppermute | solution.py:63
  504.2 98.2 %collective-permute-start.93 = (bf16[3,2,4,32,704]{4,3,2,1,0:T(8,128)(2,1)}, bf16[3,2,4,32,704]{4,3,2,1,0:T(8,128)(2,1)}, u32[]{:S(2)}, u32[]{:S(2)}) collective-permute-start(bf16[3,2,4,32,704]{4,3,2,1,0:T(8,128)(2,1)} %pad_maximum_fusion.6), channel_id=1, source_target_pairs={{0,32},{4,36},{8,40},{12,44},{16,48},{20,52},{24,56},{28,60},{32,6... | collective-permute-start | bytes 3244040 | tf_op jit(solution)/shard_map/ppermute | solution.py:63
  535.2 103.1 %all-to-all-start.3 = ((bf16[32,40,1152]{2,1,0:T(8,128)(2,1)}), bf16[32,40,1152]{2,1,0:T(8,128)(2,1)}, u32[]{:S(2)}, u32[]{:S(2)}) async-start(bf16[32,40,1152]{2,1,0:T(8,128)(2,1)} %bitcast.563), calls=%async_computation.3 | async-start | bytes 5898240 | tf_op jit(solution)/shard_map/all_to_all | solution.py:88
  547.1 62.1 %collective-permute-start.105 = (bf16[3,2,32,704]{3,2,0,1:T(8,128)(2,1)S(1)}, bf16[3,2,32,704]{3,2,0,1:T(8,128)(2,1)S(1)}, u32[]{:S(2)}, u32[]{:S(2)}) collective-permute-start(bf16[3,2,32,704]{3,2,0,1:T(8,128)(2,1)S(1)} %get-tuple-element.103), channel_id=1, source_target_pairs={{0,96},{4,100},{8,104},{12,108},{16,112},{20,116},{24,120},{28,124... | collective-permute-start | bytes 811016 | tf_op jit(solution)/shard_map/ppermute | solution.py:63
  549.6 63.3 %collective-permute-start.104 = (bf16[3,2,32,704]{3,2,0,1:T(8,128)(2,1)S(1)}, bf16[3,2,32,704]{3,2,0,1:T(8,128)(2,1)S(1)}, u32[]{:S(2)}, u32[]{:S(2)}) collective-permute-start(bf16[3,2,32,704]{3,2,0,1:T(8,128)(2,1)S(1)} %get-tuple-element.104), channel_id=1, source_target_pairs={{0,64},{4,68},{8,72},{12,76},{16,80},{20,84},{24,88},{28,92},{32,9... | collective-permute-start | bytes 811016 | tf_op jit(solution)/shard_map/ppermute | solution.py:63
  550.1 68.8 %collective-permute-start.103 = (bf16[3,2,32,704]{3,2,0,1:T(8,128)(2,1)S(1)}, bf16[3,2,32,704]{3,2,0,1:T(8,128)(2,1)S(1)}, u32[]{:S(2)}, u32[]{:S(2)}) collective-permute-start(bf16[3,2,32,704]{3,2,0,1:T(8,128)(2,1)S(1)} %get-tuple-element.102), channel_id=1, source_target_pairs={{0,32},{4,36},{8,40},{12,44},{16,48},{20,52},{24,56},{28,60},{32,6... | collective-permute-start | bytes 811016 | tf_op jit(solution)/shard_map/ppermute | solution.py:63
  619.7 32.8 %collective-permute-start.106 = (bf16[3,32,704]{2,1,0:T(8,128)(2,1)}, bf16[3,32,704]{2,1,0:T(8,128)(2,1)}, u32[]{:S(2)}, u32[]{:S(2)}) collective-permute-start(bf16[3,32,704]{2,1,0:T(8,128)(2,1)} %dynamic-slice_bitcast_fusion.30), channel_id=1, source_target_pairs={{0,16},{4,20},{8,24},{12,28},{16,0},{20,4},{24,8},{28,12},{32,48},... | collective-permute-start | bytes 405512 | tf_op jit(solution)/shard_map/ppermute | solution.py:63
  751.7 55.2 %collective-permute-start.57 = (bf16[256,2048]{1,0:T(8,128)(2,1)S(1)}, bf16[256,2048]{1,0:T(8,128)(2,1)S(1)}, u32[]{:S(2)}, u32[]{:S(2)}) collective-permute-start(bf16[256,2048]{1,0:T(8,128)(2,1)S(1)} %convolution_convert_fusion.9), channel_id=1, source_target_pairs={{0,1},{1,0},{2,3},{3,2},{4,5},{5,4},{6,7},{7,6},{8,9},{9,8},{10,11... | collective-permute-start | bytes 3145736 | tf_op jit(solution)/shard_map/ppermute | solution.py:67
  (199 other events, 2646.4 us)

commit v2 on v1

--- a/solution.py
+++ b/solution.py
@@ -53,13 +53,25 @@
     )
 
 
+def after(value, *earlier):
+    return lax.optimization_barrier((value, *earlier))[0]
+
+
 def move_fsdp(values, dz, dx, dy):
+    return route_fsdp(values, lambda z, x, y: ((z + dz) % NZ, (x + dx) % NX, (y + dy) % NY))
+
+
+def swap_along(values, fz, fx, fy):
+    return route_fsdp(values, lambda z, x, y: (z ^ fz, x ^ fx, y ^ fy))
+
+
+def route_fsdp(values, target):
     pairs = []
     for z in range(NZ):
         for x in range(NX):
             for y in range(NY):
-                target = (((z + dz) % NZ) * NX + (x + dx) % NX) * NY + (y + dy) % NY
-                pairs.append(((z * NX + x) * NY + y, target))
+                to_z, to_x, to_y = target(z, x, y)
+                pairs.append(((z * NX + x) * NY + y, (to_z * NX + to_x) * NY + to_y))
     return lax.ppermute(values, "fsdp", pairs)
 
 
@@ -88,36 +100,86 @@
     return lax.all_to_all(blocks, "fsdp", split_axis=0, concat_axis=0, tiled=True).reshape(shape)
 
 
+def along(axis):
+    grid = [[[(z * NX + x) * NY + y for y in range(NY)] for x in range(NX)] for z in range(NZ)]
+    if axis == "z":
+        return [[grid[z][x][y] for z in range(NZ)] for x in range(NX) for y in range(NY)]
+    if axis == "x":
+        return [[grid[z][x][y] for x in range(NX)] for z in range(NZ) for y in range(NY)]
+    return [list(grid[z][x]) for z in range(NZ) for x in range(NX)]
+
+
+def staged_sum(values):
+    for axis in "zxy":
+        values = lax.psum_scatter(
+            values, "fsdp", scatter_dimension=0, tiled=True, axis_index_groups=along(axis)
+        )
+    return values
+
+
 def place_kernel(cuts, spot, *refs):
-    first, second = refs[:NZ], refs[NZ : NZ + NY]
-    outs = refs[NZ + NY :]
+    first, second, outs = refs[:5], refs[5:10], refs[10:]
     z, x, y = spot[0], spot[1], spot[2]
     half = first[0].shape[3]
+
+    def part(pieces, across, along_line, xr, item, columns):
+        if across == 2:
+            across += along_line // 2
+            along_line %= 2
+        elif across == 3:
+            across = 4
+        return pieces[across][along_line, xr, item, :, columns]
+
     for zr in range(NZ):
         for xr in range(NX):
             for yr in range(NY):
-                at = (lax.rem(z + zr, NZ), lax.rem(x + xr, NX), lax.rem(y + yr, NY))
+                at = (jnp.bitwise_xor(z, zr), jnp.bitwise_xor(x, xr), jnp.bitwise_xor(y, yr))
                 for number, (item, start, width) in enumerate(cuts):
                     columns = slice(start, start + width)
-                    outs[number][at[0], at[1], at[2], :half] = first[zr][yr, xr, item, :, columns]
-                    outs[number][at[0], at[1], at[2], half:] = second[yr][zr, xr, item, :, columns]
-
-
-def gather_fsdp(stacked, spot, cuts):
-    items, rows, columns = stacked.shape
-    half = rows // 2
-    pair = jnp.stack([stacked, move_fsdp(stacked, 0, 1, 0)])
-    near_y, near_z = pair[:, :, :half], pair[:, :, half:]
-    by_y = jnp.stack([near_y] + [move_fsdp(near_y, 0, 0, -r) for r in range(1, NY)])
-    by_z = jnp.stack([near_z] + [move_fsdp(near_z, -r, 0, 0) for r in range(1, NZ)])
-    first = [by_y] + [move_fsdp(by_y, -r, 0, 0) for r in range(1, NZ)]
-    second = [by_z] + [move_fsdp(by_z, 0, 0, -r) for r in range(1, NY)]
+                    outs[number][at[0], at[1], at[2], :half] = part(
+                        first, zr, yr, xr, item, columns
+                    )
+                    outs[number][at[0], at[1], at[2], half:] = part(
+                        second, yr, zr, xr, item, columns
+                    )
+
+
+def gather_pair(stacked):
+    half = stacked.shape[1] // 2
+    pair = jnp.stack([stacked, swap_along(stacked, 0, 1, 0)])
+    return pair[:, :, :half], pair[:, :, half:]
+
+
+def gather_lines(pair):
+    near_y, near_z = pair
+    by_y = jnp.stack([near_y] + [swap_along(near_y, 0, 0, r) for r in range(1, NY)])
+    by_z = jnp.stack([near_z] + [swap_along(near_z, r, 0, 0) for r in range(1, NZ)])
+    return lax.optimization_barrier((by_y, by_z))
+
+
+def gather_near(lines):
+    by_y, by_z = lines
+    return lax.optimization_barrier(
+        (
+            swap_along(by_y, 1, 0, 0),
+            swap_along(by_y, 3, 0, 0),
+            swap_along(by_z, 0, 0, 1),
+            swap_along(by_z, 0, 0, 3),
+        )
+    )
+
+
+def gather_all(lines, near, spot, cuts):
+    by_y, by_z = lines
+    rows = 2 * by_y.shape[3]
+    first = [by_y, near[0], swap_along(near[0][:2], 3, 0, 0), swap_along(near[1][2:], 1, 0, 0), near[1]]
+    second = [by_z, near[2], swap_along(near[2][:2], 0, 0, 3), swap_along(near[3][2:], 0, 0, 1), near[3]]
     total = FSDP * rows
     wholes = pl.pallas_call(
         functools.partial(place_kernel, cuts),
         out_shape=[jax.ShapeDtypeStruct((NZ, NX, NY, rows, width), bf16) for _, _, width in cuts],
         in_specs=[pl.BlockSpec(memory_space=pltpu.SMEM)]
-        + [pl.BlockSpec(memory_space=pltpu.VMEM)] * (NZ + NY),
+        + [pl.BlockSpec(memory_space=pltpu.VMEM)] * 10,
         out_specs=[pl.BlockSpec(memory_space=pltpu.VMEM)] * len(cuts),
         compiler_params=pltpu.CompilerParams(vmem_limit_bytes=32 * 1024 * 1024),
         cost_estimate=pl.CostEstimate(
@@ -132,40 +194,46 @@
     return lax.dynamic_index_in_dim(values, index, axis, keepdims=False)
 
 
-def scatter_fsdp(join, grads, spot):
-    z, x, y = spot[0], spot[1], spot[2]
+def first_sum(cut, count, send):
+    total = cut(0).astype(f32)
+    for r in range(1, count):
+        total = total + send(cut(r), r).astype(f32)
+    return total.astype(bf16)
+
+
+def send_z(part, r):
+    return move_fsdp(part, r, 0, 0)
+
+
+def send_y(part, r):
+    return move_fsdp(part, 0, 0, r)
+
+
+def scatter_fsdp_one(join, grads, spot):
+    z, y = spot[0], spot[2]
     rows = grads[0].shape[0] // FSDP
     views = [g.reshape(NZ, NX, NY, 2, rows // 2, g.shape[1]) for g in grads]
     joined = lambda parts: join([p[None] for p in parts])
 
-    def first_sum(cut, count, send):
-        total = cut(0).astype(f32)
-        for r in range(1, count):
-            total = total + send(cut(r), r).astype(f32)
-        return total.astype(bf16)
+    one = first_sum(
+        lambda r: joined([pick(v, lax.rem(z + r, NZ), 0)[:, :, 0] for v in views]), NZ, send_z
+    )
+    two = first_sum(
+        lambda r: joined([pick(v, lax.rem(y + r, NY), 2)[:, :, 1] for v in views]), NY, send_y
+    )
+    return one, two
+
+
+def scatter_fsdp_two(parts, spot):
+    z, x, y = spot[0], spot[1], spot[2]
+    one = first_sum(lambda r: pick(parts[0], lax.rem(y + r, NY), 2), NY, send_y)
+    two = first_sum(lambda r: pick(parts[1], lax.rem(z + r, NZ), 1), NZ, send_z)
+    one, two = lax.optimization_barrier((one, two))
 
     def last_sum(kept):
         mine, theirs = pick(kept, x, 1), pick(kept, 1 - x, 1)
         return mine.astype(f32) + move_fsdp(theirs, 0, 1, 0).astype(f32)
 
-    def send_z(part, r):
-        return move_fsdp(part, r, 0, 0)
-
-    def send_y(part, r):
-        return move_fsdp(part, 0, 0, r)
-
-    def z_index(r):
-        return lax.rem(z + r, NZ)
-
-    def y_index(r):
-        return lax.rem(y + r, NY)
-
-    one = first_sum(lambda r: joined([pick(v, z_index(r), 0)[:, :, 0] for v in views]), NZ, send_z)
-    two = first_sum(
-        lambda r: joined([pick(v, y_index(r), 2)[:, :, 1] for v in views]), NY, send_y
-    )
-    one = first_sum(lambda r: pick(one, y_index(r), 2), NY, send_y)
-    two = first_sum(lambda r: pick(two, z_index(r), 1), NZ, send_z)
     return jnp.concatenate([last_sum(one), last_sum(two)], axis=1)
 
 
@@ -285,6 +353,233 @@
     )(where, qkv, qkv, qkv, grads)
 
 
+def expert_rows_kernel(
+    scal, rows_own, gate_lanes, rows_far, grads_own, grads_far,
+    eg_own, eg_far, eu_own, eu_far, ed_own, ed_far, d_gate, d_up, hidden, sent_far, dots,
+):
+    count, width = rows_own.shape[0], eg_own.shape[0]
+    experts = dots.shape[1] // 2
+    row = lax.broadcasted_iota(jnp.int32, (count, 1), 0) + pl.program_id(0) * count
+    second = (lax.rem(row, 2 * CAP) >= CAP).astype(jnp.int32)
+    column = (lax.broadcasted_iota(jnp.int32, (1, width), 1) >= width // 2).astype(jnp.int32)
+    mine = second == column
+    lane = lax.broadcasted_iota(jnp.int32, (1, 2 * experts), 1)
+    expert_of = scal[1] + second
+    high_lane, low_lane = lane == expert_of, lane == experts + expert_of
+    gate_of = jnp.sum(
+        jnp.where(high_lane | low_lane, gate_lanes[...].astype(f32), 0.0), axis=1, keepdims=True
+    )
+    gate_mine = jnp.where(mine, gate_of, 0.0)
+
+    def product(own, far, w_own, w_far):
+        return contract_last(own[...], w_own[...]) + contract_last(far[...], w_far[...])
+
+    gate_pre = product(rows_own, rows_far, eg_own, eg_far)
+    up_pre = product(rows_own, rows_far, eu_own, eu_far)
+    down_back = product(grads_own, grads_far, ed_own, ed_far) * gate_mine
+    sigmoid_v = jax.nn.sigmoid(gate_pre)
+    silu_gate = gate_pre * sigmoid_v
+    hidden_wide = silu_gate * up_pre
+    hidden[...] = (hidden_wide * gate_mine).astype(bf16)
+    gate_part = (
+        down_back * up_pre * (sigmoid_v * (1.0 + gate_pre * (1.0 - sigmoid_v)))
+    ).astype(bf16)
+    up_part = (down_back * silu_gate).astype(bf16)
+    d_gate[...] = gate_part
+    d_up[...] = up_part
+    sent_far[...] = (matmul(gate_part, eg_far[...]) + matmul(up_part, eu_far[...])).astype(bf16)
+    slot_dot = jnp.sum(hidden_wide * down_back, axis=1, keepdims=True)
+    high = slot_dot.astype(bf16).astype(f32)
+    dots[...] = jnp.where(high_lane, high, jnp.where(low_lane, slot_dot - high, 0.0)).astype(bf16)
+
+
+def expert_rows(scal, rows_own, rows_far, grads_own, grads_far, gate_w, up_w, down_w, steps=2):
+    rows, wide = grads_own.shape
+    hidden = gate_w.shape[0]
+    count = rows // steps
+    block = pl.BlockSpec((count, wide), lambda i, c: (i, 0))
+    own = pl.BlockSpec((hidden, wide), lambda i, c: (0, c[0]))
+    far = pl.BlockSpec((hidden, wide), lambda i, c: (0, 1 - c[0]))
+    narrow = pl.BlockSpec((count, hidden), lambda i, c: (i, 0))
+    lanes = pl.BlockSpec((count, LANES), lambda i, c: (i, 0))
+    last_lanes = pl.BlockSpec((count, LANES), lambda i, c: (i, wide // LANES))
+    shape = lambda columns: jax.ShapeDtypeStruct((rows, columns), bf16)
+    return pl.pallas_call(
+        expert_rows_kernel,
+        out_shape=[shape(hidden), shape(hidden), shape(hidden), shape(wide), shape(LANES)],
+        grid_spec=pltpu.PrefetchScalarGridSpec(
+            num_scalar_prefetch=1,
+            grid=(steps,),
+            in_specs=[block, last_lanes] + [block] * 3 + [own, far] * 3,
+            out_specs=[narrow] * 3 + [block, lanes],
+        ),
+        compiler_params=pltpu.CompilerParams(vmem_limit_bytes=56 * 1024 * 1024),
+        cost_estimate=pl.CostEstimate(
+            flops=16 * rows * wide * hidden,
+            bytes_accessed=12 * hidden * wide + 12 * rows * wide,
+            transcendentals=rows * hidden,
+        ),
+        name="expert_rows",
+    )(
+        scal, rows_own, rows_own, rows_far, grads_own, grads_far,
+        gate_w, gate_w, up_w, up_w, down_w, down_w,
+    )
+
+
+def join_kernel(left, right, tail, out):
+    wide = left.shape[1]
+    out[:, :wide] = (left[...].astype(f32) + right[...].astype(f32)).astype(bf16)
+    out[:, wide:] = tail[...]
+
+
+def add_and_join(left, right, tail, steps=4):
+    rows, wide = left.shape
+    block = pl.BlockSpec((rows // steps, wide), lambda i: (i, 0))
+    return pl.pallas_call(
+        join_kernel,
+        out_shape=jax.ShapeDtypeStruct((rows, wide + tail.shape[1]), bf16),
+        grid=(steps,),
+        in_specs=[block, block, pl.BlockSpec((rows // steps, tail.shape[1]), lambda i: (i, 0))],
+        out_specs=pl.BlockSpec((rows // steps, wide + tail.shape[1]), lambda i: (i, 0)),
+        cost_estimate=pl.CostEstimate(
+            flops=rows * wide, bytes_accessed=6 * rows * wide, transcendentals=0
+        ),
+        name="add_and_join",
+    )(left, right, tail)
+
+
+def combine_kernel(with_logits, core, dispatch, back, base, *refs):
+    half = base.shape[1] // 2
+    total = matmul(dispatch[...], back[...])
+    extra = 0.0
+    if with_logits:
+        gates, tile, out, logits = refs
+        experts = LANES // 2
+        lanes = total[:, half:]
+        dots = lanes + pltpu.roll(lanes, experts, 1)
+        lane = lax.broadcasted_iota(jnp.int32, dots.shape, 1)
+        dots = jnp.where(lane < experts, dots, 0.0)
+        d_logits = (dots - gates[...] * jnp.sum(dots, axis=-1, keepdims=True)).astype(bf16)
+        logits[...] = d_logits
+        extra = contract_last(d_logits, tile[...])
+    else:
+        (out,) = refs
+    sums = base[...].astype(f32) + extra
+    for number in range(2):
+        columns = slice(number * half, (number + 1) * half)
+        chosen = jnp.where(core[0] == number, total[:, :half], 0.0)
+        out[:, columns] = (sums[:, columns] + chosen).astype(out.dtype)
+
+
+def combine(core, block, dispatch, back, base, dtype, gates=None, tile=None):
+    rows, dim = base.shape[0] // 2, base.shape[1]
+    slots, width = back.shape
+    with_logits = gates is not None
+    part = lambda columns: pl.BlockSpec((rows, columns), lambda i, c: (block, 0))
+    whole = lambda shape: pl.BlockSpec(shape, lambda i, c: (0, 0))
+    specs = [part(slots), whole((slots, width)), part(dim)]
+    args = [dispatch, back, base]
+    shapes = [jax.ShapeDtypeStruct((rows, dim), dtype)]
+    outs = [whole((rows, dim))]
+    if with_logits:
+        specs += [part(LANES), whole(tile.shape)]
+        args += [gates, tile]
+        shapes.append(jax.ShapeDtypeStruct((rows, LANES), bf16))
+        outs.append(whole((rows, LANES)))
+    return pl.pallas_call(
+        functools.partial(combine_kernel, with_logits),
+        out_shape=shapes,
+        grid_spec=pltpu.PrefetchScalarGridSpec(
+            num_scalar_prefetch=1, grid=(1,), in_specs=specs, out_specs=outs
+        ),
+        compiler_params=pltpu.CompilerParams(vmem_limit_bytes=48 * 1024 * 1024),
+        cost_estimate=pl.CostEstimate(
+            flops=2 * rows * slots * width,
+            bytes_accessed=2 * slots * width + 8 * rows * dim,
+            transcendentals=0,
+        ),
+        name="combine",
+    )(core, *args)
+
+
+def shared_rows_kernel(rows, grads, weights, d_gate, d_up, hidden, out, back):
+    def weight(number):
+        part = weights[:, number]
+        return part.reshape(part.shape[0] * part.shape[1], part.shape[2])
+
+    gate_pre = matmul(rows[...], weight(0))
+    up_pre = matmul(rows[...], weight(1))
+    down_back = matmul(grads[...], weight(2))
+    sigmoid_v = jax.nn.sigmoid(gate_pre)
+    silu_gate = gate_pre * sigmoid_v
+    hidden_part = (silu_gate * up_pre).astype(bf16)
+    hidden[...] = hidden_part
+    out[...] = contract_last(hidden_part, weight(2)).astype(bf16)
+    gate_part = (
+        down_back * up_pre * (sigmoid_v * (1.0 + gate_pre * (1.0 - sigmoid_v)))
+    ).astype(bf16)
+    up_part = (down_back * silu_gate).astype(bf16)
+    d_gate[...] = gate_part
+    d_up[...] = up_part
+    back[...] = (contract_last(gate_part, weight(0)) + contract_last(up_part, weight(1))).astype(
+        bf16
+    )
+
+
+def shared_rows(rows, grads, weights, steps=2):
+    count, dim = rows.shape
+    hidden = weights.shape[3]
+    wide = pl.BlockSpec((count // steps, dim), lambda i: (i, 0))
+    narrow = pl.BlockSpec((count // steps, hidden), lambda i: (i, 0))
+    shape = lambda columns: jax.ShapeDtypeStruct((count, columns), bf16)
+    return pl.pallas_call(
+        shared_rows_kernel,
+        out_shape=[shape(hidden)] * 3 + [shape(dim)] * 2,
+        grid=(steps,),
+        in_specs=[wide, wide, pl.BlockSpec(weights.shape, lambda i: (0, 0, 0, 0))],
+        out_specs=[narrow] * 3 + [wide] * 2,
+        compiler_params=pltpu.CompilerParams(vmem_limit_bytes=56 * 1024 * 1024),
+        cost_estimate=pl.CostEstimate(
+            flops=12 * count * dim * hidden,
+            bytes_accessed=6 * dim * hidden + 8 * count * dim,
+            transcendentals=count * hidden,
+        ),
+        name="shared_rows",
+    )(rows, grads, weights)
+
+
+def shared_grads_kernel(rows, grads, d_gate, d_up, hidden, out):
+    number = pl.program_id(0)
+
+    def write(left, right):
+        out[...] = contract_first(left[...], right[...]).astype(bf16).reshape(out.shape)
+
+    pl.when(number == 0)(lambda: write(rows, d_gate))
+    pl.when(number == 1)(lambda: write(rows, d_up))
+    pl.when(number == 2)(lambda: write(grads, hidden))
+
+
+def shared_grads(rows, grads, d_gate, d_up, hidden, own_rows):
+    count, dim = rows.shape
+    width = d_gate.shape[1]
+    wide = pl.BlockSpec((count, dim), lambda i: (0, 0))
+    narrow = pl.BlockSpec((count, width), lambda i: (0, 0))
+    return pl.pallas_call(
+        shared_grads_kernel,
+        out_shape=jax.ShapeDtypeStruct((FSDP, 3, own_rows, width), bf16),
+        grid=(3,),
+        in_specs=[wide] * 2 + [narrow] * 3,
+        out_specs=pl.BlockSpec((FSDP, 1, own_rows, width), lambda i: (0, i, 0, 0)),
+        compiler_params=pltpu.CompilerParams(vmem_limit_bytes=48 * 1024 * 1024),
+        cost_estimate=pl.CostEstimate(
+            flops=6 * count * dim * width,
+            bytes_accessed=6 * dim * width + 4 * count * dim,
+            transcendentals=0,
+        ),
+        name="shared_grads",
+    )(rows, grads, d_gate, d_up, hidden)
+
+
 def expert_grads_kernel(core, rows_own, rows_far, grads_own, grads_far, d_gate, d_up, scaled, *outs):
     half = pl.program_id(0)
 
@@ -298,7 +593,7 @@
 
 
 def expert_grads(core, rows_own, rows_far, grads_own, grads_far, d_gate, d_up, scaled):
-    rows, wide = rows_own.shape
+    rows, wide = grads_own.shape
     hidden = d_gate.shape[1]
     full = pl.BlockSpec((rows, wide), lambda h, c: (0, 0))
     part = pl.BlockSpec((rows, hidden), lambda h, c: (0, 0))
@@ -359,35 +654,6 @@
         [fsdp_at // (NX * NY), lax.rem(fsdp_at // NY, NX), lax.rem(fsdp_at, NY)]
     ).astype(jnp.int32)
 
-    small_tile = jnp.concatenate(
-        [
-            w_router,
-            g_attn[:, None],
-            g_ffn[:, None],
-            jnp.zeros((own_rows, LANES - experts - 2), bf16),
-        ],
-        axis=1,
-    )
-    qkv_own = jnp.concatenate([query_matrix, key_matrix, value_matrix], axis=1)
-    w_qkv, w_tile = gather_fsdp(
-        jnp.concatenate([qkv_own, small_tile], axis=1)[None],
-        spot,
-        ((0, 0, qkv_width), (0, qkv_width, LANES)),
-    )
-    token_rows = gather_tp(tokens)
-    grad_rows = gather_tp(cotangent)
-    (w_out_all,) = gather_fsdp(w_out[None], spot, ((0, 0, q_width),))
-    wide = shared_gate.shape[1]
-    w_sgate, w_sup, w_sdown = gather_fsdp(
-        jnp.stack([shared_gate, shared_up, shared_down]),
-        spot,
-        ((0, 0, wide), (1, 0, wide), (2, 0, wide)),
-    )
-    lane = lax.broadcasted_iota(jnp.int32, (8, LANES), 1)
-    gain_pick = (lane == experts + lax.broadcasted_iota(jnp.int32, (8, LANES), 0)).astype(bf16)
-    gains = contract_last(gain_pick, w_tile)
-    gain_one, gain_two = gains[0:1], gains[1:2]
-
     route_blocks = routes.reshape(TP, tok_dev, routes.shape[1])
     own_routes = jnp.concatenate(
         [pick(route_blocks, jnp.bitwise_xor(b, rank), 0) for b in BLOCK_ORDER], axis=0
@@ -408,19 +674,51 @@
     def core_half(values):
         return lax.dynamic_slice_in_dim(values, core * half_dim, half_dim, 1)
 
+    small_tile = jnp.concatenate(
+        [
+            w_router,
+            g_attn[:, None],
+            g_ffn[:, None],
+            jnp.zeros((own_rows, LANES - experts - 2), bf16),
+        ],
+        axis=1,
+    )
+    qkv_own = jnp.concatenate([query_matrix, key_matrix, value_matrix], axis=1)
+    lines = gather_lines(
+        gather_pair(jnp.concatenate([qkv_own, small_tile, w_out], axis=1)[None])
+    )
+    near_lines = gather_near(lines)
+    token_pair = jnp.concatenate([tokens, after(move_tp(tokens, 2), *near_lines)], axis=0)
+    token_rows = jnp.concatenate([token_pair, move_tp(token_pair, 1)], axis=0)
+    grad_pair = jnp.concatenate([cotangent, after(move_tp(cotangent, 2), *near_lines)], axis=0)
+    grad_rows = jnp.concatenate([grad_pair, move_tp(grad_pair, 1)], axis=0)
+    w_qkv, w_tile, w_out_all = gather_all(
+        lines,
+        near_lines,
+        spot,
+        (
+            (0, 0, qkv_width),
+            (0, qkv_width, LANES),
+            (0, qkv_width + LANES, q_width),
+        ),
+    )
     slot_grads = contract_first(dispatch, core_half(grad_rows)).astype(bf16)
-    grads_own = swap_fsdp(slot_grads)
-    grads_far = move_tp(grads_own, 1)
+    grads_own = swap_fsdp(after(slot_grads, w_tile))
+    shared_own = jnp.concatenate([shared_gate, shared_up, shared_down], axis=0)
+    w_shared = lax.all_gather(
+        after(shared_own, w_tile), "fsdp", axis=0, tiled=True
+    ).reshape(FSDP, 3, own_rows, shared_gate.shape[1])
+    lane = lax.broadcasted_iota(jnp.int32, (8, LANES), 1)
+    gain_pick = (lane == experts + lax.broadcasted_iota(jnp.int32, (8, LANES), 0)).astype(bf16)
+    gains = contract_last(gain_pick, w_tile)
+    gain_one, gain_two = gains[0:1], gains[1:2]
 
     hidden_all = local_experts * hidden_own
 
-    def expert_halves(weights):
-        both = jnp.swapaxes(weights, 1, 2).reshape(hidden_all, dim)
-        return core_half(both), lax.dynamic_slice_in_dim(both, (1 - core) * half_dim, half_dim, 1)
-
-    eg_own, eg_far = expert_halves(expert_gate)
-    eu_own, eu_far = expert_halves(expert_up)
-    ed_own, ed_far = expert_halves(expert_down)
+    def by_hidden(weights):
+        return jnp.swapaxes(weights, 1, 2).reshape(hidden_all, dim)
+
+    gate_w, up_w, down_w = by_hidden(expert_gate), by_hidden(expert_up), by_hidden(expert_down)
 
     ends = jnp.cumsum(lengths[0])
     where = jnp.stack([rank.astype(jnp.int32), ends[0], ends[1]]).astype(jnp.int32)
@@ -428,17 +726,12 @@
     h_attn = normed_one.astype(bf16)
     qkv = matmul(h_attn, w_qkv).astype(bf16)
     attended = attend(where, qkv, heads)
-    attn_own = scatter_tp(
-        contract_last(attended[:near], w_out_all), contract_last(attended[near:], w_out_all)
-    )
+    attn_far = after(contract_last(attended[near:], w_out_all).astype(bf16), grads_own)
+    attn_own = scatter_tp(contract_last(attended[:near], w_out_all), attn_far)
     own_tokens = tokens.astype(f32)
     middle = own_tokens + attn_own
     normed_two, factor_two = norm_rows(middle, gain_two)
     h_ffn = gather_tp(normed_two.astype(bf16))
-
-    slot_rows = contract_first(dispatch, core_half(h_ffn)).astype(bf16)
-    rows_own = swap_fsdp(slot_rows)
-    rows_far = move_tp(rows_own, 1)
 
     logits = matmul(h_ffn, w_tile)
     top = jnp.max(jnp.where(hot, logits, -1e30), axis=-1, keepdims=True)
@@ -447,110 +740,77 @@
     gate_high = gates.astype(bf16)
     gate_low = (gates - gate_high.astype(f32)).astype(bf16)
     gate_lanes = jnp.concatenate([gate_high[:, :experts], gate_low[:, :experts]], axis=1)
-    gated = (matmul(gate_high, spread) * dispatch.astype(f32)).astype(bf16)
-    slot_gates = swap_fsdp(contract_first(dispatch, gate_lanes).astype(bf16))
-
-    s_gate_pre = matmul(h_ffn, w_sgate)
-    s_up_pre = matmul(h_ffn, w_sup)
-    s_hidden = (jax.nn.silu(s_gate_pre) * s_up_pre).astype(bf16)
-    grad_shidden = matmul(grad_rows, w_sdown)
-    grad_sgate_pre = (grad_shidden * s_up_pre * silu_slope(s_gate_pre)).astype(bf16)
-    grad_sup_pre = (grad_shidden * jax.nn.silu(s_gate_pre)).astype(bf16)
-    grad_sdown = contract_first(grad_rows, s_hidden).astype(bf16)
-    grad_sgate = contract_first(h_ffn, grad_sgate_pre).astype(bf16)
-    grad_sup = contract_first(h_ffn, grad_sup_pre).astype(bf16)
-    shared_sums = scatter_fsdp(
-        lambda parts: jnp.concatenate(parts, axis=0), [grad_sgate, grad_sup, grad_sdown], spot
-    )
-    shared_out = contract_last(s_hidden, w_sdown)
-    shared_back = contract_last(grad_sgate_pre, w_sgate) + contract_last(grad_sup_pre, w_sup)
-
-    row_ids = lax.broadcasted_iota(jnp.int32, (slots, 1), 0)
-    second = (row_ids % (local_experts * CAP)) // CAP
-    mine = second == (lax.broadcasted_iota(jnp.int32, (1, hidden_all), 1) // hidden_own)
-
-    gate_pre = contract_last(rows_own, eg_own) + contract_last(rows_far, eg_far)
-    up_pre = contract_last(rows_own, eu_own) + contract_last(rows_far, eu_far)
-    down_back = contract_last(grads_own, ed_own) + contract_last(grads_far, ed_far)
-    silu_gate = jax.nn.silu(gate_pre)
-    hidden_wide = jnp.where(mine, silu_gate * up_pre, 0.0)
-    hidden = hidden_wide.astype(bf16)
-    d_gate = jnp.where(mine, down_back * up_pre * silu_slope(gate_pre), 0.0).astype(bf16)
-    d_up = jnp.where(mine, down_back * silu_gate, 0.0).astype(bf16)
-    slot_dot = jnp.sum(hidden_wide * down_back, axis=1, keepdims=True)
-    lane_ids = lax.broadcasted_iota(jnp.int32, (1, LANES), 1)
-    expert_of = local_experts * fsdp_at.astype(jnp.int32) + second
-    dot_high = slot_dot.astype(bf16)
-    dot_low = (slot_dot - dot_high.astype(f32)).astype(bf16)
-    zero = jnp.zeros((), bf16)
-    dot_lanes = jnp.where(lane_ids == expert_of, dot_high, zero) + jnp.where(
-        lane_ids == experts + expert_of, dot_low, zero
-    )
-
-    def back_product(gate_w, up_w):
-        return matmul(d_gate, gate_w) + matmul(d_up, up_w)
-
-    sent_far = move_tp(back_product(eg_far, eu_far).astype(bf16), 1)
-    sent_own = (back_product(eg_own, eu_own) + sent_far.astype(f32)).astype(bf16)
-    returned = swap_fsdp(jnp.concatenate([sent_own, dot_lanes], axis=1))
-
-    out_far = move_tp(matmul(hidden, ed_far).astype(bf16), 1)
-    out_own = (matmul(hidden, ed_own) + out_far.astype(f32)).astype(bf16)
-    out_back = swap_fsdp(out_own)
-
-    is_gate = (lane_ids == expert_of) | (lane_ids == experts + expert_of)
-    gate_of = jnp.sum(jnp.where(is_gate, slot_gates.astype(f32), 0.0), axis=1, keepdims=True)
-    grad_egate, grad_eup, grad_edown = expert_grads(
-        core_vec,
-        rows_own,
-        rows_far,
-        grads_own,
-        grads_far,
-        (gate_of * d_gate.astype(f32)).astype(bf16),
-        (gate_of * d_up.astype(f32)).astype(bf16),
-        (gate_of * hidden.astype(f32)).astype(bf16),
-    )
+
+    slot_rows = contract_first(
+        dispatch, jnp.concatenate([core_half(h_ffn), gate_lanes], axis=1)
+    ).astype(bf16)
+    grads_far = move_tp(after(grads_own, slot_rows), 1)
+    rows_own = swap_fsdp(slot_rows)
+
+    rows_far = move_tp(rows_own, 1)
+    scal = jnp.stack([core.astype(jnp.int32), local_experts * fsdp_at.astype(jnp.int32)])
+    d_gate, d_up, hidden, sent_far, dot_lanes = expert_rows(
+        scal, rows_own, rows_far, grads_own, grads_far, gate_w, up_w, down_w
+    )
+    sent_far = move_tp(sent_far, 1)
+    sent_own = (matmul(d_gate, core_half(gate_w)) + matmul(d_up, core_half(up_w))).astype(bf16)
+    payload = add_and_join(sent_own, sent_far, dot_lanes)
+    returned = swap_fsdp(payload)
+
+    h_then = after(h_ffn, payload)
+    s_d_gate, s_d_up, s_hidden, shared_out, shared_back = shared_rows(h_then, grad_rows, w_shared)
+    shared_parts = shared_grads(h_then, grad_rows, s_d_gate, s_d_up, s_hidden, own_rows)
+    shared_sums = staged_sum(shared_parts)[0].astype(f32)
+
+    hidden_then = after(hidden, payload)
+    down_own = core_half(down_w)
+    down_far = lax.dynamic_slice_in_dim(down_w, (1 - core) * half_dim, half_dim, 1)
+    out_far = move_tp(matmul(hidden_then, down_far).astype(bf16), 1)
+    out_own = (matmul(hidden_then, down_own) + out_far.astype(f32)).astype(bf16)
 
     def expert_layout(grads):
         return jnp.swapaxes(grads.reshape(local_experts, hidden_own, dim), 1, 2)
 
-    def whole_width(values):
-        return jnp.concatenate(
-            [jnp.where(core == 0, values, 0.0), jnp.where(core == 1, values, 0.0)], axis=1
-        )
-
-    routed = matmul(gated, out_back)
-    out_part = shared_out + whole_width(routed)
-    output = (middle + scatter_tp(out_part[:near], out_part[near:])).astype(bf16)
-
-    combined = matmul(gated, returned)
-    dots = combined[:, half_dim : half_dim + experts] + combined[:, half_dim + experts :]
-    d_logits = dots - gates[:, :experts] * jnp.sum(dots, axis=-1, keepdims=True)
-    d_logits = jnp.pad(d_logits.astype(bf16), ((0, 0), (0, LANES - experts)))
-    ffn_part = (
-        shared_back + whole_width(combined[:, :half_dim]) + contract_last(d_logits, w_tile)
-    )
-    d_h_ffn = scatter_tp(ffn_part[:near], ffn_part[near:])
+    returned = after(returned, shared_back, shared_parts, out_own)
+    ffn_far, logits_far = combine(
+        core_vec, 1, dispatch, returned, shared_back, bf16, gates, w_tile
+    )
+    ffn_near, logits_near = combine(
+        core_vec, 0, dispatch, returned, shared_back, f32, gates, w_tile
+    )
+    d_h_ffn = scatter_tp(ffn_near, ffn_far)
     d_middle = cotangent.astype(f32) + norm_back(middle, factor_two, gain_two, d_h_ffn)
+    lane_ids = lax.broadcasted_iota(jnp.int32, (1, LANES), 1)
     gain_terms = (d_h_ffn * middle * factor_two).astype(bf16)
     gain_lane = jnp.broadcast_to(lane_ids == experts, (tok_dev, LANES)).astype(bf16)
-    grad_tile = (contract_first(h_ffn, d_logits) + contract_first(gain_terms, gain_lane)).astype(
-        bf16
-    )
-    d_att = gather_tp(d_middle.astype(bf16))
+    d_att_own = d_middle.astype(bf16)
+    d_att_near = jnp.concatenate([d_att_own, move_tp(d_att_own, 2)], axis=0)
+    out_back = swap_fsdp(after(out_own, d_att_near))
+    d_att = jnp.concatenate([d_att_near, move_tp(d_att_near, 1)], axis=0)
+    grad_tile = (
+        contract_first(h_ffn, jnp.concatenate([logits_near, logits_far], axis=0))
+        + contract_first(gain_terms, gain_lane)
+    ).astype(bf16)
     grad_wout = contract_first(d_att, attended).astype(bf16)
-    out_sums = scatter_fsdp(
-        lambda parts: jnp.concatenate(parts, axis=-1), [grad_wout, grad_tile], spot
-    )[0]
-    tile_sums = small_sum_tp(out_sums[:, q_width:])
-
     d_attended = matmul(d_att, w_out_all).astype(bf16)
     d_qkv = attend_back(where, qkv, d_attended, heads)
     grad_wqkv = contract_first(h_attn, d_qkv).astype(bf16)
-    qkv_sums = scatter_fsdp(lambda parts: parts[0], [grad_wqkv], spot)[0]
-    d_h_attn = scatter_tp(
-        contract_last(d_qkv[:near], w_qkv), contract_last(d_qkv[near:], w_qkv)
-    )
+    sum_parts = scatter_fsdp_one(
+        lambda parts: jnp.concatenate(parts, axis=-1), [grad_wout, grad_tile, grad_wqkv], spot
+    )
+    attn_far = contract_last(d_qkv[near:], w_qkv).astype(bf16)
+    d_h_attn = scatter_tp(contract_last(d_qkv[:near], w_qkv), attn_far)
+    back_then = after(out_back, attn_far)
+    (out_far,) = combine(core_vec, 1, dispatch, back_then, shared_out, bf16)
+    (out_near,) = combine(core_vec, 0, dispatch, back_then, shared_out, f32)
+    output = (middle + scatter_tp(out_near, out_far)).astype(bf16)
+    grad_egate, grad_eup, grad_edown = expert_grads(
+        core_vec, rows_own, rows_far, grads_own, grads_far, d_gate, d_up, after(hidden, grad_wqkv)
+    )
+    sum_parts = after(sum_parts, d_h_attn, out_near, grad_egate)
+    sums = scatter_fsdp_two(sum_parts, spot)[0]
+    out_sums, tile_sums = sums[:, :q_width], small_sum_tp(sums[:, q_width : q_width + LANES])
+    qkv_sums = sums[:, q_width + LANES :]
     _, factor_one = norm_rows(own_tokens, gain_one)
     grad_tokens = (d_middle + norm_back(own_tokens, factor_one, gain_one, d_h_attn)).astype(bf16)
     gain_sum = jnp.sum(qkv_sums * qkv_own.astype(f32), axis=1)
@@ -562,7 +822,7 @@
         qkv_sums[:, :q_width],
         qkv_sums[:, q_width : q_width + kv_width],
         qkv_sums[:, q_width + kv_width :],
-        out_sums[:, :q_width],
+        out_sums,
         tile_sums[:, experts],
         tile_sums[:, :experts],
         shared_sums[0],

time: 836 us -> 598 us (0.72)
  waiting for transfers between devices: 288 us -> 153 us
  starting transfers between devices: 209 us -> 95.8 us
  matrix products: 132 us -> 53.9 us
  blocking collectives: 0 us -> 68.1 us
  Pallas kernels: 39.5 us -> 106 us
  local copies, waits for them, and re-layouts: 88.7 us -> 53.9 us
  other arithmetic: 65.5 us -> 41.6 us
  between operations: 3.41 us -> 15.6 us
    ppermute x81 -> x29, waiting for transfers between devices: 213 us -> 67.9 us  [route_fsdp(): return lax.ppermute(values, 'fsdp', pairs)]
    ppermute x81 -> x29, starting transfers between devices: 121 us -> 43.6 us  [route_fsdp(): return lax.ppermute(values, 'fsdp', pairs)]
    all_to_all x0 -> x1, blocking collectives: none -> 68.1 us  [swap_fsdp(): lax.all_to_all(blocks, 'fsdp', split_axis=0, concat_axis=0, tiled=True)]
    pallas_call x3 -> x9, Pallas kernels: 7.63 us -> 73.8 us  [the longest x1 28.3 us: expert_rows(): pl.pallas_call(expert_rows_kernel, out_shape=[shape(hidden), shape(hidden...]
    dot_general x15 -> x5, matrix products: 58.7 us -> 9.47 us  [contract_last(): lax.dot_general(left_op, right_op, (((1,), (1,)), ((), ())), preferred_el...]
    ppermute x26, waiting for transfers between devices: 26.3 us -> 70.9 us  [move_tp(): return lax.ppermute(values, 'tp', [(i, i ^ flip) for i in range(TP)])]
    all_to_all x5 -> x3, waiting for transfers between devices: 49.1 us -> 14.5 us  [swap_fsdp(): lax.all_to_all(blocks, 'fsdp', split_axis=0, concat_axis=0, tiled=True)]
    ppermute x26, starting transfers between devices: 50.1 us -> 31 us  [move_tp(): return lax.ppermute(values, 'tp', [(i, i ^ flip) for i in range(TP)])]
  transfers between devices with their start and end apart: 112 -> 62, of which waited for: 42 -> 26; matrix products, arithmetic and copies ran while one was open for 30% -> 19% of each run, Pallas kernels for 4% -> 18%
where the time goes in v2:
time: 598 us; the launch traced here: 588 us
  waiting for transfers between devices  153 us (26%)
  Pallas kernels  106 us (18%)
  starting transfers between devices  95.8 us (16%)
  blocking collectives  68.1 us (11%)
  local copies, waits for them, and re-layouts  53.9 us (9%)
  matrix products  53.9 us (9%)
  other arithmetic  41.6 us (7%)
  between operations  15.6 us (3%)
    ppermute x26, waiting for transfers between devices, move_tp(): return lax.ppermute(values, 'tp', [(i, i ^ flip) for i in range(TP)])  70.9 us
    all_to_all x1, blocking collectives, swap_fsdp(): lax.all_to_all(blocks, 'fsdp', split_axis=0, concat_axis=0, tiled=True)  68.1 us
    ppermute x29, waiting for transfers between devices, route_fsdp(): return lax.ppermute(values, 'fsdp', pairs)  67.9 us
    ppermute x29, starting transfers between devices, route_fsdp(): return lax.ppermute(values, 'fsdp', pairs)  43.6 us
    ppermute x26, starting transfers between devices, move_tp(): return lax.ppermute(values, 'tp', [(i, i ^ flip) for i in range(TP)])  31 us
    dot_general x8, matrix products, matmul(): return jnp.dot(left_op, right_op, preferred_element_type=f32)  29.8 us
    unnamed x168, local copies, waits for them, and re-layouts  29.2 us
    pallas_call x1, Pallas kernels, expert_rows(): pl.pallas_call(expert_rows_kernel, out_shape=[shape(hidden), shape(hidden...  28.3 us
  transfers between devices with their start and end apart: 62, of which 26 were waited for; matrix products, arithmetic and copies ran while one was open for 19% of the time, Pallas kernels for 18%

profile of v2, /device:TPU:1, one launch (start us, length us, event | category | flops | bytes accessed | tf_op | source)
XLA Modules:
  0.0 587.8 jit_solution(1893356131693514770)
XLA Ops:
  13.5 3.8 collective-permute-done.1
  42.1 8.7 %collective-permute-done.8 = bf16[4,2,1,32,1408]{4,3,1,2,0:T(8,128)(2,1)S(1)} collective-permute-done((bf16[4,2,1,32,1408]{4,3,1,2,0:T(8,128)(2,1)S(1)}, bf16[4,2,1,32,1408]{4,3,1,2,0:T(8,128)(2,1)S(1)}, u32[]{:S(2)}, u32[]{:S(2)}) %collective-permute-start.8) | collective-permute-done | bytes 720928 | tf_op jit(solution)/shard_map/ppermute | solution.py:75
  72.1 5.2 collective-permute-done.13
  96.3 8.2 %all-to-all-start = ((bf16[32,40,1024]{2,1,0:T(8,128)(2,1)}), bf16[32,40,1024]{2,1,0:T(8,128)(2,1)}, u32[]{:S(2)}, u32[]{:S(2)}) async-start(bf16[32,40,1024]{2,1,0:T(8,128)(2,1)} %bitcast.279), calls=%async_computation | async-start | bytes 5242880 | tf_op jit(solution)/shard_map/all_to_all | solution.py:100
  114.2 4.4 convolution_convert_fusion.7.q_ref.k_ref.v_ref
  118.6 4.9 attend.1
  127.0 10.5 %all-to-all-done = bf16[32,40,1024]{2,1,0:T(8,128)(2,1)} async-done(((bf16[32,40,1024]{2,1,0:T(8,128)(2,1)}), bf16[32,40,1024]{2,1,0:T(8,128)(2,1)}, u32[]{:S(2)}, u32[]{:S(2)}) %all-to-all-start) | async-done | bytes 2621472 | tf_op jit(solution)/shard_map/all_to_all | solution.py:100
  146.0 14.8 %collective-permute-done.20 = bf16[128,2048]{1,0:T(8,128)(2,1)S(1)} collective-permute-done((bf16[128,2048]{1,0:T(8,128)(2,1)S(1)}, bf16[128,2048]{1,0:T(8,128)(2,1)S(1)}, u32[]{:S(2)}, u32[]{:S(2)}) %collective-permute-start.20) | collective-permute-done | bytes 524320 | tf_op jit(solution)/shard_map/ppermute | solution.py:79
  163.0 11.7 %collective-permute-done.21 = bf16[128,2048]{1,0:T(8,128)(2,1)S(1)} collective-permute-done((bf16[128,2048]{1,0:T(8,128)(2,1)S(1)}, bf16[128,2048]{1,0:T(8,128)(2,1)S(1)}, u32[]{:S(2)}, u32[]{:S(2)}) %collective-permute-start.21) | collective-permute-done | bytes 524320 | tf_op jit(solution)/shard_map/ppermute | solution.py:79
  187.7 68.1 %all_to_all.20 = bf16[32,40,1152]{2,1,0:T(8,128)(2,1)} all-to-all(bf16[32,40,1152]{2,1,0:T(8,128)(2,1)S(1)} %bitcast.277), channel_id=1, replica_groups=mesh['fsdp'=32,'tp'=4] {'fsdp'}, dimensions={0} | all-to-all | bytes 5898240 | tf_op jit(solution)/shard_map/all_to_all | solution.py:100
  255.8 3.8 collective-permute-start.23
  260.6 8.1 %collective-permute-done.24.grads_far = bf16[1280,1024]{1,0:T(8,128)(2,1)} collective-permute-done((bf16[1280,1024]{1,0:T(8,128)(2,1)}, bf16[1280,1024]{1,0:T(8,128)(2,1)}, u32[]{:S(2)}, u32[]{:S(2)}) %collective-permute-start.24) | collective-permute-done | bytes 2621472 | tf_op jit(solution)/shard_map/ppermute | solution.py:79
  268.7 28.3 %expert_rows.1 = (bf16[1280,704]{1,0:T(8,128)(2,1)}, bf16[1280,704]{1,0:T(8,128)(2,1)}, bf16[1280,704]{1,0:T(8,128)(2,1)}, bf16[1280,1024]{1,0:T(8,128)(2,1)}, bf16[1280,128]{1,0:T(8,128)(2,1)}) custom-call(s32[2]{0:T(128)} %pad_add_fusion.4.scal, bf16[1280,1152]{1,0:T(8,128)(2,1)} %bitcast.45.rows_own.gate_lanes, ...), custom_call_target="tpu_custom_call" | custom-call | flops 14763950080 | bytes 24379392 | tf_op jit(solution)/shard_map/expert_rows/pallas_call | solution.py:407
  297.5 4.3 fusion.6
  301.8 3.8 add_convert_fusion.1.left
  305.6 4.9 add_and_join.1
  310.5 5.1 convolution_convert_fusion.2
  315.7 4.8 all-to-all-start.2
  320.8 15.7 %shared_rows.1 = (bf16[512,704]{1,0:T(8,128)(2,1)}, bf16[512,704]{1,0:T(8,128)(2,1)}, bf16[512,704]{1,0:T(8,128)(2,1)}, bf16[512,2048]{1,0:T(8,128)(2,1)}, bf16[512,2048]{1,0:T(8,128)(2,1)}) custom-call(bf16[512,2048]{1,0:T(8,128)(2,1)} %copy-done, bf16[512,2048]{1,0:T(8,128)(2,1)} %copy-done.67, bf16[32,3,64,704]{3,2,1,0:T(8,128)(2,1)} %bitcast.338), custom_call_target="tpu_custom_call" | custom-call | flops 8858370048 | bytes 17039360 | tf_op jit(solution)/shard_map/shared_rows/pallas_call | solution.py:535
  339.9 9.4 %shared_grads.1 = bf16[32,3,64,704]{3,2,1,0:T(8,128)(2,1)} custom-call(bf16[512,2048]{1,0:T(8,128)(2,1)S(1)} %copy-done.1, bf16[512,2048]{1,0:T(8,128)(2,1)} %copy-done.67, bf16[512,704]{1,0:T(8,128)(2,1)S(1)} %copy-done.35, bf16[512,704]{1,0:T(8,128)(2,1)S(1)} %copy-done.36, bf16[512,704]{1,0:T(8,128)(2,1)S(1)} %copy-done.37), custom_call_target="tpu_custom_call" | custom-call | flops 4429185024 | bytes 12845056 | tf_op jit(solution)/shard_map/shared_grads/pallas_call | solution.py:567
  349.4 6.5 %add_convert_fusion = bf16[1280,1024]{1,0:T(8,128)(2,1)} fusion(bf16[1280,1024]{1,0:T(8,128)(2,1)} %collective-permute-done.26, bf16[1280,704]{1,0:T(8,128)(2,1)} %get-tuple-element.91.scaled, bf16[704,2048]{1,0:T(8,128)(2,1)} %bitcast.348, s32[]{:T(128)S(6)} %select_n.135), kind=kOutput, calls=%fused_computation.3 | convolution fusion | flops 1849425920 | bytes 8650756 | tf_op jit(solution)/shard_map/dot_general | solution.py:36
  356.0 4.0 all-to-all-done.2
  368.9 3.8 combine.4
  375.3 13.9 %collective-permute-done.28 = bf16[128,2048]{1,0:T(8,128)(2,1)} collective-permute-done((bf16[128,2048]{1,0:T(8,128)(2,1)}, bf16[128,2048]{1,0:T(8,128)(2,1)}, u32[]{:S(2)}, u32[]{:S(2)}) %collective-permute-start.28) | collective-permute-done | bytes 524320 | tf_op jit(solution)/shard_map/ppermute | solution.py:79
  399.0 8.2 %collective-permute-done.29 = bf16[128,2048]{1,0:T(8,128)(2,1)S(1)} collective-permute-done((bf16[128,2048]{1,0:T(8,128)(2,1)S(1)}, bf16[128,2048]{1,0:T(8,128)(2,1)S(1)}, u32[]{:S(2)}, u32[]{:S(2)}) %collective-permute-start.29) | collective-permute-done | bytes 524320 | tf_op jit(solution)/shard_map/ppermute | solution.py:79
  411.8 7.9 %all-to-all-start.3 = ((bf16[32,40,1024]{2,1,0:T(8,128)(2,1)}), bf16[32,40,1024]{2,1,0:T(8,128)(2,1)}, u32[]{:S(2)}, u32[]{:S(2)}) async-start(bf16[32,40,1024]{2,1,0:T(8,128)(2,1)} %bitcast.278), calls=%async_computation.3 | async-start | bytes 5242880 | tf_op jit(solution)/shard_map/all_to_all | solution.py:100
  422.7 6.0 %attend_back.1 = bf16[512,768]{1,0:T(8,128)(2,1)S(1)} custom-call(s32[3]{0:T(128)S(1)} %pad_add_fusion.2.where, bf16[512,768]{1,0:T(8,128)(2,1)S(1)} %copy-done.9, bf16[512,768]{1,0:T(8,128)(2,1)S(1)} %copy-done.9, bf16[512,768]{1,0:T(8,128)(2,1)S(1)} %copy-done.9, bf16[512,512]{1,0:T(8,128)(2,1)S(1)} %convolution_convert_fusion.8.g_ref), custom_call_target="tpu_custom_call" | custom-call | flops 1342177280 | bytes 1572864 | tf_op jit(solution)/shard_map/attend_back/pallas_call | solution.py:327
  452.8 20.9 %expert_grads.1 = (f32[704,2048]{1,0:T(8,128)}, f32[704,2048]{1,0:T(8,128)}, f32[704,2048]{1,0:T(8,128)}) custom-call(s32[1]{0:T(128)} %bitcast.41.core, bf16[1280,1152]{1,0:T(8,128)(2,1)} %bitcast.45.rows_own.gate_lanes, bf16[1280,1152]{1,0:T(8,128)(2,1)} %collective-permute-done.23.rows_far, bf16[1280,1024]{1,0:T(8,128)(2,1)} %bitcast.40.grads_own, ...), custom_call_target="tpu_custom_call" | custom-call | flops 11072962560 | bytes 33030144 | tf_op jit(solution)/shard_map/expert_grads/pallas_call | solution.py:601
  483.8 13.9 %collective-permute-done.35 = bf16[1,2,4,32,1408]{4,3,1,2,0:T(8,128)(2,1)} collective-permute-done((bf16[1,2,4,32,1408]{4,3,1,2,0:T(8,128)(2,1)}, bf16[1,2,4,32,1408]{4,3,1,2,0:T(8,128)(2,1)}, u32[]{:S(2)}, u32[]{:S(2)}) %collective-permute-start.35) | collective-permute-done | bytes 720928 | tf_op jit(solution)/shard_map/ppermute | solution.py:75
  506.2 10.0 %collective-permute-done.38 = bf16[1,4,2,32,1408]{4,3,2,1,0:T(8,128)(2,1)} collective-permute-done((bf16[1,4,2,32,1408]{4,3,2,1,0:T(8,128)(2,1)}, bf16[1,4,2,32,1408]{4,3,2,1,0:T(8,128)(2,1)}, u32[]{:S(2)}, u32[]{:S(2)}) %collective-permute-start.38) | collective-permute-done | bytes 720928 | tf_op jit(solution)/shard_map/ppermute | solution.py:75
  543.3 5.2 collective-permute-done.44
  567.1 11.0 %collective-permute-done.32 = bf16[128,2048]{1,0:T(8,128)(2,1)S(1)} collective-permute-done((bf16[128,2048]{1,0:T(8,128)(2,1)S(1)}, bf16[128,2048]{1,0:T(8,128)(2,1)S(1)}, u32[]{:S(2)}, u32[]{:S(2)}) %collective-permute-start.32) | collective-permute-done | bytes 524320 | tf_op jit(solution)/shard_map/ppermute | solution.py:79
  (433 shorter events, 232.5 us)
Async XLA Ops:
  34.4 16.4 %collective-permute-start.8 = (bf16[4,2,1,32,1408]{4,3,1,2,0:T(8,128)(2,1)S(1)}, bf16[4,2,1,32,1408]{4,3,1,2,0:T(8,128)(2,1)S(1)}, u32[]{:S(2)}, u32[]{:S(2)}) collective-permute-start(bf16[4,2,1,32,1408]{4,3,1,2,0:T(8,128)(2,1)S(1)} %pad_maximum_fusion.9), channel_id=1, source_target_pairs={{0,32},{4,36},{8,40},{12,44},{16,48},{20,52},{24,56},{28,60},{32,0... | collective-permute-start | bytes 2162696 | tf_op jit(solution)/shard_map/ppermute | solution.py:75
  34.8 17.2 %collective-permute-start.9 = (bf16[4,2,1,32,1408]{4,3,1,2,0:T(8,128)(2,1)S(1)}, bf16[4,2,1,32,1408]{4,3,1,2,0:T(8,128)(2,1)S(1)}, u32[]{:S(2)}, u32[]{:S(2)}) collective-permute-start(bf16[4,2,1,32,1408]{4,3,1,2,0:T(8,128)(2,1)S(1)} %pad_maximum_fusion.9), channel_id=1, source_target_pairs={{0,96},{4,100},{8,104},{12,108},{16,112},{20,116},{24,120},{28,124... | collective-permute-start | bytes 2162696 | tf_op jit(solution)/shard_map/ppermute | solution.py:75
  37.1 15.2 %collective-permute-start.10 = (bf16[4,2,1,32,1408]{4,3,2,1,0:T(8,128)(2,1)S(1)}, bf16[4,2,1,32,1408]{4,3,2,1,0:T(8,128)(2,1)}, u32[]{:S(2)}, u32[]{:S(2)}) collective-permute-start(bf16[4,2,1,32,1408]{4,3,2,1,0:T(8,128)(2,1)S(1)} %pad_maximum_fusion.10.refs_5_), channel_id=1, source_target_pairs={{0,4},{4,0},{8,12},{12,8},{16,20},{20,16},{24,28},{28,24},{32,36},... | collective-permute-start | bytes 2162696 | tf_op jit(solution)/shard_map/ppermute | solution.py:75
  37.1 17.8 %collective-permute-start.11 = (bf16[4,2,1,32,1408]{4,3,2,1,0:T(8,128)(2,1)S(1)}, bf16[4,2,1,32,1408]{4,3,2,1,0:T(8,128)(2,1)}, u32[]{:S(2)}, u32[]{:S(2)}) collective-permute-start(bf16[4,2,1,32,1408]{4,3,2,1,0:T(8,128)(2,1)S(1)} %pad_maximum_fusion.10.refs_5_), channel_id=1, source_target_pairs={{0,12},{4,8},{8,4},{12,0},{16,28},{20,24},{24,20},{28,16},{32,44},... | collective-permute-start | bytes 2162696 | tf_op jit(solution)/shard_map/ppermute | solution.py:75
  40.8 14.1 %collective-permute-start.17 = (bf16[128,2048]{1,0:T(8,128)(2,1)S(1)}, bf16[128,2048]{1,0:T(8,128)(2,1)}, u32[]{:S(2)}, u32[]{:S(2)}) collective-permute-start(bf16[128,2048]{1,0:T(8,128)(2,1)S(1)} %copy-done.45), channel_id=1, source_target_pairs={{0,2},{1,3},{2,0},{3,1},{4,6},{5,7},{6,4},{7,5},{8,10},{9,11},{10,... | collective-permute-start | bytes 1572872 | tf_op jit(solution)/shard_map/ppermute | solution.py:79
  50.8 18.4 %collective-permute-start = (bf16[128,2048]{1,0:T(8,128)(2,1)}, bf16[128,2048]{1,0:T(8,128)(2,1)}, u32[]{:S(2)}, u32[]{:S(2)}) collective-permute-start(bf16[128,2048]{1,0:T(8,128)(2,1)} %param.17), channel_id=1, source_target_pairs={{0,2},{1,3},{2,0},{3,1},{4,6},{5,7},{6,4},{7,5},{8,10},{9,11},{10,... | collective-permute-start | bytes 1572872 | tf_op jit(solution)/shard_map/ppermute | solution.py:79
  57.0 33.5 %collective-permute-start.18 = (bf16[256,2048]{1,0:T(8,128)(2,1)}, bf16[256,2048]{1,0:T(8,128)(2,1)}, u32[]{:S(2)}, u32[]{:S(2)}) collective-permute-start(bf16[256,2048]{1,0:T(8,128)(2,1)} %pad_maximum_fusion.4), channel_id=1, source_target_pairs={{0,1},{1,0},{2,3},{3,2},{4,5},{5,4},{6,7},{7,6},{8,9},{9,8},{10,11... | collective-permute-start | bytes 3145736 | tf_op jit(solution)/shard_map/ppermute | solution.py:79
  66.2 11.8 %collective-permute-start.14 = (bf16[2,2,1,32,1408]{4,3,1,2,0:T(8,128)(2,1)}, bf16[2,2,1,32,1408]{4,3,1,2,0:T(8,128)(2,1)S(1)}, u32[]{:S(2)}, u32[]{:S(2)}) collective-permute-start(bf16[2,2,1,32,1408]{4,3,1,2,0:T(8,128)(2,1)} %slice.206), channel_id=1, source_target_pairs={{0,32},{4,36},{8,40},{12,44},{16,48},{20,52},{24,56},{28,60},{32,0... | collective-permute-start | bytes 1081352 | tf_op jit(solution)/shard_map/ppermute | solution.py:75
  66.6 12.1 %collective-permute-start.15 = (bf16[2,2,1,32,1408]{4,3,2,1,0:T(8,128)(2,1)S(1)}, bf16[2,2,1,32,1408]{4,3,2,1,0:T(8,128)(2,1)S(1)}, u32[]{:S(2)}, u32[]{:S(2)}) collective-permute-start(bf16[2,2,1,32,1408]{4,3,2,1,0:T(8,128)(2,1)S(1)} %slice.207), channel_id=1, source_target_pairs={{0,12},{4,8},{8,4},{12,0},{16,28},{20,24},{24,20},{28,16},{32,44},... | collective-permute-start | bytes 1081352 | tf_op jit(solution)/shard_map/ppermute | solution.py:75
  96.3 41.2 %all-to-all-start = ((bf16[32,40,1024]{2,1,0:T(8,128)(2,1)}), bf16[32,40,1024]{2,1,0:T(8,128)(2,1)}, u32[]{:S(2)}, u32[]{:S(2)}) async-start(bf16[32,40,1024]{2,1,0:T(8,128)(2,1)} %bitcast.279), calls=%async_computation | async-start | bytes 5242880 | tf_op jit(solution)/shard_map/all_to_all | solution.py:100
  104.5 216.4 %all-gather.2.cloned.1.call-start = ((), (), s32[]{:S(2)}) async-start(), calls=%async_computation.7 | async-start | bytes 9732096 | tf_op jit(solution)/shard_map/all_gather | solution.py:708
  145.3 15.4 %collective-permute-start.20 = (bf16[128,2048]{1,0:T(8,128)(2,1)S(1)}, bf16[128,2048]{1,0:T(8,128)(2,1)S(1)}, u32[]{:S(2)}, u32[]{:S(2)}) collective-permute-start(bf16[128,2048]{1,0:T(8,128)(2,1)S(1)} %slice.392), channel_id=1, source_target_pairs={{0,2},{1,3},{2,0},{3,1},{4,6},{5,7},{6,4},{7,5},{8,10},{9,11},{10,... | collective-permute-start | bytes 1572872 | tf_op jit(solution)/shard_map/ppermute | solution.py:79
  162.3 12.4 %collective-permute-start.21 = (bf16[128,2048]{1,0:T(8,128)(2,1)S(1)}, bf16[128,2048]{1,0:T(8,128)(2,1)S(1)}, u32[]{:S(2)}, u32[]{:S(2)}) collective-permute-start(bf16[128,2048]{1,0:T(8,128)(2,1)S(1)} %multiply_convert_fusion.1), channel_id=1, source_target_pairs={{0,2},{1,3},{2,0},{3,1},{4,6},{5,7},{6,4},{7,5},{8,10},{9,11},{10,... | collective-permute-start | bytes 1572872 | tf_op jit(solution)/shard_map/ppermute | solution.py:79
  255.8 12.9 %collective-permute-start.23 = (bf16[1280,1152]{1,0:T(8,128)(2,1)}, bf16[1280,1152]{1,0:T(8,128)(2,1)}, u32[]{:S(2)}, u32[]{:S(2)}) collective-permute-start(bf16[1280,1152]{1,0:T(8,128)(2,1)} %bitcast.45.rows_own.gate_lanes), channel_id=1, source_target_pairs={{0,1},{1,0},{2,3},{3,2},{4,5},{5,4},{6,7},{7,6},{8,9},{9,8},{10,11... | collective-permute-start | bytes 8847368 | tf_op jit(solution)/shard_map/ppermute | solution.py:79
  315.6 33.8 %collective-permute-start.26 = (bf16[1280,1024]{1,0:T(8,128)(2,1)}, bf16[1280,1024]{1,0:T(8,128)(2,1)}, u32[]{:S(2)}, u32[]{:S(2)}) collective-permute-start(bf16[1280,1024]{1,0:T(8,128)(2,1)} %convolution_convert_fusion.2), channel_id=1, source_target_pairs={{0,1},{1,0},{2,3},{3,2},{4,5},{5,4},{6,7},{7,6},{8,9},{9,8},{10,11... | collective-permute-start | bytes 7864328 | tf_op jit(solution)/shard_map/ppermute | solution.py:79
  315.7 44.2 %all-to-all-start.2 = ((bf16[32,40,1152]{2,1,0:T(8,128)(2,1)}), bf16[32,40,1152]{2,1,0:T(8,128)(2,1)}, u32[]{:S(2)}, u32[]{:S(2)}) async-start(bf16[32,40,1152]{2,1,0:T(8,128)(2,1)} %bitcast.272), calls=%async_computation.2 | async-start | bytes 5898240 | tf_op jit(solution)/shard_map/all_to_all | solution.py:100
  320.6 185.5 %reduce-scatter.4.cloned.1.call-start = ((), (), s32[]{:S(2)}) async-start(), calls=%async_computation.8 | async-start | bytes 11796480 | tf_op jit(solution)/shard_map/reduce_scatter | solution.py:114
  375.2 13.9 %collective-permute-start.28 = (bf16[128,2048]{1,0:T(8,128)(2,1)}, bf16[128,2048]{1,0:T(8,128)(2,1)}, u32[]{:S(2)}, u32[]{:S(2)}) collective-permute-start(bf16[128,2048]{1,0:T(8,128)(2,1)} %slice.391), channel_id=1, source_target_pairs={{0,2},{1,3},{2,0},{3,1},{4,6},{5,7},{6,4},{7,5},{8,10},{9,11},{10,... | collective-permute-start | bytes 1572872 | tf_op jit(solution)/shard_map/ppermute | solution.py:79
  394.3 12.9 %collective-permute-start.29 = (bf16[128,2048]{1,0:T(8,128)(2,1)S(1)}, bf16[128,2048]{1,0:T(8,128)(2,1)S(1)}, u32[]{:S(2)}, u32[]{:S(2)}) collective-permute-start(bf16[128,2048]{1,0:T(8,128)(2,1)S(1)} %get-tuple-element.102), channel_id=1, source_target_pairs={{0,2},{1,3},{2,0},{3,1},{4,6},{5,7},{6,4},{7,5},{8,10},{9,11},{10,... | collective-permute-start | bytes 1572872 | tf_op jit(solution)/shard_map/ppermute | solution.py:79
  411.8 107.5 %all-to-all-start.3 = ((bf16[32,40,1024]{2,1,0:T(8,128)(2,1)}), bf16[32,40,1024]{2,1,0:T(8,128)(2,1)}, u32[]{:S(2)}, u32[]{:S(2)}) async-start(bf16[32,40,1024]{2,1,0:T(8,128)(2,1)} %bitcast.278), calls=%async_computation.3 | async-start | bytes 5242880 | tf_op jit(solution)/shard_map/all_to_all | solution.py:100
  419.7 136.1 %reduce-scatter.6.cloned.1.call-start = ((), (), s32[]{:S(2)}) async-start(), calls=%async_computation.9 | async-start | bytes 3538944 | tf_op jit(solution)/shard_map/reduce_scatter | solution.py:114
  430.8 69.6 %collective-permute-start.33 = (bf16[256,2048]{1,0:T(8,128)(2,1)}, bf16[256,2048]{1,0:T(8,128)(2,1)}, u32[]{:S(2)}, u32[]{:S(2)}) collective-permute-start(bf16[256,2048]{1,0:T(8,128)(2,1)} %convolution_convert_fusion.6), channel_id=1, source_target_pairs={{0,1},{1,0},{2,3},{3,2},{4,5},{5,4},{6,7},{7,6},{8,9},{9,8},{10,11... | collective-permute-start | bytes 3145736 | tf_op jit(solution)/shard_map/ppermute | solution.py:79
  440.6 40.3 %collective-permute-start.37 = (bf16[1,2,4,32,1408]{4,3,1,2,0:T(8,128)(2,1)}, bf16[1,2,4,32,1408]{4,3,1,2,0:T(8,128)(2,1)}, u32[]{:S(2)}, u32[]{:S(2)}) collective-permute-start(bf16[1,2,4,32,1408]{4,3,1,2,0:T(8,128)(2,1)} %pad_maximum_fusion.13), channel_id=1, source_target_pairs={{0,96},{4,100},{8,104},{12,108},{16,112},{20,116},{24,120},{28,124... | collective-permute-start | bytes 2162696 | tf_op jit(solution)/shard_map/ppermute | solution.py:75
  444.5 39.3 %collective-permute-start.36 = (bf16[1,2,4,32,1408]{4,3,1,2,0:T(8,128)(2,1)}, bf16[1,2,4,32,1408]{4,3,1,2,0:T(8,128)(2,1)}, u32[]{:S(2)}, u32[]{:S(2)}) collective-permute-start(bf16[1,2,4,32,1408]{4,3,1,2,0:T(8,128)(2,1)} %pad_maximum_fusion.12), channel_id=1, source_target_pairs={{0,64},{4,68},{8,72},{12,76},{16,80},{20,84},{24,88},{28,92},{32,9... | collective-permute-start | bytes 2162696 | tf_op jit(solution)/shard_map/ppermute | solution.py:75
  446.6 51.1 %collective-permute-start.35 = (bf16[1,2,4,32,1408]{4,3,1,2,0:T(8,128)(2,1)}, bf16[1,2,4,32,1408]{4,3,1,2,0:T(8,128)(2,1)}, u32[]{:S(2)}, u32[]{:S(2)}) collective-permute-start(bf16[1,2,4,32,1408]{4,3,1,2,0:T(8,128)(2,1)} %pad_maximum_fusion.11), channel_id=1, source_target_pairs={{0,32},{4,36},{8,40},{12,44},{16,48},{20,52},{24,56},{28,60},{32,6... | collective-permute-start | bytes 2162696 | tf_op jit(solution)/shard_map/ppermute | solution.py:75
  448.7 57.5 %collective-permute-start.40 = (bf16[1,4,2,32,1408]{4,3,2,1,0:T(8,128)(2,1)}, bf16[1,4,2,32,1408]{4,3,2,1,0:T(8,128)(2,1)}, u32[]{:S(2)}, u32[]{:S(2)}) collective-permute-start(bf16[1,4,2,32,1408]{4,3,2,1,0:T(8,128)(2,1)} %pad_maximum_fusion.16), channel_id=1, source_target_pairs={{0,12},{4,0},{8,4},{12,8},{16,28},{20,16},{24,20},{28,24},{32,44},... | collective-permute-start | bytes 2162696 | tf_op jit(solution)/shard_map/ppermute | solution.py:75
  480.9 25.3 %collective-permute-start.39 = (bf16[1,4,2,32,1408]{4,3,2,1,0:T(8,128)(2,1)}, bf16[1,4,2,32,1408]{4,3,2,1,0:T(8,128)(2,1)}, u32[]{:S(2)}, u32[]{:S(2)}) collective-permute-start(bf16[1,4,2,32,1408]{4,3,2,1,0:T(8,128)(2,1)} %pad_maximum_fusion.15), channel_id=1, source_target_pairs={{0,8},{4,12},{8,0},{12,4},{16,24},{20,28},{24,16},{28,20},{32,40},... | collective-permute-start | bytes 2162696 | tf_op jit(solution)/shard_map/ppermute | solution.py:75
  483.8 32.5 %collective-permute-start.38 = (bf16[1,4,2,32,1408]{4,3,2,1,0:T(8,128)(2,1)}, bf16[1,4,2,32,1408]{4,3,2,1,0:T(8,128)(2,1)}, u32[]{:S(2)}, u32[]{:S(2)}) collective-permute-start(bf16[1,4,2,32,1408]{4,3,2,1,0:T(8,128)(2,1)} %pad_maximum_fusion.14), channel_id=1, source_target_pairs={{0,4},{4,8},{8,12},{12,0},{16,20},{20,24},{24,28},{28,16},{32,36},... | collective-permute-start | bytes 2162696 | tf_op jit(solution)/shard_map/ppermute | solution.py:75
  504.9 21.4 %collective-permute-start.34 = (bf16[128,2048]{1,0:T(8,128)(2,1)}, bf16[128,2048]{1,0:T(8,128)(2,1)}, u32[]{:S(2)}, u32[]{:S(2)}) collective-permute-start(bf16[128,2048]{1,0:T(8,128)(2,1)} %slice.389), channel_id=1, source_target_pairs={{0,2},{1,3},{2,0},{3,1},{4,6},{5,7},{6,4},{7,5},{8,10},{9,11},{10,... | collective-permute-start | bytes 1572872 | tf_op jit(solution)/shard_map/ppermute | solution.py:79
  506.2 72.9 %reduce-scatter.8.cloned.1.call-start = ((), (), s32[]{:S(2)}) async-start(), calls=%async_computation.10 | async-start | bytes 1474560 | tf_op jit(solution)/shard_map/reduce_scatter | solution.py:114
  522.9 38.6 %collective-permute-start.31 = (bf16[256,2048]{1,0:T(8,128)(2,1)}, bf16[256,2048]{1,0:T(8,128)(2,1)}, u32[]{:S(2)}, u32[]{:S(2)}) collective-permute-start(bf16[256,2048]{1,0:T(8,128)(2,1)} %combine.7), channel_id=1, source_target_pairs={{0,1},{1,0},{2,3},{3,2},{4,5},{5,4},{6,7},{7,6},{8,9},{9,8},{10,11... | collective-permute-start | bytes 3145736 | tf_op jit(solution)/shard_map/ppermute | solution.py:79
  564.7 13.3 %collective-permute-start.32 = (bf16[128,2048]{1,0:T(8,128)(2,1)S(1)}, bf16[128,2048]{1,0:T(8,128)(2,1)S(1)}, u32[]{:S(2)}, u32[]{:S(2)}) collective-permute-start(bf16[128,2048]{1,0:T(8,128)(2,1)S(1)} %slice.390), channel_id=1, source_target_pairs={{0,2},{1,3},{2,0},{3,1},{4,6},{5,7},{6,4},{7,5},{8,10},{9,11},{10,... | collective-permute-start | bytes 1572872 | tf_op jit(solution)/shard_map/ppermute | solution.py:79
  (113 other events, 824.2 us)
Sparse Core Ops, SparseCore 0:
  142.4 136.2 all-gather.1
  349.5 145.9 reduce-scatter.3
  506.3 41.4 reduce-scatter.5
  555.9 22.3 reduce-scatter.7

commit v3 on v2

--- a/solution.py
+++ b/solution.py
@@ -57,10 +57,6 @@
     return lax.optimization_barrier((value, *earlier))[0]
 
 
-def move_fsdp(values, dz, dx, dy):
-    return route_fsdp(values, lambda z, x, y: ((z + dz) % NZ, (x + dx) % NX, (y + dy) % NY))
-
-
 def swap_along(values, fz, fx, fy):
     return route_fsdp(values, lambda z, x, y: (z ^ fz, x ^ fx, y ^ fy))
 
@@ -84,8 +80,11 @@
     return jnp.concatenate([pair, move_tp(pair, 1)], axis=0)
 
 
-def scatter_tp(near_part, far_part):
-    summed = near_part + move_tp(far_part.astype(bf16), 1).astype(f32)
+def sum_cores(near_part, far_part):
+    return near_part + move_tp(far_part.astype(bf16), 1).astype(f32)
+
+
+def sum_chips(summed):
     rows = summed.shape[0] // 2
     return summed[:rows] + move_tp(summed[rows:].astype(bf16), 2).astype(f32)
 
@@ -100,48 +99,43 @@
     return lax.all_to_all(blocks, "fsdp", split_axis=0, concat_axis=0, tiled=True).reshape(shape)
 
 
-def along(axis):
-    grid = [[[(z * NX + x) * NY + y for y in range(NY)] for x in range(NX)] for z in range(NZ)]
-    if axis == "z":
-        return [[grid[z][x][y] for z in range(NZ)] for x in range(NX) for y in range(NY)]
-    if axis == "x":
-        return [[grid[z][x][y] for x in range(NX)] for z in range(NZ) for y in range(NY)]
-    return [list(grid[z][x]) for z in range(NZ) for x in range(NX)]
-
-
-def staged_sum(values):
-    for axis in "zxy":
-        values = lax.psum_scatter(
-            values, "fsdp", scatter_dimension=0, tiled=True, axis_index_groups=along(axis)
-        )
-    return values
+def sum_along_z(values):
+    lines = [[z * NX * NY + i for z in range(NZ)] for i in range(NX * NY)]
+    return lax.psum_scatter(
+        values, "fsdp", scatter_dimension=0, tiled=True, axis_index_groups=lines
+    )
+
+
+def sum_across(values):
+    planes = [[z * NX * NY + i for i in range(NX * NY)] for z in range(NZ)]
+    parts = lax.all_to_all(
+        values, "fsdp", split_axis=0, concat_axis=0, tiled=True, axis_index_groups=planes
+    )
+    return jnp.sum(parts.astype(f32), axis=0)
 
 
 def place_kernel(cuts, spot, *refs):
-    first, second, outs = refs[:5], refs[5:10], refs[10:]
+    pieces, outs, held, sems = refs[:10], refs[10 : 10 + len(cuts)], refs[-11:-1], refs[-1]
     z, x, y = spot[0], spot[1], spot[2]
-    half = first[0].shape[3]
-
-    def part(pieces, across, along_line, xr, item, columns):
-        if across == 2:
-            across += along_line // 2
-            along_line %= 2
-        elif across == 3:
-            across = 4
-        return pieces[across][along_line, xr, item, :, columns]
-
-    for zr in range(NZ):
-        for xr in range(NX):
-            for yr in range(NY):
+    half = pieces[0].shape[3]
+    copies = [pltpu.make_async_copy(pieces[i], held[i], sems.at[i]) for i in range(10)]
+    for copy in copies:
+        copy.start()
+    for number in range(10):
+        copies[number].wait()
+        lines, across = divmod(number, 5)
+        opposite = across in (2, 3)
+        for place in range(held[number].shape[0]):
+            along_line = place + 2 * (across == 3)
+            step = 2 if opposite else (0, 1, 2, 2, 3)[across]
+            zr, yr = (step, along_line) if lines == 0 else (along_line, step)
+            rows = slice(lines * half, (lines + 1) * half)
+            for xr in range(NX):
                 at = (jnp.bitwise_xor(z, zr), jnp.bitwise_xor(x, xr), jnp.bitwise_xor(y, yr))
-                for number, (item, start, width) in enumerate(cuts):
-                    columns = slice(start, start + width)
-                    outs[number][at[0], at[1], at[2], :half] = part(
-                        first, zr, yr, xr, item, columns
-                    )
-                    outs[number][at[0], at[1], at[2], half:] = part(
-                        second, yr, zr, xr, item, columns
-                    )
+                for out, (item, start, width) in zip(outs, cuts):
+                    out[at[0], at[1], at[2], rows] = held[number][
+                        place, xr, item, :, start : start + width
+                    ]
 
 
 def gather_pair(stacked):
@@ -179,9 +173,11 @@
         functools.partial(place_kernel, cuts),
         out_shape=[jax.ShapeDtypeStruct((NZ, NX, NY, rows, width), bf16) for _, _, width in cuts],
         in_specs=[pl.BlockSpec(memory_space=pltpu.SMEM)]
-        + [pl.BlockSpec(memory_space=pltpu.VMEM)] * 10,
+        + [pl.BlockSpec(memory_space=pl.ANY)] * 10,
         out_specs=[pl.BlockSpec(memory_space=pltpu.VMEM)] * len(cuts),
-        compiler_params=pltpu.CompilerParams(vmem_limit_bytes=32 * 1024 * 1024),
+        scratch_shapes=[pltpu.VMEM(piece.shape, bf16) for piece in first + second]
+        + [pltpu.SemaphoreType.DMA((10,))],
+        compiler_params=pltpu.CompilerParams(vmem_limit_bytes=60 * 1024 * 1024),
         cost_estimate=pl.CostEstimate(
             flops=0, bytes_accessed=4 * total * sum(w for _, _, w in cuts), transcendentals=0
         ),
@@ -194,45 +190,51 @@
     return lax.dynamic_index_in_dim(values, index, axis, keepdims=False)
 
 
-def first_sum(cut, count, send):
-    total = cut(0).astype(f32)
-    for r in range(1, count):
-        total = total + send(cut(r), r).astype(f32)
+def add_up(own, received):
+    total = own.astype(f32)
+    for part in received:
+        total = total + part.astype(f32)
     return total.astype(bf16)
 
 
-def send_z(part, r):
-    return move_fsdp(part, r, 0, 0)
-
-
-def send_y(part, r):
-    return move_fsdp(part, 0, 0, r)
-
-
-def scatter_fsdp_one(join, grads, spot):
-    z, y = spot[0], spot[2]
-    rows = grads[0].shape[0] // FSDP
-    views = [g.reshape(NZ, NX, NY, 2, rows // 2, g.shape[1]) for g in grads]
-    joined = lambda parts: join([p[None] for p in parts])
-
-    one = first_sum(
-        lambda r: joined([pick(v, lax.rem(z + r, NZ), 0)[:, :, 0] for v in views]), NZ, send_z
-    )
-    two = first_sum(
-        lambda r: joined([pick(v, lax.rem(y + r, NY), 2)[:, :, 1] for v in views]), NY, send_y
-    )
-    return one, two
+def trade_pieces(pieces):
+    for_z, for_y = pieces
+    near = [swap_along(for_z[1], 1, 0, 0), swap_along(for_z[3], 3, 0, 0)]
+    across = [swap_along(for_y[1], 0, 0, 1), swap_along(for_y[3], 0, 0, 3)]
+    near.append(swap_along(for_z[2], 2, 0, 0))
+    across.append(swap_along(for_y[2], 0, 0, 2))
+    return near, across
+
+
+def add_pieces(own_z, own_y, received):
+    return lax.optimization_barrier((add_up(own_z, received[0]), add_up(own_y, received[1])))
+
+
+def write_pieces(spot, whole, item, for_z, for_y):
+    for r in range(NZ):
+        for_z[r][item] = whole[jnp.bitwise_xor(spot[0], r), :, :, 0]
+    for r in range(NY):
+        for_y[r][item] = whole[:, :, jnp.bitwise_xor(spot[2], r), 1]
+
+
+def piece_shapes(items, half, columns):
+    return [jax.ShapeDtypeStruct((items, NX, NY, half, columns), bf16)] * NZ + [
+        jax.ShapeDtypeStruct((items, NZ, NX, half, columns), bf16)
+    ] * NY
 
 
 def scatter_fsdp_two(parts, spot):
     z, x, y = spot[0], spot[1], spot[2]
-    one = first_sum(lambda r: pick(parts[0], lax.rem(y + r, NY), 2), NY, send_y)
-    two = first_sum(lambda r: pick(parts[1], lax.rem(z + r, NZ), 1), NZ, send_z)
-    one, two = lax.optimization_barrier((one, two))
+    halves = (
+        [pick(parts[0], jnp.bitwise_xor(y, r), 2) for r in range(NY)],
+        [pick(parts[1], jnp.bitwise_xor(z, r), 1) for r in range(NZ)],
+    )
+    in_z, in_y = trade_pieces((halves[1], halves[0]))
+    one, two = lax.optimization_barrier((add_up(halves[0][0], in_y), add_up(halves[1][0], in_z)))
 
     def last_sum(kept):
         mine, theirs = pick(kept, x, 1), pick(kept, 1 - x, 1)
-        return mine.astype(f32) + move_fsdp(theirs, 0, 1, 0).astype(f32)
+        return mine.astype(f32) + swap_along(theirs, 0, 1, 0).astype(f32)
 
     return jnp.concatenate([last_sum(one), last_sum(two)], axis=1)
 
@@ -578,6 +580,44 @@
         ),
         name="shared_grads",
     )(rows, grads, d_gate, d_up, hidden)
+
+
+def attention_grads_kernel(spot, d_att, attended, rows, logits, gains, gain_lane, h_attn, d_qkv, *refs):
+    for_z, for_y, whole = refs[:NZ], refs[NZ : NZ + NY], refs[-1]
+    wide = attended.shape[1]
+
+    def put(start, value):
+        shape = (*whole.shape[:-1], value.shape[1])
+        whole[..., start : start + value.shape[1]] = value.astype(bf16).reshape(shape)
+
+    put(0, contract_first(d_att[...], attended[...]))
+    put(wide, contract_first(rows[...], logits[...]) + contract_first(gains[...], gain_lane[...]))
+    put(wide + LANES, contract_first(h_attn[...], d_qkv[...]))
+    write_pieces(spot, whole, 0, for_z, for_y)
+
+
+def attention_grads(spot, *args):
+    d_att, attended, d_qkv = args[0], args[1], args[-1]
+    count, dim = d_att.shape
+    half = dim // FSDP // 2
+    width = attended.shape[1] + LANES + d_qkv.shape[1]
+    shapes = piece_shapes(1, half, width)
+    outs = pl.pallas_call(
+        attention_grads_kernel,
+        out_shape=shapes,
+        in_specs=[pl.BlockSpec(memory_space=pltpu.SMEM)]
+        + [pl.BlockSpec(memory_space=pltpu.VMEM)] * len(args),
+        out_specs=[pl.BlockSpec(memory_space=pltpu.VMEM)] * len(shapes),
+        scratch_shapes=[pltpu.VMEM((NZ, NX, NY, 2, half, width), bf16)],
+        compiler_params=pltpu.CompilerParams(vmem_limit_bytes=48 * 1024 * 1024),
+        cost_estimate=pl.CostEstimate(
+            flops=2 * count * dim * width,
+            bytes_accessed=2 * dim * width + 8 * count * dim,
+            transcendentals=0,
+        ),
+        name="attention_grads",
+    )(spot, *args)
+    return outs[:NZ], outs[NZ:]
 
 
 def expert_grads_kernel(core, rows_own, rows_far, grads_own, grads_far, d_gate, d_up, scaled, *outs):
@@ -684,14 +724,14 @@
         axis=1,
     )
     qkv_own = jnp.concatenate([query_matrix, key_matrix, value_matrix], axis=1)
-    lines = gather_lines(
-        gather_pair(jnp.concatenate([qkv_own, small_tile, w_out], axis=1)[None])
-    )
+    pair = gather_pair(jnp.concatenate([qkv_own, small_tile, w_out], axis=1)[None])
+    grad_other = move_tp(cotangent, 2)
+    *lines, grad_other = lax.optimization_barrier((*gather_lines(pair), grad_other))
+    grad_pair = jnp.concatenate([cotangent, grad_other], axis=0)
     near_lines = gather_near(lines)
+    grad_rows = jnp.concatenate([grad_pair, move_tp(grad_pair, 1)], axis=0)
     token_pair = jnp.concatenate([tokens, after(move_tp(tokens, 2), *near_lines)], axis=0)
     token_rows = jnp.concatenate([token_pair, move_tp(token_pair, 1)], axis=0)
-    grad_pair = jnp.concatenate([cotangent, after(move_tp(cotangent, 2), *near_lines)], axis=0)
-    grad_rows = jnp.concatenate([grad_pair, move_tp(grad_pair, 1)], axis=0)
     w_qkv, w_tile, w_out_all = gather_all(
         lines,
         near_lines,
@@ -706,7 +746,7 @@
     grads_own = swap_fsdp(after(slot_grads, w_tile))
     shared_own = jnp.concatenate([shared_gate, shared_up, shared_down], axis=0)
     w_shared = lax.all_gather(
-        after(shared_own, w_tile), "fsdp", axis=0, tiled=True
+        shared_own, "fsdp", axis=0, tiled=True
     ).reshape(FSDP, 3, own_rows, shared_gate.shape[1])
     lane = lax.broadcasted_iota(jnp.int32, (8, LANES), 1)
     gain_pick = (lane == experts + lax.broadcasted_iota(jnp.int32, (8, LANES), 0)).astype(bf16)
@@ -727,7 +767,7 @@
     qkv = matmul(h_attn, w_qkv).astype(bf16)
     attended = attend(where, qkv, heads)
     attn_far = after(contract_last(attended[near:], w_out_all).astype(bf16), grads_own)
-    attn_own = scatter_tp(contract_last(attended[:near], w_out_all), attn_far)
+    attn_own = sum_chips(sum_cores(contract_last(attended[:near], w_out_all), attn_far))
     own_tokens = tokens.astype(f32)
     middle = own_tokens + attn_own
     normed_two, factor_two = norm_rows(middle, gain_two)
@@ -747,6 +787,13 @@
     grads_far = move_tp(after(grads_own, slot_rows), 1)
     rows_own = swap_fsdp(slot_rows)
 
+    h_then = after(h_ffn, slot_rows)
+    s_d_gate, s_d_up, s_hidden, shared_out, shared_back = shared_rows(h_then, grad_rows, w_shared)
+    shared_parts = shared_grads(h_then, grad_rows, s_d_gate, s_d_up, s_hidden, own_rows)
+    shared_lines = sum_along_z(shared_parts)
+
+    rows_own = after(rows_own, shared_back, shared_parts)
+
     rows_far = move_tp(rows_own, 1)
     scal = jnp.stack([core.astype(jnp.int32), local_experts * fsdp_at.astype(jnp.int32)])
     d_gate, d_up, hidden, sent_far, dot_lanes = expert_rows(
@@ -757,12 +804,10 @@
     payload = add_and_join(sent_own, sent_far, dot_lanes)
     returned = swap_fsdp(payload)
 
-    h_then = after(h_ffn, payload)
-    s_d_gate, s_d_up, s_hidden, shared_out, shared_back = shared_rows(h_then, grad_rows, w_shared)
-    shared_parts = shared_grads(h_then, grad_rows, s_d_gate, s_d_up, s_hidden, own_rows)
-    shared_sums = staged_sum(shared_parts)[0].astype(f32)
-
     hidden_then = after(hidden, payload)
+    grad_egate, grad_eup, grad_edown = expert_grads(
+        core_vec, rows_own, rows_far, grads_own, grads_far, d_gate, d_up, hidden_then
+    )
     down_own = core_half(down_w)
     down_far = lax.dynamic_slice_in_dim(down_w, (1 - core) * half_dim, half_dim, 1)
     out_far = move_tp(matmul(hidden_then, down_far).astype(bf16), 1)
@@ -771,14 +816,14 @@
     def expert_layout(grads):
         return jnp.swapaxes(grads.reshape(local_experts, hidden_own, dim), 1, 2)
 
-    returned = after(returned, shared_back, shared_parts, out_own)
+    returned = after(returned, out_own, grad_egate)
     ffn_far, logits_far = combine(
         core_vec, 1, dispatch, returned, shared_back, bf16, gates, w_tile
     )
     ffn_near, logits_near = combine(
         core_vec, 0, dispatch, returned, shared_back, f32, gates, w_tile
     )
-    d_h_ffn = scatter_tp(ffn_near, ffn_far)
+    d_h_ffn = sum_chips(sum_cores(ffn_near, ffn_far))
     d_middle = cotangent.astype(f32) + norm_back(middle, factor_two, gain_two, d_h_ffn)
     lane_ids = lax.broadcasted_iota(jnp.int32, (1, LANES), 1)
     gain_terms = (d_h_ffn * middle * factor_two).astype(bf16)
@@ -787,27 +832,34 @@
     d_att_near = jnp.concatenate([d_att_own, move_tp(d_att_own, 2)], axis=0)
     out_back = swap_fsdp(after(out_own, d_att_near))
     d_att = jnp.concatenate([d_att_near, move_tp(d_att_near, 1)], axis=0)
-    grad_tile = (
-        contract_first(h_ffn, jnp.concatenate([logits_near, logits_far], axis=0))
-        + contract_first(gain_terms, gain_lane)
-    ).astype(bf16)
-    grad_wout = contract_first(d_att, attended).astype(bf16)
-    d_attended = matmul(d_att, w_out_all).astype(bf16)
+
+    d_attended = matmul(after(d_att, shared_lines), w_out_all).astype(bf16)
     d_qkv = attend_back(where, qkv, d_attended, heads)
-    grad_wqkv = contract_first(h_attn, d_qkv).astype(bf16)
-    sum_parts = scatter_fsdp_one(
-        lambda parts: jnp.concatenate(parts, axis=-1), [grad_wout, grad_tile, grad_wqkv], spot
-    )
-    attn_far = contract_last(d_qkv[near:], w_qkv).astype(bf16)
-    d_h_attn = scatter_tp(contract_last(d_qkv[:near], w_qkv), attn_far)
-    back_then = after(out_back, attn_far)
+    grad_pieces = attention_grads(
+        spot,
+        d_att,
+        attended,
+        h_ffn,
+        jnp.concatenate([logits_near, logits_far], axis=0),
+        gain_terms,
+        gain_lane,
+        h_attn,
+        d_qkv,
+    )
+    grad_received = trade_pieces(grad_pieces)
+    sum_parts = add_pieces(grad_pieces[0][0], grad_pieces[1][0], grad_received)
+    first_part = grad_received[0][0]
+    d_qkv_then = after(d_qkv, first_part)
+    attn_far = contract_last(d_qkv_then[near:], w_qkv).astype(bf16)
+    d_h_half = sum_cores(contract_last(d_qkv_then[:near], w_qkv), attn_far)
+    back_then = after(out_back, first_part)
     (out_far,) = combine(core_vec, 1, dispatch, back_then, shared_out, bf16)
     (out_near,) = combine(core_vec, 0, dispatch, back_then, shared_out, f32)
-    output = (middle + scatter_tp(out_near, out_far)).astype(bf16)
-    grad_egate, grad_eup, grad_edown = expert_grads(
-        core_vec, rows_own, rows_far, grads_own, grads_far, d_gate, d_up, after(hidden, grad_wqkv)
-    )
-    sum_parts = after(sum_parts, d_h_attn, out_near, grad_egate)
+    out_half = sum_cores(out_near, out_far)
+    shared_sums = sum_across(after(shared_lines, first_part))
+    sum_parts = lax.optimization_barrier((*sum_parts, d_h_half, out_half))[:2]
+    d_h_attn = sum_chips(d_h_half)
+    output = (middle + sum_chips(out_half)).astype(bf16)
     sums = scatter_fsdp_two(sum_parts, spot)[0]
     out_sums, tile_sums = sums[:, :q_width], small_sum_tp(sums[:, q_width : q_width + LANES])
     qkv_sums = sums[:, q_width + LANES :]

time: 598 us -> 562 us (0.940)
  blocking collectives: 68.1 us -> 0 us
  starting transfers between devices: 95.8 us -> 131 us
  waiting for transfers between devices: 153 us -> 184 us
  local copies, waits for them, and re-layouts: 53.9 us -> 29.5 us
  other arithmetic: 41.6 us -> 30.4 us
  Pallas kernels: 106 us -> 117 us
  matrix products: 53.9 us -> 44.5 us
    all_to_all x1 -> x0, blocking collectives: 68.1 us -> none  [swap_fsdp(): lax.all_to_all(blocks, 'fsdp', split_axis=0, concat_axis=0, tiled=True)]
    all_to_all x3 -> x4, waiting for transfers between devices: 14.5 us -> 42.7 us  [swap_fsdp(): lax.all_to_all(blocks, 'fsdp', split_axis=0, concat_axis=0, tiled=True)]
    unnamed x168 -> x126, local copies, waits for them, and re-layouts: 29.2 us -> 13.2 us
    all_to_all x3 -> x4, starting transfers between devices: 20.9 us -> 32.9 us  [swap_fsdp(): lax.all_to_all(blocks, 'fsdp', split_axis=0, concat_axis=0, tiled=True)]
    ppermute x29, waiting for transfers between devices: 67.9 us -> 78.9 us  [route_fsdp(): return lax.ppermute(values, 'fsdp', pairs)]
    ppermute x26, starting transfers between devices: 31 us -> 40.3 us  [move_tp(): return lax.ppermute(values, 'tp', [(i, i ^ flip) for i in range(TP)])]
    ppermute x26, waiting for transfers between devices: 70.9 us -> 62.8 us  [move_tp(): return lax.ppermute(values, 'tp', [(i, i ^ flip) for i in range(TP)])]
    pallas_call x0 -> x1, Pallas kernels: none -> 8.17 us  [attention_grads(): pl.pallas_call(attention_grads_kernel, out_shape=shapes, in_specs=[pl.Blo...]
  transfers between devices with their start and end apart: 62 -> 62, of which waited for: 26 -> 30; matrix products, arithmetic and copies ran while one was open for 19% -> 16% of each run, Pallas kernels for 18% -> 21%
where the time goes in v3:
time: 562 us; the launch traced here: 553 us
  waiting for transfers between devices  184 us (33%)
  starting transfers between devices  131 us (23%)
  Pallas kernels  117 us (21%)
  matrix products  44.5 us (8%)
  other arithmetic  30.4 us (5%)
  local copies, waits for them, and re-layouts  29.5 us (5%)
  between operations  15.3 us (3%)
    ppermute x29, waiting for transfers between devices, route_fsdp(): return lax.ppermute(values, 'fsdp', pairs)  78.9 us
    ppermute x26, waiting for transfers between devices, move_tp(): return lax.ppermute(values, 'tp', [(i, i ^ flip) for i in range(TP)])  62.8 us
    ppermute x29, starting transfers between devices, route_fsdp(): return lax.ppermute(values, 'fsdp', pairs)  50.7 us
    all_to_all x4, waiting for transfers between devices, swap_fsdp(): lax.all_to_all(blocks, 'fsdp', split_axis=0, concat_axis=0, tiled=True)  42.7 us
    ppermute x26, starting transfers between devices, move_tp(): return lax.ppermute(values, 'tp', [(i, i ^ flip) for i in range(TP)])  40.3 us
    all_to_all x4, starting transfers between devices, swap_fsdp(): lax.all_to_all(blocks, 'fsdp', split_axis=0, concat_axis=0, tiled=True)  32.9 us
    pallas_call x1, Pallas kernels, expert_rows(): pl.pallas_call(expert_rows_kernel, out_shape=[shape(hidden), shape(hidden...  28.4 us
    dot_general x8, matrix products, matmul(): return jnp.dot(left_op, right_op, preferred_element_type=f32)  27.5 us
  transfers between devices with their start and end apart: 62, of which 30 were waited for; matrix products, arithmetic and copies ran while one was open for 16% of the time, Pallas kernels for 21%

profile of v3, /device:TPU:1, one launch (start us, length us, event | category | flops | bytes accessed | tf_op | source)
XLA Modules:
  0.0 553.0 jit_solution(2678042361070233690)
XLA Ops:
  41.3 6.9 %collective-permute-start.18 = (bf16[256,2048]{1,0:T(8,128)(2,1)}, bf16[256,2048]{1,0:T(8,128)(2,1)}, u32[]{:S(2)}, u32[]{:S(2)}) collective-permute-start(bf16[256,2048]{1,0:T(8,128)(2,1)} %pad_maximum_fusion.4), channel_id=1, source_target_pairs={{0,1},{1,0},{2,3},{3,2},{4,5},{5,4},{6,7},{7,6},{8,9},{9,8},{10,11... | collective-permute-start | bytes 3145736 | tf_op jit(solution)/shard_map/ppermute | solution.py:75
  57.4 21.8 %collective-permute-done.9 = bf16[4,2,1,32,1408]{4,3,1,2,0:T(8,128)(2,1)} collective-permute-done((bf16[4,2,1,32,1408]{4,3,1,2,0:T(8,128)(2,1)}, bf16[4,2,1,32,1408]{4,3,1,2,0:T(8,128)(2,1)}, u32[]{:S(2)}, u32[]{:S(2)}) %collective-permute-start.9) | collective-permute-done | bytes 720928 | tf_op jit(solution)/shard_map/ppermute | solution.py:71
  93.9 5.5 collective-permute-done.17.refs_8_
  104.8 6.2 %place.1 = (bf16[4,2,4,64,768]{4,3,2,1,0:T(8,128)(2,1)}, bf16[4,2,4,64,128]{4,3,2,1,0:T(8,128)(2,1)}, bf16[4,2,4,64,512]{4,3,2,1,0:T(8,128)(2,1)}) custom-call(s32[3]{0:T(128)} %pad_add_fusion.3.spot, bf16[4,2,1,32,1408]{4,3,2,1,0:T(8,128)(2,1)} %bitcast.24.refs_0_, bf16[4,2,1,32,1408]{4,3,2,1,0:T(8,128)(2,1)} %bitcast.25.refs_1_, ...), custom_call_target="tpu_custom_call" | custom-call | bytes 11534336 | tf_op jit(solution)/shard_map/place/pallas_call | solution.py:172
  110.9 5.2 all-to-all-start
  124.6 4.9 attend.1.attended
  132.1 21.0 %all-to-all-done = bf16[32,40,1024]{2,1,0:T(8,128)(2,1)} async-done(((bf16[32,40,1024]{2,1,0:T(8,128)(2,1)}), bf16[32,40,1024]{2,1,0:T(8,128)(2,1)}, u32[]{:S(2)}, u32[]{:S(2)}) %all-to-all-start) | async-done | bytes 2621472 | tf_op jit(solution)/shard_map/all_to_all | solution.py:99
  163.0 11.7 %collective-permute-done.20 = bf16[128,2048]{1,0:T(8,128)(2,1)S(1)} collective-permute-done((bf16[128,2048]{1,0:T(8,128)(2,1)S(1)}, bf16[128,2048]{1,0:T(8,128)(2,1)S(1)}, u32[]{:S(2)}, u32[]{:S(2)}) %collective-permute-start.20) | collective-permute-done | bytes 524320 | tf_op jit(solution)/shard_map/ppermute | solution.py:75
  176.8 10.8 %collective-permute-done.21 = bf16[128,2048]{1,0:T(8,128)(2,1)S(1)} collective-permute-done((bf16[128,2048]{1,0:T(8,128)(2,1)S(1)}, bf16[128,2048]{1,0:T(8,128)(2,1)S(1)}, u32[]{:S(2)}, u32[]{:S(2)}) %collective-permute-start.21) | collective-permute-done | bytes 524320 | tf_op jit(solution)/shard_map/ppermute | solution.py:75
  202.3 12.4 %all-to-all-start.1 = ((bf16[32,40,1152]{2,1,0:T(8,128)(2,1)}), bf16[32,40,1152]{2,1,0:T(8,128)(2,1)}, u32[]{:S(2)}, u32[]{:S(2)}) async-start(bf16[32,40,1152]{2,1,0:T(8,128)(2,1)} %bitcast.142), calls=%async_computation.1 | async-start | bytes 5898240 | tf_op jit(solution)/shard_map/all_to_all | solution.py:99
  215.1 15.7 %shared_rows.1 = (bf16[512,704]{1,0:T(8,128)(2,1)}, bf16[512,704]{1,0:T(8,128)(2,1)}, bf16[512,704]{1,0:T(8,128)(2,1)}, bf16[512,2048]{1,0:T(8,128)(2,1)}, bf16[512,2048]{1,0:T(8,128)(2,1)}) custom-call(bf16[512,2048]{1,0:T(8,128)(2,1)} %copy-done.7, bf16[512,2048]{1,0:T(8,128)(2,1)} %copy-done.52, bf16[32,3,64,704]{3,2,1,0:T(8,128)(2,1)} %bitcast.181), custom_call_target="tpu_custom_call" | custom-call | flops 8858370048 | bytes 17039360 | tf_op jit(solution)/shard_map/shared_rows/pallas_call | solution.py:537
  234.2 9.1 %shared_grads.1 = bf16[32,3,64,704]{3,2,1,0:T(8,128)(2,1)} custom-call(bf16[512,2048]{1,0:T(8,128)(2,1)S(1)} %copy-done.8, bf16[512,2048]{1,0:T(8,128)(2,1)} %copy-done.52, bf16[512,704]{1,0:T(8,128)(2,1)S(1)} %copy-done.22, bf16[512,704]{1,0:T(8,128)(2,1)S(1)} %copy-done.23, bf16[512,704]{1,0:T(8,128)(2,1)S(1)} %copy-done.24), custom_call_target="tpu_custom_call" | custom-call | flops 4429185024 | bytes 12845056 | tf_op jit(solution)/shard_map/shared_grads/pallas_call | solution.py:569
  243.3 9.3 %all-to-all-done.1 = bf16[32,40,1152]{2,1,0:T(8,128)(2,1)} async-done(((bf16[32,40,1152]{2,1,0:T(8,128)(2,1)}), bf16[32,40,1152]{2,1,0:T(8,128)(2,1)}, u32[]{:S(2)}, u32[]{:S(2)}) %all-to-all-start.1) | async-done | bytes 2949152 | tf_op jit(solution)/shard_map/all_to_all | solution.py:99
  256.6 8.3 %collective-permute-done.24.grads_far = bf16[1280,1024]{1,0:T(8,128)(2,1)} collective-permute-done((bf16[1280,1024]{1,0:T(8,128)(2,1)}, bf16[1280,1024]{1,0:T(8,128)(2,1)}, u32[]{:S(2)}, u32[]{:S(2)}) %collective-permute-start.24) | collective-permute-done | bytes 2621472 | tf_op jit(solution)/shard_map/ppermute | solution.py:75
  265.0 28.4 %expert_rows.1 = (bf16[1280,704]{1,0:T(8,128)(2,1)}, bf16[1280,704]{1,0:T(8,128)(2,1)}, bf16[1280,704]{1,0:T(8,128)(2,1)}, bf16[1280,1024]{1,0:T(8,128)(2,1)}, bf16[1280,128]{1,0:T(8,128)(2,1)}) custom-call(s32[2]{0:T(128)} %pad_add_fusion.4.scal, bf16[1280,1152]{1,0:T(8,128)(2,1)} %bitcast.45.rows_own.gate_lanes, ...), custom_call_target="tpu_custom_call" | custom-call | flops 14763950080 | bytes 24379392 | tf_op jit(solution)/shard_map/expert_rows/pallas_call | solution.py:409
  301.9 5.0 add_and_join.1
  306.9 5.1 convolution_convert_fusion.2
  312.1 7.5 %all-to-all-start.2 = ((bf16[32,40,1152]{2,1,0:T(8,128)(2,1)}), bf16[32,40,1152]{2,1,0:T(8,128)(2,1)}, u32[]{:S(2)}, u32[]{:S(2)}) async-start(bf16[32,40,1152]{2,1,0:T(8,128)(2,1)} %bitcast.135), calls=%async_computation.2 | async-start | bytes 5898240 | tf_op jit(solution)/shard_map/all_to_all | solution.py:99
  319.6 21.1 %expert_grads.1 = (f32[704,2048]{1,0:T(8,128)}, f32[704,2048]{1,0:T(8,128)}, f32[704,2048]{1,0:T(8,128)}) custom-call(s32[1]{0:T(128)} %bitcast.41.core, bf16[1280,1152]{1,0:T(8,128)(2,1)} %bitcast.45.rows_own.gate_lanes, bf16[1280,1152]{1,0:T(8,128)(2,1)} %collective-permute-done.23.rows_far, bf16[1280,1024]{1,0:T(8,128)(2,1)} %bitcast.40.grads_own, ...), custom_call_target="tpu_custom_call" | custom-call | flops 11072962560 | bytes 33030144 | tf_op jit(solution)/shard_map/expert_grads/pallas_call | solution.py:641
  340.8 6.2 %add_convert_fusion = bf16[1280,1024]{1,0:T(8,128)(2,1)} fusion(bf16[1280,1024]{1,0:T(8,128)(2,1)} %collective-permute-done.26, bf16[1280,704]{1,0:T(8,128)(2,1)} %get-tuple-element.98.scaled, bf16[704,2048]{1,0:T(8,128)(2,1)S(1)} %bitcast.191, s32[]{:T(128)S(6)} %select_n.105), kind=kOutput, calls=%fused_computation.3 | convolution fusion | flops 1849425920 | bytes 8486916 | tf_op jit(solution)/shard_map/dot_general | solution.py:36
  347.0 12.5 %all-to-all-done.2 = bf16[32,40,1152]{2,1,0:T(8,128)(2,1)} async-done(((bf16[32,40,1152]{2,1,0:T(8,128)(2,1)}), bf16[32,40,1152]{2,1,0:T(8,128)(2,1)}, u32[]{:S(2)}, u32[]{:S(2)}) %all-to-all-start.2) | async-done | bytes 2949152 | tf_op jit(solution)/shard_map/all_to_all | solution.py:99
  371.6 12.9 %collective-permute-done.28 = bf16[128,2048]{1,0:T(8,128)(2,1)S(1)} collective-permute-done((bf16[128,2048]{1,0:T(8,128)(2,1)S(1)}, bf16[128,2048]{1,0:T(8,128)(2,1)S(1)}, u32[]{:S(2)}, u32[]{:S(2)}) %collective-permute-start.28) | collective-permute-done | bytes 524320 | tf_op jit(solution)/shard_map/ppermute | solution.py:75
  387.0 12.1 %collective-permute-done.29 = bf16[128,2048]{1,0:T(8,128)(2,1)S(1)} collective-permute-done((bf16[128,2048]{1,0:T(8,128)(2,1)S(1)}, bf16[128,2048]{1,0:T(8,128)(2,1)S(1)}, u32[]{:S(2)}, u32[]{:S(2)}) %collective-permute-start.29) | collective-permute-done | bytes 524320 | tf_op jit(solution)/shard_map/ppermute | solution.py:75
  401.8 7.9 %all-to-all-start.3 = ((bf16[32,40,1024]{2,1,0:T(8,128)(2,1)}), bf16[32,40,1024]{2,1,0:T(8,128)(2,1)}, u32[]{:S(2)}, u32[]{:S(2)}) async-start(bf16[32,40,1024]{2,1,0:T(8,128)(2,1)} %bitcast.143), calls=%async_computation.3 | async-start | bytes 5242880 | tf_op jit(solution)/shard_map/all_to_all | solution.py:99
  416.1 6.0 %attend_back.1.d_qkv = bf16[512,768]{1,0:T(8,128)(2,1)S(1)} custom-call(s32[3]{0:T(128)S(1)} %pad_add_fusion.2.where, bf16[512,768]{1,0:T(8,128)(2,1)S(1)} %copy-done.3, bf16[512,768]{1,0:T(8,128)(2,1)S(1)} %copy-done.3, bf16[512,768]{1,0:T(8,128)(2,1)S(1)} %copy-done.3, bf16[512,512]{1,0:T(8,128)(2,1)S(1)} %convolution_convert_fusion.6.g_ref), custom_call_target="tpu_custom_call" | custom-call | flops 1342177280 | bytes 1572864 | tf_op jit(solution)/shard_map/attend_back/pallas_call | solution.py:329
  423.1 8.2 %attention_grads.1 = (bf16[1,2,4,32,1408]{4,3,2,1,0:T(8,128)(2,1)S(1)}, bf16[1,2,4,32,1408]{4,3,2,1,0:T(8,128)(2,1)S(1)}, bf16[1,2,4,32,1408]{4,3,2,1,0:T(8,128)...) custom-call(s32[3]{0:T(128)S(1)} %copy-done.21, ...), custom_call_target="tpu_custom_call" | custom-call | flops 2952790016 | bytes 14155776 | tf_op jit(solution)/shard_map/attention_grads/pallas_call | solution.py:605
  440.1 17.1 %collective-permute-done.31 = bf16[1,2,4,32,1408]{4,3,1,2,0:T(8,128)(2,1)S(1)} collective-permute-done((bf16[1,2,4,32,1408]{4,3,1,2,0:T(8,128)(2,1)S(1)}, bf16[1,2,4,32,1408]{4,3,1,2,0:T(8,128)(2,1)S(1)}, u32[]{:S(2)}, u32[]{:S(2)}) %collective-permute-start.31) | collective-permute-done | bytes 720928 | tf_op jit(solution)/shard_map/ppermute | solution.py:71
  463.2 6.9 %all-to-all-start.4 = ((bf16[8,3,64,704]{3,2,1,0:T(8,128)(2,1)}), bf16[8,3,64,704]{3,2,1,0:T(8,128)(2,1)}, u32[]{:S(2)}, u32[]{:S(2)}) async-start(bf16[8,3,64,704]{3,2,1,0:T(8,128)(2,1)} %reduce-scatter.2.cloned.1.call-done), calls=%async_computation.5 | async-start | bytes 4718592 | tf_op jit(solution)/shard_map/all_to_all | solution.py:111
  486.2 11.4 %collective-permute-start.41 = (bf16[1,2,32,1408]{3,2,1,0:T(8,128)(2,1)S(1)}, bf16[1,2,32,1408]{3,2,1,0:T(8,128)(2,1)S(1)}, u32[]{:S(2)}, u32[]{:S(2)}) collective-permute-start(bf16[1,2,32,1408]{3,2,1,0:T(8,128)(2,1)S(1)} %get-tuple-element.139), channel_id=1, source_target_pairs={{0,4},{4,0},{8,12},{12,8},{16,20},{20,16},{24,28},{28,24},{32,36},... | collective-permute-start | bytes 540680 | tf_op jit(solution)/shard_map/ppermute | solution.py:71
  502.2 4.7 collective-permute-done.41
  511.5 4.8 collective-permute-done.46
  526.1 6.0 %collective-permute-start.51 = (f32[64]{0:T(128)S(1)}, f32[64]{0:T(128)S(1)}, u32[]{:S(2)}, u32[]{:S(2)}) collective-permute-start(f32[64]{0:T(128)S(1)} %fusion.40), channel_id=1, source_target_pairs={{0,3},{1,2},{2,1},{3,0},{4,7},{5,6},{6,5},{7,4},{8,11},{9,10},{10,... | collective-permute-start | bytes 776 | tf_op jit(solution)/shard_map/ppermute | solution.py:75
  (332 shorter events, 205.2 us)
Async XLA Ops:
  7.2 207.9 %all-gather.2.cloned.1.call-start = ((), (), s32[]{:S(2)}) async-start(), calls=%async_computation.6 | async-start | bytes 9732096 | tf_op jit(solution)/shard_map/all_gather | solution.py:748
  15.3 22.4 %collective-permute-start.8 = (bf16[128,2048]{1,0:T(8,128)(2,1)}, bf16[128,2048]{1,0:T(8,128)(2,1)S(1)}, u32[]{:S(2)}, u32[]{:S(2)}) collective-permute-start(bf16[128,2048]{1,0:T(8,128)(2,1)} %param.33), channel_id=1, source_target_pairs={{0,2},{1,3},{2,0},{3,1},{4,6},{5,7},{6,4},{7,5},{8,10},{9,11},{10,... | collective-permute-start | bytes 1572872 | tf_op jit(solution)/shard_map/ppermute | solution.py:75
  37.6 14.3 %collective-permute-start.10 = (bf16[4,2,1,32,1408]{4,3,1,2,0:T(8,128)(2,1)}, bf16[4,2,1,32,1408]{4,3,1,2,0:T(8,128)(2,1)S(1)}, u32[]{:S(2)}, u32[]{:S(2)}) collective-permute-start(bf16[4,2,1,32,1408]{4,3,1,2,0:T(8,128)(2,1)} %pad_maximum_fusion.7), channel_id=1, source_target_pairs={{0,96},{4,100},{8,104},{12,108},{16,112},{20,116},{24,120},{28,124... | collective-permute-start | bytes 2162696 | tf_op jit(solution)/shard_map/ppermute | solution.py:71
  41.3 46.0 %collective-permute-start.18 = (bf16[256,2048]{1,0:T(8,128)(2,1)}, bf16[256,2048]{1,0:T(8,128)(2,1)}, u32[]{:S(2)}, u32[]{:S(2)}) collective-permute-start(bf16[256,2048]{1,0:T(8,128)(2,1)} %pad_maximum_fusion.4), channel_id=1, source_target_pairs={{0,1},{1,0},{2,3},{3,2},{4,5},{5,4},{6,7},{7,6},{8,9},{9,8},{10,11... | collective-permute-start | bytes 3145736 | tf_op jit(solution)/shard_map/ppermute | solution.py:75
  48.2 31.1 %collective-permute-start.9 = (bf16[4,2,1,32,1408]{4,3,1,2,0:T(8,128)(2,1)}, bf16[4,2,1,32,1408]{4,3,1,2,0:T(8,128)(2,1)}, u32[]{:S(2)}, u32[]{:S(2)}) collective-permute-start(bf16[4,2,1,32,1408]{4,3,1,2,0:T(8,128)(2,1)} %pad_maximum_fusion.7), channel_id=1, source_target_pairs={{0,32},{4,36},{8,40},{12,44},{16,48},{20,52},{24,56},{28,60},{32,0... | collective-permute-start | bytes 2162696 | tf_op jit(solution)/shard_map/ppermute | solution.py:71
  48.2 31.1 %collective-permute-start.12 = (bf16[4,2,1,32,1408]{4,3,2,1,0:T(8,128)(2,1)S(1)}, bf16[4,2,1,32,1408]{4,3,2,1,0:T(8,128)(2,1)}, u32[]{:S(2)}, u32[]{:S(2)}) collective-permute-start(bf16[4,2,1,32,1408]{4,3,2,1,0:T(8,128)(2,1)S(1)} %pad_maximum_fusion.8.refs_5_), channel_id=1, source_target_pairs={{0,12},{4,8},{8,4},{12,0},{16,28},{20,24},{24,20},{28,16},{32,44},... | collective-permute-start | bytes 2162696 | tf_op jit(solution)/shard_map/ppermute | solution.py:71
  48.9 30.4 %collective-permute-start.11 = (bf16[4,2,1,32,1408]{4,3,2,1,0:T(8,128)(2,1)S(1)}, bf16[4,2,1,32,1408]{4,3,2,1,0:T(8,128)(2,1)}, u32[]{:S(2)}, u32[]{:S(2)}) collective-permute-start(bf16[4,2,1,32,1408]{4,3,2,1,0:T(8,128)(2,1)S(1)} %pad_maximum_fusion.8.refs_5_), channel_id=1, source_target_pairs={{0,4},{4,0},{8,12},{12,8},{16,20},{20,16},{24,28},{28,24},{32,36},... | collective-permute-start | bytes 2162696 | tf_op jit(solution)/shard_map/ppermute | solution.py:71
  52.0 31.5 %collective-permute-start = (bf16[128,2048]{1,0:T(8,128)(2,1)S(1)}, bf16[128,2048]{1,0:T(8,128)(2,1)S(1)}, u32[]{:S(2)}, u32[]{:S(2)}) collective-permute-start(bf16[128,2048]{1,0:T(8,128)(2,1)S(1)} %copy-done.28), channel_id=1, source_target_pairs={{0,2},{1,3},{2,0},{3,1},{4,6},{5,7},{6,4},{7,5},{8,10},{9,11},{10,... | collective-permute-start | bytes 1572872 | tf_op jit(solution)/shard_map/ppermute | solution.py:75
  83.5 15.9 %collective-permute-start.17 = (bf16[2,2,1,32,1408]{4,3,2,1,0:T(8,128)(2,1)S(1)}, bf16[2,2,1,32,1408]{4,3,2,1,0:T(8,128)(2,1)S(1)}, u32[]{:S(2)}, u32[]{:S(2)}) collective-permute-start(bf16[2,2,1,32,1408]{4,3,2,1,0:T(8,128)(2,1)S(1)} %slice.133), channel_id=1, source_target_pairs={{0,4},{4,0},{8,12},{12,8},{16,20},{20,16},{24,28},{28,24},{32,36},... | collective-permute-start | bytes 1081352 | tf_op jit(solution)/shard_map/ppermute | solution.py:71
  84.6 18.3 %collective-permute-start.16 = (bf16[2,2,1,32,1408]{4,3,2,1,0:T(8,128)(2,1)S(1)}, bf16[2,2,1,32,1408]{4,3,2,1,0:T(8,128)(2,1)S(1)}, u32[]{:S(2)}, u32[]{:S(2)}) collective-permute-start(bf16[2,2,1,32,1408]{4,3,2,1,0:T(8,128)(2,1)S(1)} %slice.132), channel_id=1, source_target_pairs={{0,12},{4,8},{8,4},{12,0},{16,28},{20,24},{24,20},{28,16},{32,44},... | collective-permute-start | bytes 1081352 | tf_op jit(solution)/shard_map/ppermute | solution.py:71
  85.4 17.5 %collective-permute-start.15 = (bf16[2,2,1,32,1408]{4,3,1,2,0:T(8,128)(2,1)S(1)}, bf16[2,2,1,32,1408]{4,3,1,2,0:T(8,128)(2,1)S(1)}, u32[]{:S(2)}, u32[]{:S(2)}) collective-permute-start(bf16[2,2,1,32,1408]{4,3,1,2,0:T(8,128)(2,1)S(1)} %slice.131), channel_id=1, source_target_pairs={{0,32},{4,36},{8,40},{12,44},{16,48},{20,52},{24,56},{28,60},{32,0... | collective-permute-start | bytes 1081352 | tf_op jit(solution)/shard_map/ppermute | solution.py:71
  85.6 18.4 %collective-permute-start.14 = (bf16[2,2,1,32,1408]{4,3,1,2,0:T(8,128)(2,1)S(1)}, bf16[2,2,1,32,1408]{4,3,1,2,0:T(8,128)(2,1)S(1)}, u32[]{:S(2)}, u32[]{:S(2)}) collective-permute-start(bf16[2,2,1,32,1408]{4,3,1,2,0:T(8,128)(2,1)S(1)} %slice.130), channel_id=1, source_target_pairs={{0,96},{4,100},{8,104},{12,108},{16,112},{20,116},{24,120},{28,124... | collective-permute-start | bytes 1081352 | tf_op jit(solution)/shard_map/ppermute | solution.py:71
  87.3 30.5 %collective-permute-start.13 = (bf16[256,2048]{1,0:T(8,128)(2,1)}, bf16[256,2048]{1,0:T(8,128)(2,1)}, u32[]{:S(2)}, u32[]{:S(2)}) collective-permute-start(bf16[256,2048]{1,0:T(8,128)(2,1)} %pad_maximum_fusion.3), channel_id=1, source_target_pairs={{0,1},{1,0},{2,3},{3,2},{4,5},{5,4},{6,7},{7,6},{8,9},{9,8},{10,11... | collective-permute-start | bytes 3145736 | tf_op jit(solution)/shard_map/ppermute | solution.py:75
  110.9 42.2 %all-to-all-start = ((bf16[32,40,1024]{2,1,0:T(8,128)(2,1)}), bf16[32,40,1024]{2,1,0:T(8,128)(2,1)}, u32[]{:S(2)}, u32[]{:S(2)}) async-start(bf16[32,40,1024]{2,1,0:T(8,128)(2,1)} %bitcast.144), calls=%async_computation | async-start | bytes 5242880 | tf_op jit(solution)/shard_map/all_to_all | solution.py:99
  161.5 13.2 %collective-permute-start.20 = (bf16[128,2048]{1,0:T(8,128)(2,1)S(1)}, bf16[128,2048]{1,0:T(8,128)(2,1)S(1)}, u32[]{:S(2)}, u32[]{:S(2)}) collective-permute-start(bf16[128,2048]{1,0:T(8,128)(2,1)S(1)} %slice.248), channel_id=1, source_target_pairs={{0,2},{1,3},{2,0},{3,1},{4,6},{5,7},{6,4},{7,5},{8,10},{9,11},{10,... | collective-permute-start | bytes 1572872 | tf_op jit(solution)/shard_map/ppermute | solution.py:75
  202.3 50.4 %all-to-all-start.1 = ((bf16[32,40,1152]{2,1,0:T(8,128)(2,1)}), bf16[32,40,1152]{2,1,0:T(8,128)(2,1)}, u32[]{:S(2)}, u32[]{:S(2)}) async-start(bf16[32,40,1152]{2,1,0:T(8,128)(2,1)} %bitcast.142), calls=%async_computation.1 | async-start | bytes 5898240 | tf_op jit(solution)/shard_map/all_to_all | solution.py:99
  214.7 197.9 %reduce-scatter.2.cloned.1.call-start = ((), (), s32[]{:S(2)}) async-start(), calls=%async_computation.7 | async-start | bytes 11796480 | tf_op jit(solution)/shard_map/reduce_scatter | solution.py:104
  311.9 28.8 %collective-permute-start.26 = (bf16[1280,1024]{1,0:T(8,128)(2,1)}, bf16[1280,1024]{1,0:T(8,128)(2,1)}, u32[]{:S(2)}, u32[]{:S(2)}) collective-permute-start(bf16[1280,1024]{1,0:T(8,128)(2,1)} %convolution_convert_fusion.2), channel_id=1, source_target_pairs={{0,1},{1,0},{2,3},{3,2},{4,5},{5,4},{6,7},{7,6},{8,9},{9,8},{10,11... | collective-permute-start | bytes 7864328 | tf_op jit(solution)/shard_map/ppermute | solution.py:75
  312.1 47.3 %all-to-all-start.2 = ((bf16[32,40,1152]{2,1,0:T(8,128)(2,1)}), bf16[32,40,1152]{2,1,0:T(8,128)(2,1)}, u32[]{:S(2)}, u32[]{:S(2)}) async-start(bf16[32,40,1152]{2,1,0:T(8,128)(2,1)} %bitcast.135), calls=%async_computation.2 | async-start | bytes 5898240 | tf_op jit(solution)/shard_map/all_to_all | solution.py:99
  370.9 13.6 %collective-permute-start.28 = (bf16[128,2048]{1,0:T(8,128)(2,1)S(1)}, bf16[128,2048]{1,0:T(8,128)(2,1)S(1)}, u32[]{:S(2)}, u32[]{:S(2)}) collective-permute-start(bf16[128,2048]{1,0:T(8,128)(2,1)S(1)} %slice.247), channel_id=1, source_target_pairs={{0,2},{1,3},{2,0},{3,1},{4,6},{5,7},{6,4},{7,5},{8,10},{9,11},{10,... | collective-permute-start | bytes 1572872 | tf_op jit(solution)/shard_map/ppermute | solution.py:75
  386.4 12.6 %collective-permute-start.29 = (bf16[128,2048]{1,0:T(8,128)(2,1)S(1)}, bf16[128,2048]{1,0:T(8,128)(2,1)S(1)}, u32[]{:S(2)}, u32[]{:S(2)}) collective-permute-start(bf16[128,2048]{1,0:T(8,128)(2,1)S(1)} %get-tuple-element.129), channel_id=1, source_target_pairs={{0,2},{1,3},{2,0},{3,1},{4,6},{5,7},{6,4},{7,5},{8,10},{9,11},{10,... | collective-permute-start | bytes 1572872 | tf_op jit(solution)/shard_map/ppermute | solution.py:75
  401.8 61.3 %all-to-all-start.3 = ((bf16[32,40,1024]{2,1,0:T(8,128)(2,1)}), bf16[32,40,1024]{2,1,0:T(8,128)(2,1)}, u32[]{:S(2)}, u32[]{:S(2)}) async-start(bf16[32,40,1024]{2,1,0:T(8,128)(2,1)} %bitcast.143), calls=%async_computation.3 | async-start | bytes 5242880 | tf_op jit(solution)/shard_map/all_to_all | solution.py:99
  431.3 25.9 %collective-permute-start.31 = (bf16[1,2,4,32,1408]{4,3,1,2,0:T(8,128)(2,1)S(1)}, bf16[1,2,4,32,1408]{4,3,1,2,0:T(8,128)(2,1)S(1)}, u32[]{:S(2)}, u32[]{:S(2)}) collective-permute-start(bf16[1,2,4,32,1408]{4,3,1,2,0:T(8,128)(2,1)S(1)} %copy.62), channel_id=1, source_target_pairs={{0,32},{4,36},{8,40},{12,44},{16,48},{20,52},{24,56},{28,60},{32,0... | collective-permute-start | bytes 2162696 | tf_op jit(solution)/shard_map/ppermute | solution.py:71
  433.5 39.5 %collective-permute-start.37 = (bf16[1,2,4,32,1408]{4,3,1,2,0:T(8,128)(2,1)}, bf16[1,2,4,32,1408]{4,3,1,2,0:T(8,128)(2,1)}, u32[]{:S(2)}, u32[]{:S(2)}) collective-permute-start(bf16[1,2,4,32,1408]{4,3,1,2,0:T(8,128)(2,1)} %copy.65), channel_id=1, source_target_pairs={{0,64},{4,68},{8,72},{12,76},{16,80},{20,84},{24,88},{28,92},{32,9... | collective-permute-start | bytes 2162696 | tf_op jit(solution)/shard_map/ppermute | solution.py:71
  436.9 37.7 %collective-permute-start.36 = (bf16[1,2,4,32,1408]{4,3,1,2,0:T(8,128)(2,1)}, bf16[1,2,4,32,1408]{4,3,1,2,0:T(8,128)(2,1)}, u32[]{:S(2)}, u32[]{:S(2)}) collective-permute-start(bf16[1,2,4,32,1408]{4,3,1,2,0:T(8,128)(2,1)} %copy.64), channel_id=1, source_target_pairs={{0,96},{4,100},{8,104},{12,108},{16,112},{20,116},{24,120},{28,124... | collective-permute-start | bytes 2162696 | tf_op jit(solution)/shard_map/ppermute | solution.py:71
  437.2 39.2 %collective-permute-start.38 = (bf16[1,4,2,32,1408]{4,3,2,1,0:T(8,128)(2,1)}, bf16[1,4,2,32,1408]{4,3,2,1,0:T(8,128)(2,1)}, u32[]{:S(2)}, u32[]{:S(2)}) collective-permute-start(bf16[1,4,2,32,1408]{4,3,2,1,0:T(8,128)(2,1)} %get-tuple-element.115), channel_id=1, source_target_pairs={{0,4},{4,0},{8,12},{12,8},{16,20},{20,16},{24,28},{28,24},{32,36},... | collective-permute-start | bytes 2162696 | tf_op jit(solution)/shard_map/ppermute | solution.py:71
  438.3 38.1 %collective-permute-start.39 = (bf16[1,4,2,32,1408]{4,3,2,1,0:T(8,128)(2,1)}, bf16[1,4,2,32,1408]{4,3,2,1,0:T(8,128)(2,1)}, u32[]{:S(2)}, u32[]{:S(2)}) collective-permute-start(bf16[1,4,2,32,1408]{4,3,2,1,0:T(8,128)(2,1)} %get-tuple-element.116), channel_id=1, source_target_pairs={{0,12},{4,8},{8,4},{12,0},{16,28},{20,24},{24,20},{28,16},{32,44},... | collective-permute-start | bytes 2162696 | tf_op jit(solution)/shard_map/ppermute | solution.py:71
  457.3 21.0 %collective-permute-start.40 = (bf16[1,4,2,32,1408]{4,3,2,1,0:T(8,128)(2,1)}, bf16[1,4,2,32,1408]{4,3,2,1,0:T(8,128)(2,1)}, u32[]{:S(2)}, u32[]{:S(2)}) collective-permute-start(bf16[1,4,2,32,1408]{4,3,2,1,0:T(8,128)(2,1)} %get-tuple-element.117), channel_id=1, source_target_pairs={{0,8},{4,12},{8,0},{12,4},{16,24},{20,28},{24,16},{28,20},{32,40},... | collective-permute-start | bytes 2162696 | tf_op jit(solution)/shard_map/ppermute | solution.py:71
  463.2 79.9 %all-to-all-start.4 = ((bf16[8,3,64,704]{3,2,1,0:T(8,128)(2,1)}), bf16[8,3,64,704]{3,2,1,0:T(8,128)(2,1)}, u32[]{:S(2)}, u32[]{:S(2)}) async-start(bf16[8,3,64,704]{3,2,1,0:T(8,128)(2,1)} %reduce-scatter.2.cloned.1.call-done), calls=%async_computation.5 | async-start | bytes 4718592 | tf_op jit(solution)/shard_map/all_to_all | solution.py:111
  484.2 55.9 %collective-permute-start.35 = (bf16[128,2048]{1,0:T(8,128)(2,1)S(1)}, bf16[128,2048]{1,0:T(8,128)(2,1)S(1)}, u32[]{:S(2)}, u32[]{:S(2)}) collective-permute-start(bf16[128,2048]{1,0:T(8,128)(2,1)S(1)} %slice.245), channel_id=1, source_target_pairs={{0,2},{1,3},{2,0},{3,1},{4,6},{5,7},{6,4},{7,5},{8,10},{9,11},{10,... | collective-permute-start | bytes 1572872 | tf_op jit(solution)/shard_map/ppermute | solution.py:75
  484.7 55.9 %collective-permute-start.33 = (bf16[128,2048]{1,0:T(8,128)(2,1)S(1)}, bf16[128,2048]{1,0:T(8,128)(2,1)S(1)}, u32[]{:S(2)}, u32[]{:S(2)}) collective-permute-start(bf16[128,2048]{1,0:T(8,128)(2,1)S(1)} %slice.246), channel_id=1, source_target_pairs={{0,2},{1,3},{2,0},{3,1},{4,6},{5,7},{6,4},{7,5},{8,10},{9,11},{10,... | collective-permute-start | bytes 1572872 | tf_op jit(solution)/shard_map/ppermute | solution.py:75
  486.2 20.7 %collective-permute-start.41 = (bf16[1,2,32,1408]{3,2,1,0:T(8,128)(2,1)S(1)}, bf16[1,2,32,1408]{3,2,1,0:T(8,128)(2,1)S(1)}, u32[]{:S(2)}, u32[]{:S(2)}) collective-permute-start(bf16[1,2,32,1408]{3,2,1,0:T(8,128)(2,1)S(1)} %get-tuple-element.139), channel_id=1, source_target_pairs={{0,4},{4,0},{8,12},{12,8},{16,20},{20,16},{24,28},{28,24},{32,36},... | collective-permute-start | bytes 540680 | tf_op jit(solution)/shard_map/ppermute | solution.py:71
  (92 other events, 803.6 us)
Sparse Core Ops, SparseCore 0:
  11.0 148.9 all-gather.1
  243.5 122.1 reduce-scatter.1

commit v4 on v3

--- a/solution.py
+++ b/solution.py
@@ -34,11 +34,6 @@
 
 def matmul(left_op, right_op):
     return jnp.dot(left_op, right_op, preferred_element_type=f32)
-
-
-def silu_slope(values):
-    sigmoid_v = jax.nn.sigmoid(values)
-    return sigmoid_v * (1.0 + values * (1.0 - sigmoid_v))
 
 
 def norm_rows(values, gain_vec):
@@ -379,7 +374,7 @@
     gate_pre = product(rows_own, rows_far, eg_own, eg_far)
     up_pre = product(rows_own, rows_far, eu_own, eu_far)
     down_back = product(grads_own, grads_far, ed_own, ed_far) * gate_mine
-    sigmoid_v = jax.nn.sigmoid(gate_pre)
+    sigmoid_v = 0.5 + 0.5 * jnp.tanh(0.5 * gate_pre)
     silu_gate = gate_pre * sigmoid_v
     hidden_wide = silu_gate * up_pre
     hidden[...] = (hidden_wide * gate_mine).astype(bf16)
@@ -512,7 +507,7 @@
     gate_pre = matmul(rows[...], weight(0))
     up_pre = matmul(rows[...], weight(1))
     down_back = matmul(grads[...], weight(2))
-    sigmoid_v = jax.nn.sigmoid(gate_pre)
+    sigmoid_v = 0.5 + 0.5 * jnp.tanh(0.5 * gate_pre)
     silu_gate = gate_pre * sigmoid_v
     hidden_part = (silu_gate * up_pre).astype(bf16)
     hidden[...] = hidden_part
@@ -861,12 +856,14 @@
     d_h_attn = sum_chips(d_h_half)
     output = (middle + sum_chips(out_half)).astype(bf16)
     sums = scatter_fsdp_two(sum_parts, spot)[0]
-    out_sums, tile_sums = sums[:, :q_width], small_sum_tp(sums[:, q_width : q_width + LANES])
-    qkv_sums = sums[:, q_width + LANES :]
+    out_sums, qkv_sums = sums[:, :q_width], sums[:, q_width + LANES :]
+    gain_sum = jnp.sum(qkv_sums * qkv_own.astype(f32), axis=1, keepdims=True)
+    tile_sums = small_sum_tp(
+        sums[:, q_width : q_width + LANES] + jnp.where(lane_ids == experts + 1, gain_sum, 0.0)
+    )
     _, factor_one = norm_rows(own_tokens, gain_one)
     grad_tokens = (d_middle + norm_back(own_tokens, factor_one, gain_one, d_h_attn)).astype(bf16)
-    gain_sum = jnp.sum(qkv_sums * qkv_own.astype(f32), axis=1)
-    grad_g_attn = small_sum_tp(gain_sum) / g_attn.astype(f32)
+    grad_g_attn = tile_sums[:, experts + 1] / g_attn.astype(f32)
     return (
         output,
         grad_tokens,

time: 562 us -> 559 us (level)
    ppermute x26 -> x23, starting transfers between devices: 40.3 us -> 37.8 us  [move_tp(): return lax.ppermute(values, 'tp', [(i, i ^ flip) for i in range(TP)])]
    ppermute x26 -> x23, waiting for transfers between devices: 62.8 us -> 62.6 us  [move_tp(): return lax.ppermute(values, 'tp', [(i, i ^ flip) for i in range(TP)])]
  transfers between devices with their start and end apart: 62 -> 59, of which waited for: 30 -> 29; matrix products, arithmetic and copies ran while one was open for 16% -> 16% of each run, Pallas kernels for 21% -> 21%
where the time goes in v4:
time: 559 us; the launch traced here: 550 us
  waiting for transfers between devices  184 us (33%)
  starting transfers between devices  129 us (23%)
  Pallas kernels  117 us (21%)
  matrix products  44.5 us (8%)
  other arithmetic  30.3 us (5%)
  local copies, waits for them, and re-layouts  29.6 us (5%)
  between operations  15.3 us (3%)
    ppermute x29, waiting for transfers between devices, route_fsdp(): return lax.ppermute(values, 'fsdp', pairs)  78.9 us
    ppermute x23, waiting for transfers between devices, move_tp(): return lax.ppermute(values, 'tp', [(i, i ^ flip) for i in range(TP)])  62.6 us
    ppermute x29, starting transfers between devices, route_fsdp(): return lax.ppermute(values, 'fsdp', pairs)  50.8 us
    all_to_all x4, waiting for transfers between devices, swap_fsdp(): lax.all_to_all(blocks, 'fsdp', split_axis=0, concat_axis=0, tiled=True)  42.7 us
    ppermute x23, starting transfers between devices, move_tp(): return lax.ppermute(values, 'tp', [(i, i ^ flip) for i in range(TP)])  37.8 us
    all_to_all x4, starting transfers between devices, swap_fsdp(): lax.all_to_all(blocks, 'fsdp', split_axis=0, concat_axis=0, tiled=True)  32.8 us
    pallas_call x1, Pallas kernels, expert_rows(): pl.pallas_call(expert_rows_kernel, out_shape=[shape(hidden), shape(hidden...  28.1 us
    dot_general x8, matrix products, matmul(): return jnp.dot(left_op, right_op, preferred_element_type=f32)  27.5 us
  transfers between devices with their start and end apart: 59, of which 29 were waited for; matrix products, arithmetic and copies ran while one was open for 16% of the time, Pallas kernels for 21%

profile of v4, /device:TPU:1, one launch (start us, length us, event | category | flops | bytes accessed | tf_op | source)
XLA Modules:
  0.0 549.9 jit_solution(16795496111624020322)
XLA Ops:
  41.4 6.9 %collective-permute-start.18 = (bf16[256,2048]{1,0:T(8,128)(2,1)}, bf16[256,2048]{1,0:T(8,128)(2,1)}, u32[]{:S(2)}, u32[]{:S(2)}) collective-permute-start(bf16[256,2048]{1,0:T(8,128)(2,1)} %pad_maximum_fusion.4), channel_id=1, source_target_pairs={{0,1},{1,0},{2,3},{3,2},{4,5},{5,4},{6,7},{7,6},{8,9},{9,8},{10,11... | collective-permute-start | bytes 3145736 | tf_op jit(solution)/shard_map/ppermute | solution.py:70
  57.4 21.8 %collective-permute-done.9 = bf16[4,2,1,32,1408]{4,3,1,2,0:T(8,128)(2,1)} collective-permute-done((bf16[4,2,1,32,1408]{4,3,1,2,0:T(8,128)(2,1)}, bf16[4,2,1,32,1408]{4,3,1,2,0:T(8,128)(2,1)}, u32[]{:S(2)}, u32[]{:S(2)}) %collective-permute-start.9) | collective-permute-done | bytes 720928 | tf_op jit(solution)/shard_map/ppermute | solution.py:66
  94.0 5.8 %collective-permute-done.17.refs_8_ = bf16[2,2,1,32,1408]{4,3,2,1,0:T(8,128)(2,1)S(1)} collective-permute-done((bf16[2,2,1,32,1408]{4,3,2,1,0:T(8,128)(2,1)S(1)}, bf16[2,2,1,32,1408]{4,3,2,1,0:T(8,128)(2,1)S(1)}, u32[]{:S(2)}, u32[]{:S(2)}) %collective-permute-start.17) | collective-permute-done | bytes 360480 | tf_op jit(solution)/shard_map/ppermute | solution.py:66
  104.8 6.2 %place.1 = (bf16[4,2,4,64,768]{4,3,2,1,0:T(8,128)(2,1)}, bf16[4,2,4,64,128]{4,3,2,1,0:T(8,128)(2,1)}, bf16[4,2,4,64,512]{4,3,2,1,0:T(8,128)(2,1)}) custom-call(s32[3]{0:T(128)} %pad_add_fusion.3.spot, bf16[4,2,1,32,1408]{4,3,2,1,0:T(8,128)(2,1)} %bitcast.24.refs_0_, bf16[4,2,1,32,1408]{4,3,2,1,0:T(8,128)(2,1)} %bitcast.25.refs_1_, ...), custom_call_target="tpu_custom_call" | custom-call | bytes 11534336 | tf_op jit(solution)/shard_map/place/pallas_call | solution.py:167
  111.0 5.2 all-to-all-start
  124.6 4.9 attend.1.attended
  132.2 20.9 %all-to-all-done = bf16[32,40,1024]{2,1,0:T(8,128)(2,1)} async-done(((bf16[32,40,1024]{2,1,0:T(8,128)(2,1)}), bf16[32,40,1024]{2,1,0:T(8,128)(2,1)}, u32[]{:S(2)}, u32[]{:S(2)}) %all-to-all-start) | async-done | bytes 2621472 | tf_op jit(solution)/shard_map/all_to_all | solution.py:94
  163.2 11.7 %collective-permute-done.20 = bf16[128,2048]{1,0:T(8,128)(2,1)S(1)} collective-permute-done((bf16[128,2048]{1,0:T(8,128)(2,1)S(1)}, bf16[128,2048]{1,0:T(8,128)(2,1)S(1)}, u32[]{:S(2)}, u32[]{:S(2)}) %collective-permute-start.20) | collective-permute-done | bytes 524320 | tf_op jit(solution)/shard_map/ppermute | solution.py:70
  176.9 10.8 %collective-permute-done.21 = bf16[128,2048]{1,0:T(8,128)(2,1)S(1)} collective-permute-done((bf16[128,2048]{1,0:T(8,128)(2,1)S(1)}, bf16[128,2048]{1,0:T(8,128)(2,1)S(1)}, u32[]{:S(2)}, u32[]{:S(2)}) %collective-permute-start.21) | collective-permute-done | bytes 524320 | tf_op jit(solution)/shard_map/ppermute | solution.py:70
  202.4 12.2 %all-to-all-start.1 = ((bf16[32,40,1152]{2,1,0:T(8,128)(2,1)}), bf16[32,40,1152]{2,1,0:T(8,128)(2,1)}, u32[]{:S(2)}, u32[]{:S(2)}) async-start(bf16[32,40,1152]{2,1,0:T(8,128)(2,1)} %bitcast.142), calls=%async_computation.1 | async-start | bytes 5898240 | tf_op jit(solution)/shard_map/all_to_all | solution.py:94
  215.1 15.6 %shared_rows.1 = (bf16[512,704]{1,0:T(8,128)(2,1)}, bf16[512,704]{1,0:T(8,128)(2,1)}, bf16[512,704]{1,0:T(8,128)(2,1)}, bf16[512,2048]{1,0:T(8,128)(2,1)}, bf16[512,2048]{1,0:T(8,128)(2,1)}) custom-call(bf16[512,2048]{1,0:T(8,128)(2,1)} %copy-done.7, bf16[512,2048]{1,0:T(8,128)(2,1)} %copy-done.52, bf16[32,3,64,704]{3,2,1,0:T(8,128)(2,1)} %bitcast.181), custom_call_target="tpu_custom_call" | custom-call | flops 8858370048 | bytes 17039360 | tf_op jit(solution)/shard_map/shared_rows/pallas_call | solution.py:532
  234.1 9.1 %shared_grads.1 = bf16[32,3,64,704]{3,2,1,0:T(8,128)(2,1)} custom-call(bf16[512,2048]{1,0:T(8,128)(2,1)S(1)} %copy-done.8, bf16[512,2048]{1,0:T(8,128)(2,1)} %copy-done.52, bf16[512,704]{1,0:T(8,128)(2,1)S(1)} %copy-done.22, bf16[512,704]{1,0:T(8,128)(2,1)S(1)} %copy-done.23, bf16[512,704]{1,0:T(8,128)(2,1)S(1)} %copy-done.24), custom_call_target="tpu_custom_call" | custom-call | flops 4429185024 | bytes 12845056 | tf_op jit(solution)/shard_map/shared_grads/pallas_call | solution.py:564
  243.3 9.3 %all-to-all-done.1 = bf16[32,40,1152]{2,1,0:T(8,128)(2,1)} async-done(((bf16[32,40,1152]{2,1,0:T(8,128)(2,1)}), bf16[32,40,1152]{2,1,0:T(8,128)(2,1)}, u32[]{:S(2)}, u32[]{:S(2)}) %all-to-all-start.1) | async-done | bytes 2949152 | tf_op jit(solution)/shard_map/all_to_all | solution.py:94
  256.5 8.3 %collective-permute-done.24.grads_far = bf16[1280,1024]{1,0:T(8,128)(2,1)} collective-permute-done((bf16[1280,1024]{1,0:T(8,128)(2,1)}, bf16[1280,1024]{1,0:T(8,128)(2,1)}, u32[]{:S(2)}, u32[]{:S(2)}) %collective-permute-start.24) | collective-permute-done | bytes 2621472 | tf_op jit(solution)/shard_map/ppermute | solution.py:70
  264.9 28.1 %expert_rows.1 = (bf16[1280,704]{1,0:T(8,128)(2,1)}, bf16[1280,704]{1,0:T(8,128)(2,1)}, bf16[1280,704]{1,0:T(8,128)(2,1)}, bf16[1280,1024]{1,0:T(8,128)(2,1)}, bf16[1280,128]{1,0:T(8,128)(2,1)}) custom-call(s32[2]{0:T(128)} %pad_add_fusion.4.scal, bf16[1280,1152]{1,0:T(8,128)(2,1)} %bitcast.45.rows_own.gate_lanes, ...), custom_call_target="tpu_custom_call" | custom-call | flops 14763950080 | bytes 24379392 | tf_op jit(solution)/shard_map/expert_rows/pallas_call | solution.py:404
  301.5 5.0 add_and_join.1
  306.5 5.1 convolution_convert_fusion.2
  311.7 7.6 %all-to-all-start.2 = ((bf16[32,40,1152]{2,1,0:T(8,128)(2,1)}), bf16[32,40,1152]{2,1,0:T(8,128)(2,1)}, u32[]{:S(2)}, u32[]{:S(2)}) async-start(bf16[32,40,1152]{2,1,0:T(8,128)(2,1)} %bitcast.135), calls=%async_computation.2 | async-start | bytes 5898240 | tf_op jit(solution)/shard_map/all_to_all | solution.py:94
  319.3 21.1 %expert_grads.1 = (f32[704,2048]{1,0:T(8,128)}, f32[704,2048]{1,0:T(8,128)}, f32[704,2048]{1,0:T(8,128)}) custom-call(s32[1]{0:T(128)} %bitcast.41.core, bf16[1280,1152]{1,0:T(8,128)(2,1)} %bitcast.45.rows_own.gate_lanes, bf16[1280,1152]{1,0:T(8,128)(2,1)} %collective-permute-done.23.rows_far, bf16[1280,1024]{1,0:T(8,128)(2,1)} %bitcast.40.grads_own, ...), custom_call_target="tpu_custom_call" | custom-call | flops 11072962560 | bytes 33030144 | tf_op jit(solution)/shard_map/expert_grads/pallas_call | solution.py:636
  340.5 6.2 %add_convert_fusion = bf16[1280,1024]{1,0:T(8,128)(2,1)} fusion(bf16[1280,1024]{1,0:T(8,128)(2,1)} %collective-permute-done.26, bf16[1280,704]{1,0:T(8,128)(2,1)} %get-tuple-element.98.scaled, bf16[704,2048]{1,0:T(8,128)(2,1)S(1)} %bitcast.191, s32[]{:T(128)S(6)} %select_n.109), kind=kOutput, calls=%fused_computation.3 | convolution fusion | flops 1849425920 | bytes 8486916 | tf_op jit(solution)/shard_map/dot_general | solution.py:36
  346.7 12.5 %all-to-all-done.2 = bf16[32,40,1152]{2,1,0:T(8,128)(2,1)} async-done(((bf16[32,40,1152]{2,1,0:T(8,128)(2,1)}), bf16[32,40,1152]{2,1,0:T(8,128)(2,1)}, u32[]{:S(2)}, u32[]{:S(2)}) %all-to-all-start.2) | async-done | bytes 2949152 | tf_op jit(solution)/shard_map/all_to_all | solution.py:94
  371.2 13.0 %collective-permute-done.28 = bf16[128,2048]{1,0:T(8,128)(2,1)S(1)} collective-permute-done((bf16[128,2048]{1,0:T(8,128)(2,1)S(1)}, bf16[128,2048]{1,0:T(8,128)(2,1)S(1)}, u32[]{:S(2)}, u32[]{:S(2)}) %collective-permute-start.28) | collective-permute-done | bytes 524320 | tf_op jit(solution)/shard_map/ppermute | solution.py:70
  386.6 12.1 %collective-permute-done.29 = bf16[128,2048]{1,0:T(8,128)(2,1)S(1)} collective-permute-done((bf16[128,2048]{1,0:T(8,128)(2,1)S(1)}, bf16[128,2048]{1,0:T(8,128)(2,1)S(1)}, u32[]{:S(2)}, u32[]{:S(2)}) %collective-permute-start.29) | collective-permute-done | bytes 524320 | tf_op jit(solution)/shard_map/ppermute | solution.py:70
  401.5 7.9 %all-to-all-start.3 = ((bf16[32,40,1024]{2,1,0:T(8,128)(2,1)}), bf16[32,40,1024]{2,1,0:T(8,128)(2,1)}, u32[]{:S(2)}, u32[]{:S(2)}) async-start(bf16[32,40,1024]{2,1,0:T(8,128)(2,1)} %bitcast.143), calls=%async_computation.3 | async-start | bytes 5242880 | tf_op jit(solution)/shard_map/all_to_all | solution.py:94
  415.8 6.0 %attend_back.1.d_qkv = bf16[512,768]{1,0:T(8,128)(2,1)S(1)} custom-call(s32[3]{0:T(128)S(1)} %pad_add_fusion.2.where, bf16[512,768]{1,0:T(8,128)(2,1)S(1)} %copy-done.3, bf16[512,768]{1,0:T(8,128)(2,1)S(1)} %copy-done.3, bf16[512,768]{1,0:T(8,128)(2,1)S(1)} %copy-done.3, bf16[512,512]{1,0:T(8,128)(2,1)S(1)} %convolution_convert_fusion.6.g_ref), custom_call_target="tpu_custom_call" | custom-call | flops 1342177280 | bytes 1572864 | tf_op jit(solution)/shard_map/attend_back/pallas_call | solution.py:324
  422.7 8.2 %attention_grads.1 = (bf16[1,2,4,32,1408]{4,3,2,1,0:T(8,128)(2,1)S(1)}, bf16[1,2,4,32,1408]{4,3,2,1,0:T(8,128)(2,1)S(1)}, bf16[1,2,4,32,1408]{4,3,2,1,0:T(8,128)...) custom-call(s32[3]{0:T(128)S(1)} %copy-done.21, ...), custom_call_target="tpu_custom_call" | custom-call | flops 2952790016 | bytes 14155776 | tf_op jit(solution)/shard_map/attention_grads/pallas_call | solution.py:600
  439.8 17.1 %collective-permute-done.31 = bf16[1,2,4,32,1408]{4,3,1,2,0:T(8,128)(2,1)S(1)} collective-permute-done((bf16[1,2,4,32,1408]{4,3,1,2,0:T(8,128)(2,1)S(1)}, bf16[1,2,4,32,1408]{4,3,1,2,0:T(8,128)(2,1)S(1)}, u32[]{:S(2)}, u32[]{:S(2)}) %collective-permute-start.31) | collective-permute-done | bytes 720928 | tf_op jit(solution)/shard_map/ppermute | solution.py:66
  462.8 6.9 %all-to-all-start.4 = ((bf16[8,3,64,704]{3,2,1,0:T(8,128)(2,1)}), bf16[8,3,64,704]{3,2,1,0:T(8,128)(2,1)}, u32[]{:S(2)}, u32[]{:S(2)}) async-start(bf16[8,3,64,704]{3,2,1,0:T(8,128)(2,1)} %reduce-scatter.2.cloned.1.call-done), calls=%async_computation.5 | async-start | bytes 4718592 | tf_op jit(solution)/shard_map/all_to_all | solution.py:106
  485.9 11.4 %collective-permute-start.41 = (bf16[1,2,32,1408]{3,2,1,0:T(8,128)(2,1)S(1)}, bf16[1,2,32,1408]{3,2,1,0:T(8,128)(2,1)S(1)}, u32[]{:S(2)}, u32[]{:S(2)}) collective-permute-start(bf16[1,2,32,1408]{3,2,1,0:T(8,128)(2,1)S(1)} %get-tuple-element.141), channel_id=1, source_target_pairs={{0,4},{4,0},{8,12},{12,8},{16,20},{20,16},{24,28},{28,24},{32,36},... | collective-permute-start | bytes 540680 | tf_op jit(solution)/shard_map/ppermute | solution.py:66
  501.9 4.7 collective-permute-done.41
  511.2 4.8 collective-permute-done.46
  526.4 5.9 %collective-permute-start.51 = (f32[64,128]{1,0:T(8,128)S(1)}, f32[64,128]{1,0:T(8,128)S(1)}, u32[]{:S(2)}, u32[]{:S(2)}) collective-permute-start(f32[64,128]{1,0:T(8,128)S(1)} %get-tuple-element.151), channel_id=1, source_target_pairs={{0,3},{1,2},{2,1},{3,0},{4,7},{5,6},{6,5},{7,4},{8,11},{9,10},{10,... | collective-permute-start | bytes 98312 | tf_op jit(solution)/shard_map/ppermute | solution.py:70
  (327 shorter events, 202.2 us)
Async XLA Ops:
  7.2 207.9 %all-gather.2.cloned.1.call-start = ((), (), s32[]{:S(2)}) async-start(), calls=%async_computation.6 | async-start | bytes 9732096 | tf_op jit(solution)/shard_map/all_gather | solution.py:743
  15.3 22.4 %collective-permute-start.8 = (bf16[128,2048]{1,0:T(8,128)(2,1)}, bf16[128,2048]{1,0:T(8,128)(2,1)S(1)}, u32[]{:S(2)}, u32[]{:S(2)}) collective-permute-start(bf16[128,2048]{1,0:T(8,128)(2,1)} %param.33), channel_id=1, source_target_pairs={{0,2},{1,3},{2,0},{3,1},{4,6},{5,7},{6,4},{7,5},{8,10},{9,11},{10,... | collective-permute-start | bytes 1572872 | tf_op jit(solution)/shard_map/ppermute | solution.py:70
  37.7 14.3 %collective-permute-start.10 = (bf16[4,2,1,32,1408]{4,3,1,2,0:T(8,128)(2,1)}, bf16[4,2,1,32,1408]{4,3,1,2,0:T(8,128)(2,1)S(1)}, u32[]{:S(2)}, u32[]{:S(2)}) collective-permute-start(bf16[4,2,1,32,1408]{4,3,1,2,0:T(8,128)(2,1)} %pad_maximum_fusion.7), channel_id=1, source_target_pairs={{0,96},{4,100},{8,104},{12,108},{16,112},{20,116},{24,120},{28,124... | collective-permute-start | bytes 2162696 | tf_op jit(solution)/shard_map/ppermute | solution.py:66
  41.4 46.0 %collective-permute-start.18 = (bf16[256,2048]{1,0:T(8,128)(2,1)}, bf16[256,2048]{1,0:T(8,128)(2,1)}, u32[]{:S(2)}, u32[]{:S(2)}) collective-permute-start(bf16[256,2048]{1,0:T(8,128)(2,1)} %pad_maximum_fusion.4), channel_id=1, source_target_pairs={{0,1},{1,0},{2,3},{3,2},{4,5},{5,4},{6,7},{7,6},{8,9},{9,8},{10,11... | collective-permute-start | bytes 3145736 | tf_op jit(solution)/shard_map/ppermute | solution.py:70
  48.2 31.0 %collective-permute-start.9 = (bf16[4,2,1,32,1408]{4,3,1,2,0:T(8,128)(2,1)}, bf16[4,2,1,32,1408]{4,3,1,2,0:T(8,128)(2,1)}, u32[]{:S(2)}, u32[]{:S(2)}) collective-permute-start(bf16[4,2,1,32,1408]{4,3,1,2,0:T(8,128)(2,1)} %pad_maximum_fusion.7), channel_id=1, source_target_pairs={{0,32},{4,36},{8,40},{12,44},{16,48},{20,52},{24,56},{28,60},{32,0... | collective-permute-start | bytes 2162696 | tf_op jit(solution)/shard_map/ppermute | solution.py:66
  48.3 31.0 %collective-permute-start.12 = (bf16[4,2,1,32,1408]{4,3,2,1,0:T(8,128)(2,1)S(1)}, bf16[4,2,1,32,1408]{4,3,2,1,0:T(8,128)(2,1)}, u32[]{:S(2)}, u32[]{:S(2)}) collective-permute-start(bf16[4,2,1,32,1408]{4,3,2,1,0:T(8,128)(2,1)S(1)} %pad_maximum_fusion.8.refs_5_), channel_id=1, source_target_pairs={{0,12},{4,8},{8,4},{12,0},{16,28},{20,24},{24,20},{28,16},{32,44},... | collective-permute-start | bytes 2162696 | tf_op jit(solution)/shard_map/ppermute | solution.py:66
  48.9 30.3 %collective-permute-start.11 = (bf16[4,2,1,32,1408]{4,3,2,1,0:T(8,128)(2,1)S(1)}, bf16[4,2,1,32,1408]{4,3,2,1,0:T(8,128)(2,1)}, u32[]{:S(2)}, u32[]{:S(2)}) collective-permute-start(bf16[4,2,1,32,1408]{4,3,2,1,0:T(8,128)(2,1)S(1)} %pad_maximum_fusion.8.refs_5_), channel_id=1, source_target_pairs={{0,4},{4,0},{8,12},{12,8},{16,20},{20,16},{24,28},{28,24},{32,36},... | collective-permute-start | bytes 2162696 | tf_op jit(solution)/shard_map/ppermute | solution.py:66
  52.0 31.5 %collective-permute-start = (bf16[128,2048]{1,0:T(8,128)(2,1)S(1)}, bf16[128,2048]{1,0:T(8,128)(2,1)S(1)}, u32[]{:S(2)}, u32[]{:S(2)}) collective-permute-start(bf16[128,2048]{1,0:T(8,128)(2,1)S(1)} %copy-done.28), channel_id=1, source_target_pairs={{0,2},{1,3},{2,0},{3,1},{4,6},{5,7},{6,4},{7,5},{8,10},{9,11},{10,... | collective-permute-start | bytes 1572872 | tf_op jit(solution)/shard_map/ppermute | solution.py:70
  83.5 16.3 %collective-permute-start.17 = (bf16[2,2,1,32,1408]{4,3,2,1,0:T(8,128)(2,1)S(1)}, bf16[2,2,1,32,1408]{4,3,2,1,0:T(8,128)(2,1)S(1)}, u32[]{:S(2)}, u32[]{:S(2)}) collective-permute-start(bf16[2,2,1,32,1408]{4,3,2,1,0:T(8,128)(2,1)S(1)} %slice.136), channel_id=1, source_target_pairs={{0,4},{4,0},{8,12},{12,8},{16,20},{20,16},{24,28},{28,24},{32,36},... | collective-permute-start | bytes 1081352 | tf_op jit(solution)/shard_map/ppermute | solution.py:66
  84.7 18.6 %collective-permute-start.16 = (bf16[2,2,1,32,1408]{4,3,2,1,0:T(8,128)(2,1)S(1)}, bf16[2,2,1,32,1408]{4,3,2,1,0:T(8,128)(2,1)S(1)}, u32[]{:S(2)}, u32[]{:S(2)}) collective-permute-start(bf16[2,2,1,32,1408]{4,3,2,1,0:T(8,128)(2,1)S(1)} %slice.135), channel_id=1, source_target_pairs={{0,12},{4,8},{8,4},{12,0},{16,28},{20,24},{24,20},{28,16},{32,44},... | collective-permute-start | bytes 1081352 | tf_op jit(solution)/shard_map/ppermute | solution.py:66
  85.5 17.8 %collective-permute-start.15 = (bf16[2,2,1,32,1408]{4,3,1,2,0:T(8,128)(2,1)S(1)}, bf16[2,2,1,32,1408]{4,3,1,2,0:T(8,128)(2,1)S(1)}, u32[]{:S(2)}, u32[]{:S(2)}) collective-permute-start(bf16[2,2,1,32,1408]{4,3,1,2,0:T(8,128)(2,1)S(1)} %slice.134), channel_id=1, source_target_pairs={{0,32},{4,36},{8,40},{12,44},{16,48},{20,52},{24,56},{28,60},{32,0... | collective-permute-start | bytes 1081352 | tf_op jit(solution)/shard_map/ppermute | solution.py:66
  85.7 18.4 %collective-permute-start.14 = (bf16[2,2,1,32,1408]{4,3,1,2,0:T(8,128)(2,1)S(1)}, bf16[2,2,1,32,1408]{4,3,1,2,0:T(8,128)(2,1)S(1)}, u32[]{:S(2)}, u32[]{:S(2)}) collective-permute-start(bf16[2,2,1,32,1408]{4,3,1,2,0:T(8,128)(2,1)S(1)} %slice.133), channel_id=1, source_target_pairs={{0,96},{4,100},{8,104},{12,108},{16,112},{20,116},{24,120},{28,124... | collective-permute-start | bytes 1081352 | tf_op jit(solution)/shard_map/ppermute | solution.py:66
  87.4 30.5 %collective-permute-start.13 = (bf16[256,2048]{1,0:T(8,128)(2,1)}, bf16[256,2048]{1,0:T(8,128)(2,1)}, u32[]{:S(2)}, u32[]{:S(2)}) collective-permute-start(bf16[256,2048]{1,0:T(8,128)(2,1)} %pad_maximum_fusion.3), channel_id=1, source_target_pairs={{0,1},{1,0},{2,3},{3,2},{4,5},{5,4},{6,7},{7,6},{8,9},{9,8},{10,11... | collective-permute-start | bytes 3145736 | tf_op jit(solution)/shard_map/ppermute | solution.py:70
  111.0 42.2 %all-to-all-start = ((bf16[32,40,1024]{2,1,0:T(8,128)(2,1)}), bf16[32,40,1024]{2,1,0:T(8,128)(2,1)}, u32[]{:S(2)}, u32[]{:S(2)}) async-start(bf16[32,40,1024]{2,1,0:T(8,128)(2,1)} %bitcast.144), calls=%async_computation | async-start | bytes 5242880 | tf_op jit(solution)/shard_map/all_to_all | solution.py:94
  161.7 13.2 %collective-permute-start.20 = (bf16[128,2048]{1,0:T(8,128)(2,1)S(1)}, bf16[128,2048]{1,0:T(8,128)(2,1)S(1)}, u32[]{:S(2)}, u32[]{:S(2)}) collective-permute-start(bf16[128,2048]{1,0:T(8,128)(2,1)S(1)} %slice.254), channel_id=1, source_target_pairs={{0,2},{1,3},{2,0},{3,1},{4,6},{5,7},{6,4},{7,5},{8,10},{9,11},{10,... | collective-permute-start | bytes 1572872 | tf_op jit(solution)/shard_map/ppermute | solution.py:70
  202.4 50.1 %all-to-all-start.1 = ((bf16[32,40,1152]{2,1,0:T(8,128)(2,1)}), bf16[32,40,1152]{2,1,0:T(8,128)(2,1)}, u32[]{:S(2)}, u32[]{:S(2)}) async-start(bf16[32,40,1152]{2,1,0:T(8,128)(2,1)} %bitcast.142), calls=%async_computation.1 | async-start | bytes 5898240 | tf_op jit(solution)/shard_map/all_to_all | solution.py:94
  214.6 197.6 %reduce-scatter.2.cloned.1.call-start = ((), (), s32[]{:S(2)}) async-start(), calls=%async_computation.7 | async-start | bytes 11796480 | tf_op jit(solution)/shard_map/reduce_scatter | solution.py:99
  311.5 28.9 %collective-permute-start.26 = (bf16[1280,1024]{1,0:T(8,128)(2,1)}, bf16[1280,1024]{1,0:T(8,128)(2,1)}, u32[]{:S(2)}, u32[]{:S(2)}) collective-permute-start(bf16[1280,1024]{1,0:T(8,128)(2,1)} %convolution_convert_fusion.2), channel_id=1, source_target_pairs={{0,1},{1,0},{2,3},{3,2},{4,5},{5,4},{6,7},{7,6},{8,9},{9,8},{10,11... | collective-permute-start | bytes 7864328 | tf_op jit(solution)/shard_map/ppermute | solution.py:70
  311.7 47.4 %all-to-all-start.2 = ((bf16[32,40,1152]{2,1,0:T(8,128)(2,1)}), bf16[32,40,1152]{2,1,0:T(8,128)(2,1)}, u32[]{:S(2)}, u32[]{:S(2)}) async-start(bf16[32,40,1152]{2,1,0:T(8,128)(2,1)} %bitcast.135), calls=%async_computation.2 | async-start | bytes 5898240 | tf_op jit(solution)/shard_map/all_to_all | solution.py:94
  370.6 13.6 %collective-permute-start.28 = (bf16[128,2048]{1,0:T(8,128)(2,1)S(1)}, bf16[128,2048]{1,0:T(8,128)(2,1)S(1)}, u32[]{:S(2)}, u32[]{:S(2)}) collective-permute-start(bf16[128,2048]{1,0:T(8,128)(2,1)S(1)} %slice.253), channel_id=1, source_target_pairs={{0,2},{1,3},{2,0},{3,1},{4,6},{5,7},{6,4},{7,5},{8,10},{9,11},{10,... | collective-permute-start | bytes 1572872 | tf_op jit(solution)/shard_map/ppermute | solution.py:70
  386.1 12.6 %collective-permute-start.29 = (bf16[128,2048]{1,0:T(8,128)(2,1)S(1)}, bf16[128,2048]{1,0:T(8,128)(2,1)S(1)}, u32[]{:S(2)}, u32[]{:S(2)}) collective-permute-start(bf16[128,2048]{1,0:T(8,128)(2,1)S(1)} %get-tuple-element.131), channel_id=1, source_target_pairs={{0,2},{1,3},{2,0},{3,1},{4,6},{5,7},{6,4},{7,5},{8,10},{9,11},{10,... | collective-permute-start | bytes 1572872 | tf_op jit(solution)/shard_map/ppermute | solution.py:70
  401.5 61.3 %all-to-all-start.3 = ((bf16[32,40,1024]{2,1,0:T(8,128)(2,1)}), bf16[32,40,1024]{2,1,0:T(8,128)(2,1)}, u32[]{:S(2)}, u32[]{:S(2)}) async-start(bf16[32,40,1024]{2,1,0:T(8,128)(2,1)} %bitcast.143), calls=%async_computation.3 | async-start | bytes 5242880 | tf_op jit(solution)/shard_map/all_to_all | solution.py:94
  431.0 25.9 %collective-permute-start.31 = (bf16[1,2,4,32,1408]{4,3,1,2,0:T(8,128)(2,1)S(1)}, bf16[1,2,4,32,1408]{4,3,1,2,0:T(8,128)(2,1)S(1)}, u32[]{:S(2)}, u32[]{:S(2)}) collective-permute-start(bf16[1,2,4,32,1408]{4,3,1,2,0:T(8,128)(2,1)S(1)} %copy.62), channel_id=1, source_target_pairs={{0,32},{4,36},{8,40},{12,44},{16,48},{20,52},{24,56},{28,60},{32,0... | collective-permute-start | bytes 2162696 | tf_op jit(solution)/shard_map/ppermute | solution.py:66
  433.1 39.5 %collective-permute-start.37 = (bf16[1,2,4,32,1408]{4,3,1,2,0:T(8,128)(2,1)}, bf16[1,2,4,32,1408]{4,3,1,2,0:T(8,128)(2,1)}, u32[]{:S(2)}, u32[]{:S(2)}) collective-permute-start(bf16[1,2,4,32,1408]{4,3,1,2,0:T(8,128)(2,1)} %copy.65), channel_id=1, source_target_pairs={{0,64},{4,68},{8,72},{12,76},{16,80},{20,84},{24,88},{28,92},{32,9... | collective-permute-start | bytes 2162696 | tf_op jit(solution)/shard_map/ppermute | solution.py:66
  436.6 37.7 %collective-permute-start.36 = (bf16[1,2,4,32,1408]{4,3,1,2,0:T(8,128)(2,1)}, bf16[1,2,4,32,1408]{4,3,1,2,0:T(8,128)(2,1)}, u32[]{:S(2)}, u32[]{:S(2)}) collective-permute-start(bf16[1,2,4,32,1408]{4,3,1,2,0:T(8,128)(2,1)} %copy.64), channel_id=1, source_target_pairs={{0,96},{4,100},{8,104},{12,108},{16,112},{20,116},{24,120},{28,124... | collective-permute-start | bytes 2162696 | tf_op jit(solution)/shard_map/ppermute | solution.py:66
  436.8 39.3 %collective-permute-start.38 = (bf16[1,4,2,32,1408]{4,3,2,1,0:T(8,128)(2,1)}, bf16[1,4,2,32,1408]{4,3,2,1,0:T(8,128)(2,1)}, u32[]{:S(2)}, u32[]{:S(2)}) collective-permute-start(bf16[1,4,2,32,1408]{4,3,2,1,0:T(8,128)(2,1)} %get-tuple-element.115), channel_id=1, source_target_pairs={{0,4},{4,0},{8,12},{12,8},{16,20},{20,16},{24,28},{28,24},{32,36},... | collective-permute-start | bytes 2162696 | tf_op jit(solution)/shard_map/ppermute | solution.py:66
  438.0 38.1 %collective-permute-start.39 = (bf16[1,4,2,32,1408]{4,3,2,1,0:T(8,128)(2,1)}, bf16[1,4,2,32,1408]{4,3,2,1,0:T(8,128)(2,1)}, u32[]{:S(2)}, u32[]{:S(2)}) collective-permute-start(bf16[1,4,2,32,1408]{4,3,2,1,0:T(8,128)(2,1)} %get-tuple-element.116), channel_id=1, source_target_pairs={{0,12},{4,8},{8,4},{12,0},{16,28},{20,24},{24,20},{28,16},{32,44},... | collective-permute-start | bytes 2162696 | tf_op jit(solution)/shard_map/ppermute | solution.py:66
  456.9 21.0 %collective-permute-start.40 = (bf16[1,4,2,32,1408]{4,3,2,1,0:T(8,128)(2,1)}, bf16[1,4,2,32,1408]{4,3,2,1,0:T(8,128)(2,1)}, u32[]{:S(2)}, u32[]{:S(2)}) collective-permute-start(bf16[1,4,2,32,1408]{4,3,2,1,0:T(8,128)(2,1)} %get-tuple-element.117), channel_id=1, source_target_pairs={{0,8},{4,12},{8,0},{12,4},{16,24},{20,28},{24,16},{28,20},{32,40},... | collective-permute-start | bytes 2162696 | tf_op jit(solution)/shard_map/ppermute | solution.py:66
  462.8 77.1 %all-to-all-start.4 = ((bf16[8,3,64,704]{3,2,1,0:T(8,128)(2,1)}), bf16[8,3,64,704]{3,2,1,0:T(8,128)(2,1)}, u32[]{:S(2)}, u32[]{:S(2)}) async-start(bf16[8,3,64,704]{3,2,1,0:T(8,128)(2,1)} %reduce-scatter.2.cloned.1.call-done), calls=%async_computation.5 | async-start | bytes 4718592 | tf_op jit(solution)/shard_map/all_to_all | solution.py:106
  483.8 53.1 %collective-permute-start.35 = (bf16[128,2048]{1,0:T(8,128)(2,1)S(1)}, bf16[128,2048]{1,0:T(8,128)(2,1)S(1)}, u32[]{:S(2)}, u32[]{:S(2)}) collective-permute-start(bf16[128,2048]{1,0:T(8,128)(2,1)S(1)} %slice.251), channel_id=1, source_target_pairs={{0,2},{1,3},{2,0},{3,1},{4,6},{5,7},{6,4},{7,5},{8,10},{9,11},{10,... | collective-permute-start | bytes 1572872 | tf_op jit(solution)/shard_map/ppermute | solution.py:70
  484.3 53.0 %collective-permute-start.33 = (bf16[128,2048]{1,0:T(8,128)(2,1)S(1)}, bf16[128,2048]{1,0:T(8,128)(2,1)S(1)}, u32[]{:S(2)}, u32[]{:S(2)}) collective-permute-start(bf16[128,2048]{1,0:T(8,128)(2,1)S(1)} %slice.252), channel_id=1, source_target_pairs={{0,2},{1,3},{2,0},{3,1},{4,6},{5,7},{6,4},{7,5},{8,10},{9,11},{10,... | collective-permute-start | bytes 1572872 | tf_op jit(solution)/shard_map/ppermute | solution.py:70
  485.9 20.6 %collective-permute-start.41 = (bf16[1,2,32,1408]{3,2,1,0:T(8,128)(2,1)S(1)}, bf16[1,2,32,1408]{3,2,1,0:T(8,128)(2,1)S(1)}, u32[]{:S(2)}, u32[]{:S(2)}) collective-permute-start(bf16[1,2,32,1408]{3,2,1,0:T(8,128)(2,1)S(1)} %get-tuple-element.141), channel_id=1, source_target_pairs={{0,4},{4,0},{8,12},{12,8},{16,20},{20,16},{24,28},{28,24},{32,36},... | collective-permute-start | bytes 540680 | tf_op jit(solution)/shard_map/ppermute | solution.py:66
  (89 other events, 788.8 us)
Sparse Core Ops, SparseCore 0:
  11.0 148.8 all-gather.1
  243.4 122.1 reduce-scatter.1
